TPU v7x, 32 devices: a whole 2x2x4 slice. The times are simulated.
32 devices in a mesh: seq: 16 (over z, x, core), tp: 2 (over y).
Axes of the slice: x: 2, y: 2, z: 4, core: 2. Of those that a mesh axis runs over, the one named last changes fastest.
Arguments:
- values: bfloat16 [4096, 4096], P('seq', 'tp'), may hold values from -6 to 6
- gate: bfloat16 [4096, 4096], P('seq', 'tp'), may hold values from -6 to 6
- out_grad: bfloat16 [4096, 4096], P('seq', 'tp'), may hold values from -6 to 6
- out_weight: bfloat16 [4096, 4096], P(None, 'tp'), may hold values from -0.09375 to 0.09375
- filt: float32 [4096, 4096], P('seq', 'tp'), may hold values from -6 to 6
- decay: float32 [4096], P('tp'), may hold values from 0.5 to 16
Outputs:
- d_values: bfloat16 [4096, 4096], P('seq', 'tp')
- d_gate: bfloat16 [4096, 4096], P('seq', 'tp')
- d_filt: float32 [4096, 4096], P('seq', 'tp')
- decay_grad: float32 [4096], P('tp')
- d_out_weight: float32 [4096, 4096], P('seq', 'tp')
All inputs are finite; a program needn't handle non-finite values.
Results may differ from a plain program's by a relative error of at most 0.0085.
Values may be sent and summed in bfloat16 or wider, within the bound.
No kernel may reach another device: no remote copies, remote signals or barrier semaphores. Data moves between devices by JAX's collectives and lax.ppermute only.
A program may use at most 192 MiB of HBM per device.

v0:
```python
import functools
import math

import jax
import jax.numpy as jnp
import ml_dtypes
import numpy as np
from jax import lax
from jax.experimental import pallas as pl
from jax.experimental.pallas import tpu as pltpu
from jax.sharding import PartitionSpec as P

BF16 = jnp.bfloat16
F32 = jnp.float32
RADIX = 128
STEP = 16
VMEM_BYTES = 48 * 1024 * 1024


def middle_tables(length):
    padded = 2 * length
    outer = padded // RADIX
    k1 = np.arange(outer // 2 + 1)
    r = np.arange(RADIX)
    index = k1[:, None, None] * r[None, None, :] + outer * (r[:, None] * r[None, :])[None]
    phase = 2.0 * np.pi * (index % padded) / padded
    cos, sin = np.cos(phase), np.sin(phase)
    table = np.concatenate(
        [np.concatenate([cos, sin], axis=2), np.concatenate([-sin, cos], axis=2)], axis=1
    )
    there = jnp.asarray(table.astype(ml_dtypes.bfloat16))
    back = jnp.asarray(np.swapaxes(table, 1, 2).astype(ml_dtypes.bfloat16))
    return there, back


def real_forward(points):
    size = len(points)
    if size == 2:
        if points[1] is None:
            return [points[0], points[0]], [None, None]
        return [points[0] + points[1], points[0] - points[1]], [None, None]
    even_re, even_im = real_forward(points[0::2])
    odd_re, odd_im = real_forward(points[1::2])
    half = size // 2
    re, im = [None] * (half + 1), [None] * (half + 1)
    re[0], re[half] = even_re[0] + odd_re[0], even_re[0] - odd_re[0]
    for k in range(1, half // 2):
        cos = math.cos(2.0 * math.pi * k / size)
        sin = math.sin(2.0 * math.pi * k / size)
        turn_re = cos * odd_re[k] + sin * odd_im[k]
        turn_im = cos * odd_im[k] - sin * odd_re[k]
        re[k], im[k] = even_re[k] + turn_re, even_im[k] + turn_im
        re[half - k], im[half - k] = even_re[k] - turn_re, turn_im - even_im[k]
    re[half // 2], im[half // 2] = even_re[half // 2], -odd_re[half // 2]
    return re, im


def real_backward(re, im, wanted):
    half = len(re) - 1
    size = 2 * half
    if size == 2:
        return [re[0] + re[1]] + ([re[0] - re[1]] if wanted > 1 else [None])
    quarter = half // 2
    even_re, even_im = [None] * (quarter + 1), [None] * (quarter + 1)
    odd_re, odd_im = [None] * (quarter + 1), [None] * (quarter + 1)
    even_re[0], odd_re[0] = re[0] + re[half], re[0] - re[half]
    for k in range(1, quarter):
        cos = math.cos(2.0 * math.pi * k / size)
        sin = math.sin(2.0 * math.pi * k / size)
        even_re[k], even_im[k] = re[k] + re[half - k], im[k] - im[half - k]
        diff_re, diff_im = re[k] - re[half - k], im[k] + im[half - k]
        odd_re[k] = cos * diff_re - sin * diff_im
        odd_im[k] = cos * diff_im + sin * diff_re
    even_re[quarter], odd_re[quarter] = 2.0 * re[quarter], -2.0 * im[quarter]
    even = real_backward(even_re, even_im, wanted // 2)
    odd = real_backward(odd_re, odd_im, wanted // 2)
    return [point for pair in zip(even, odd) for point in pair]


def load_points(ref, chunk, half):
    per = ref.shape[1] // RADIX
    return [ref[p // per, pl.ds((p % per) * RADIX + chunk * STEP, STEP), :] for p in range(half)]


def outer_forward(x_ref, mid_ref):
    half = mid_ref.shape[0] - 1

    def chunk_body(chunk, carry):
        points = [x.astype(F32) for x in load_points(x_ref, chunk, half)]
        re, im = real_forward(points + [None] * half)
        for k in range(half + 1):
            mid_ref[k, pl.ds(chunk * STEP, STEP), :] = re[k].astype(BF16)
            low = jnp.zeros_like(re[k]) if im[k] is None else im[k]
            mid_ref[k, pl.ds(RADIX + chunk * STEP, STEP), :] = low.astype(BF16)
        return carry

    lax.fori_loop(0, RADIX // STEP, chunk_body, 0)


def outer_backward(mid_ref, chunk, scale):
    half = mid_ref.shape[0] - 1
    re = [mid_ref[k, pl.ds(chunk * STEP, STEP), :].astype(F32) for k in range(half + 1)]
    im = [
        mid_ref[k, pl.ds(RADIX + chunk * STEP, STEP), :].astype(F32) if 0 < k < half else None
        for k in range(half + 1)
    ]
    return [scale * point for point in real_backward(re, im, half)[:half]]


def matmul(a, b):
    return jnp.dot(a, b, preferred_element_type=F32)


def product(a, b):
    a_re, a_im, b_re, b_im = a[:RADIX], a[RADIX:], b[:RADIX], b[RADIX:]
    return jnp.concatenate([a_re * b_re - a_im * b_im, a_re * b_im + a_im * b_re]).astype(BF16)


def conj_product(a, b):
    a_re, a_im, b_re, b_im = a[:RADIX], a[RADIX:], b[:RADIX], b[RADIX:]
    return jnp.concatenate([a_re * b_re + a_im * b_im, a_re * b_im - a_im * b_re]).astype(BF16)


def conv_kernel(v_ref, k_ref, there_ref, back_ref, spec_v_ref, spec_k_ref, out_ref, mid_v, mid_k):
    half = mid_v.shape[0] - 1
    scale = 0.5 / (half * RADIX)
    outer_forward(v_ref, mid_v)
    outer_forward(k_ref, mid_k)

    def freq_body(k, carry):
        spec_v = matmul(there_ref[k], mid_v[k])
        spec_k = matmul(there_ref[k], mid_k[k])
        spec_v_ref[k] = spec_v
        spec_k_ref[k] = spec_k
        mid_v[k] = matmul(back_ref[k], product(spec_v, spec_k)).astype(BF16)
        return carry

    lax.fori_loop(0, half + 1, freq_body, 0)
    per = out_ref.shape[1] // RADIX

    def chunk_body(chunk, carry):
        for p, point in enumerate(outer_backward(mid_v, chunk, scale)):
            rows = pl.ds((p % per) * RADIX + chunk * STEP, STEP)
            out_ref[p // per, rows, :] = point.astype(BF16)
        return carry

    lax.fori_loop(0, RADIX // STEP, chunk_body, 0)


def grad_kernel(
    g_ref, k_ref, spec_v_ref, spec_k_ref, there_ref, back_ref, cg_ref, kg_ref, mid_g, mid_c
):
    half = mid_g.shape[0] - 1
    length = half * RADIX
    scale = 0.5 / length
    outer_forward(g_ref, mid_g)

    def freq_body(k, carry):
        spec_g = matmul(there_ref[k], mid_g[k])
        back = back_ref[k]
        mid_c[k] = matmul(back, conj_product(spec_k_ref[k], spec_g)).astype(BF16)
        mid_g[k] = matmul(back, conj_product(spec_v_ref[k], spec_g)).astype(BF16)
        return carry

    lax.fori_loop(0, half + 1, freq_body, 0)
    rows = g_ref.shape[1]
    per = rows // RADIX

    def chunk_body(chunk, total):
        for p, point in enumerate(outer_backward(mid_c, chunk, scale)):
            here = pl.ds((p % per) * RADIX + chunk * STEP, STEP)
            cg_ref[p // per, here, :] = point.astype(BF16)
        kernel = load_points(k_ref, chunk, half)
        first = lax.broadcasted_iota(jnp.int32, total.shape, 0) + chunk * STEP
        for p, point in enumerate(outer_backward(mid_g, chunk, scale)):
            here = pl.ds((p % per) * RADIX + chunk * STEP, STEP)
            kg_ref[p // per, here, :] = point.astype(BF16)
            place = (first + p * RADIX).astype(F32) * (1.0 / length)
            total = total + place * point * kernel[p].astype(F32)
        return total

    total = jnp.zeros((STEP, g_ref.shape[2]), F32)
    total = lax.fori_loop(0, RADIX // STEP, chunk_body, total)
    total = -(1.0 / math.sqrt(length)) * jnp.sum(total, axis=0, keepdims=True)
    high = total.astype(BF16).astype(F32)
    row = lax.broadcasted_iota(jnp.int32, (STEP, g_ref.shape[2]), 0)
    extra = jnp.where(row == 0, high, jnp.where(row == 1, total - high, 0.0)).astype(BF16)
    for device in range(kg_ref.shape[0]):
        kg_ref[device, pl.ds(rows, STEP), :] = extra


def pack_kernel(v_ref, filt_ref, decay_ref, start_ref, out_ref, *, length):
    own = out_ref.shape[3]
    rows = v_ref.shape[0]
    row = lax.broadcasted_iota(jnp.int32, (rows, own), 0) + start_ref[0]
    position = row.astype(F32) * (1.0 / length)
    for d in range(out_ref.shape[0]):
        cols = slice(d * own, (d + 1) * own)
        out_ref[d, 0] = v_ref[:, cols]
        window = jnp.exp(-decay_ref[:, cols] * position)
        out_ref[d, 1] = (filt_ref[:, cols] * window * (1.0 / math.sqrt(length))).astype(BF16)


def gated_kernel(grad_ref, gate_ref, out_ref):
    own = out_ref.shape[2]
    for d in range(out_ref.shape[0]):
        cols = slice(d * own, (d + 1) * own)
        out_ref[d] = (grad_ref[:, cols].astype(F32) * gate_ref[:, cols].astype(F32)).astype(BF16)


def out_kernel(moved_ref, grad_ref, gate_ref, d_gate_ref, gated_ref):
    own = moved_ref.shape[2]
    for d in range(moved_ref.shape[0]):
        cols = slice(d * own, (d + 1) * own)
        conv_out = moved_ref[d].astype(F32)
        d_gate_ref[:, cols] = (grad_ref[:, cols].astype(F32) * conv_out).astype(BF16)
        gated_ref[:, cols] = (gate_ref[:, cols].astype(F32) * conv_out).astype(BF16)


def values_kernel(moved_ref, out_ref):
    own = moved_ref.shape[2]
    for d in range(moved_ref.shape[0]):
        out_ref[:, slice(d * own, (d + 1) * own)] = moved_ref[d]


def filt_kernel(moved_ref, decay_ref, start_ref, d_filt_ref, decay_grad_ref, *, length):
    own = moved_ref.shape[2]
    rows = d_filt_ref.shape[0]
    row = lax.broadcasted_iota(jnp.int32, (rows, own), 0) + start_ref[0]
    position = row.astype(F32) * (1.0 / length)
    for d in range(moved_ref.shape[0]):
        cols = slice(d * own, (d + 1) * own)
        window = jnp.exp(-decay_ref[:, cols] * position)
        kernel_grad = moved_ref[d, pl.ds(0, rows), :].astype(F32)
        d_filt_ref[:, cols] = kernel_grad * window * (1.0 / math.sqrt(length))
        extra = moved_ref[d, pl.ds(rows, STEP), :].astype(F32)
        decay_grad_ref[:, cols] = extra[0:1] + extra[1:2]


def call(kernel, outs, args, scratch=(), flops=0, scalar=()):
    whole = pl.BlockSpec(memory_space=pltpu.VMEM)
    specs = [
        pl.BlockSpec(memory_space=pltpu.SMEM) if i in scalar else whole for i in range(len(args))
    ]
    moved = sum(math.prod(a.shape) * a.dtype.itemsize for a in (*args, *outs))
    return pl.pallas_call(
        kernel,
        out_shape=outs,
        in_specs=specs,
        out_specs=[whole] * len(outs),
        scratch_shapes=list(scratch),
        compiler_params=pltpu.CompilerParams(vmem_limit_bytes=VMEM_BYTES),
        cost_estimate=pl.CostEstimate(flops=flops, bytes_accessed=moved, transcendentals=0),
    )(*args)


def struct(shape, dtype):
    return jax.ShapeDtypeStruct(shape, dtype)


def swap(array, axis, size, bit):
    return lax.ppermute(array, axis, [(i, i ^ bit) for i in range(size)])


def gather_columns(block, axis):
    size = lax.axis_size(axis)
    if size != 2:
        return lax.all_gather(block, axis, axis=1, tiled=True)
    other = swap(block, axis, size, 1)
    first = lax.axis_index(axis) == 0
    return jnp.concatenate(
        [jnp.where(first, block, other), jnp.where(first, other, block)], axis=1
    )


def line_reduce_scatter(parts, size, inner, beside):
    outer = size // inner
    z = lax.axis_index("seq") // inner
    total = lax.dynamic_index_in_dim(parts, z, 0, keepdims=False).astype(F32)
    right = left = None
    for step in range(1, outer):
        ahead = lax.dynamic_index_in_dim(
            parts, jnp.minimum(z + outer - step, outer - 1), 0, keepdims=False
        )
        behind = lax.dynamic_index_in_dim(
            parts, jnp.maximum(z - outer + step, 0), 0, keepdims=False
        )
        if right is not None:
            ahead = (ahead.astype(F32) + right.astype(F32)).astype(BF16)
            behind = (behind.astype(F32) + left.astype(F32)).astype(BF16)
        to_right = [(i, i + inner) for i in range(size) if i // inner < step]
        to_left = [(i, i - inner) for i in range(size) if i // inner >= outer - step]
        right = lax.ppermute(ahead, "seq", to_right)
        left = lax.ppermute(behind, "seq", to_left)
        if step == 1:
            right, left, beside = lax.optimization_barrier((right, left, beside))
    if right is not None:
        total = total + right.astype(F32) + left.astype(F32)
    return total, beside


def exchange(blocks):
    return lax.all_to_all(blocks, "seq", split_axis=0, concat_axis=0, tiled=True)


def on_device(values, gate, out_grad, out_weight, filt, decay):
    rows, width = values.shape
    seq = lax.axis_size("seq")
    me = lax.axis_index("seq")
    length = rows * seq
    own = width // seq
    norm_scale = 1.0 / math.sqrt(length)
    inner = 4 if seq % 4 == 0 else 1
    outer = seq // inner
    half = length // RADIX
    there, back = middle_tables(length)
    blocks = struct((seq, rows, own), BF16)
    spectrum = struct((half + 1, 2 * RADIX, own), F32)
    mid = pltpu.VMEM((half + 1, 2 * RADIX, own), BF16)
    inner_flops = 2 * (half + 1) * (2 * RADIX) ** 2 * own
    start = (me * rows).astype(jnp.int32)[None]
    rates = decay[None, :]

    full_grad = gather_columns(out_grad, "tp")
    (packed,) = call(
        functools.partial(pack_kernel, length=length),
        [struct((seq, 2, rows, own), BF16)],
        (values, filt, rates, start),
        scalar=(3,),
    )
    moved = exchange(packed)

    grad_y = jnp.dot(full_grad, out_weight, preferred_element_type=F32).astype(BF16)
    (gated_grad,) = call(gated_kernel, [blocks], (grad_y, gate))
    gated_grad, moved = lax.optimization_barrier((gated_grad, moved))
    grad_c = exchange(gated_grad)

    features = full_grad.shape[1] // seq
    by_inner = full_grad.reshape(rows, outer, inner, features)
    bits = [0]
    high = inner // 2
    while high:
        bits = bits + [bit ^ high for bit in bits]
        high //= 2
    grads = []
    for bit in bits:
        target = (me % inner) ^ bit
        piece = lax.dynamic_index_in_dim(by_inner, target, 2, keepdims=False)
        piece = piece.reshape(rows, outer * features)
        grads.append(swap(piece, "seq", seq, bit) if bit else piece)
    grads = jnp.concatenate(grads, axis=0)

    values_c, kernel_c = moved[:, 0], moved[:, 1]
    spec_v, spec_k, conv_out_c = call(
        conv_kernel,
        [spectrum, spectrum, blocks],
        (values_c, kernel_c, there, back),
        scratch=(mid, mid),
        flops=6 * inner_flops,
    )
    conv_out_c, grad_c, grads = lax.optimization_barrier((conv_out_c, grad_c, grads))
    conv_out = exchange(conv_out_c)

    conv_grad_c, kernel_grad_c = call(
        grad_kernel,
        [blocks, struct((seq, rows + STEP, own), BF16)],
        (grad_c, kernel_c, spec_v, spec_k, there, back),
        scratch=(mid, mid),
        flops=6 * inner_flops,
    )
    conv_grad_c, kernel_grad_c, conv_out = lax.optimization_barrier(
        (conv_grad_c, kernel_grad_c, conv_out)
    )
    conv_grad = exchange(conv_grad_c)

    block = struct((rows, width), BF16)
    d_gate, gated_out = call(out_kernel, [block, block], (conv_out, grad_y, gate))
    outs = [gated_out]
    high = inner // 2
    while high:
        outs = outs + [swap(part, "seq", seq, high) for part in outs]
        high //= 2
    *outs, conv_grad, kernel_grad_c = lax.optimization_barrier(
        (*outs, conv_grad, kernel_grad_c)
    )
    kernel_grad = exchange(kernel_grad_c)
    (d_values,) = call(values_kernel, [block], (conv_grad,))
    terms = lax.dot_general(
        grads,
        jnp.concatenate(outs, axis=0),
        (((0,), (0,)), ((), ())),
        preferred_element_type=F32,
    ).astype(BF16)
    terms = terms.reshape(outer, features, width)
    total, kernel_grad = line_reduce_scatter(terms, seq, inner, kernel_grad)
    d_out_weight = total * norm_scale
    d_filt, decay_grad = call(
        functools.partial(filt_kernel, length=length),
        [struct((rows, width), F32), struct((1, width), F32)],
        (kernel_grad, rates, start),
        scalar=(2,),
    )
    return (d_values, d_gate, d_filt, decay_grad[0], d_out_weight)


def solution(mesh):
    in_specs = (
        P("seq", "tp"),
        P("seq", "tp"),
        P("seq", "tp"),
        P(None, "tp"),
        P("seq", "tp"),
        P("tp"),
    )
    out_specs = (P("seq", "tp"), P("seq", "tp"), P("seq", "tp"), P("tp"), P("seq", "tp"))
    return jax.shard_map(
        on_device, mesh=mesh, in_specs=in_specs, out_specs=out_specs, check_vma=False
    )
```

profile of v0, /device:TPU:0, one launch (start us, length us, event | category | flops | bytes accessed | tf_op | source)
XLA Modules:
  0.0 343.8 jit_solution(12527066964898994554)
XLA Ops:
  6.0 7.5 %all-to-all-start = ((bf16[16,2,256,128]{3,2,1,0:T(8,128)(2,1)}), bf16[16,2,256,128]{3,2,1,0:T(8,128)(2,1)}, u32[]{:S(2)}, u32[]{:S(2)}) async-start(bf16[16,2,256,128]{3,2,1,0:T(8,128)(2,1)} %shard_map.120), calls=%async_computation | async-start | bytes 4194304 | tf_op jit(solution)/shard_map/all_to_all | solution.py:303
  15.6 23.9 %collective-permute-done = bf16[256,2048]{0,1:T(8,128)(2,1)S(1)} collective-permute-done((bf16[256,2048]{0,1:T(8,128)(2,1)S(1)}, bf16[256,2048]{0,1:T(8,128)(2,1)S(1)}, u32[]{:S(2)}, u32[]{:S(2)}) %collective-permute-start) | collective-permute-done | bytes 1048608 | tf_op jit(solution)/shard_map/ppermute | solution.py:262
  41.0 11.5 %convolution_convert_fusion.grad_ref = bf16[256,2048]{1,0:T(8,128)(2,1)S(1)} fusion(bf16[4096,2048]{1,0:T(8,128)(2,1)} %param.11, bf16[256,2048]{0,1:T(8,128)(2,1)S(1)} %get-tuple-element.68, bf16[256,2048]{0,1:T(8,128)(2,1)S(1)} %get-tuple-element.67), kind=kOutput, calls=%fused_computation.9 | convolution fusion | flops 4299685888 | bytes 19922944 | tf_op jit(solution)/shard_map/dot_general | solution.py:333
  54.7 11.2 %all-to-all-start.1 = ((bf16[16,256,128]{2,1,0:T(8,128)(2,1)}), bf16[16,256,128]{2,1,0:T(8,128)(2,1)S(1)}, u32[]{:S(2)}, u32[]{:S(2)}) async-start(bf16[16,256,128]{2,1,0:T(8,128)(2,1)} %copy-done.1), calls=%async_computation.1 | async-start | bytes 2097152 | tf_op jit(solution)/shard_map/all_to_all | solution.py:303
  67.8 2.0 collective-permute-start.1
  70.0 22.0 %collective-permute-done.1 = bf16[256,1024]{0,1:T(8,128)(2,1)S(1)} collective-permute-done((bf16[256,1024]{0,1:T(8,128)(2,1)S(1)}, bf16[256,1024]{0,1:T(8,128)(2,1)S(1)}, u32[]{:S(2)}, u32[]{:S(2)}) %collective-permute-start.1) | collective-permute-done | bytes 524320 | tf_op jit(solution)/shard_map/ppermute | solution.py:262
  92.0 10.3 %collective-permute-done.3 = bf16[256,1024]{0,1:T(8,128)(2,1)S(1)} collective-permute-done((bf16[256,1024]{0,1:T(8,128)(2,1)S(1)}, bf16[256,1024]{0,1:T(8,128)(2,1)S(1)}, u32[]{:S(2)}, u32[]{:S(2)}) %collective-permute-start.3) | collective-permute-done | bytes 524320 | tf_op jit(solution)/shard_map/ppermute | solution.py:262
  105.6 26.4 %shard_map.121 = (f32[33,256,128]{2,1,0:T(8,128)}, f32[33,256,128]{2,1,0:T(8,128)}, bf16[16,256,128]{2,1,0:T(8,128)(2,1)S(1)}) custom-call(bf16[16,256,128]{2,1,0:T(8,128)(2,1)S(1)} %get-tuple-element.66.v_ref, bf16[16,256,128]{2,1,0:T(8,128)(2,1)S(1)} %get-tuple-element.65.k_ref, bf16[33,256,256]{2,1,0:T(8,128)(2,1)} %constant.93.clone.there_ref, ...), custom_call_target="tpu_custom_call" | custom-call | flops 3321888768 | bytes 20447232 | tf_op jit(solution)/shard_map/pallas_call | solution.py:246
  133.9 4.7 %all-to-all-start.2 = ((bf16[16,256,128]{2,1,0:T(8,128)(2,1)}), bf16[16,256,128]{2,1,0:T(8,128)(2,1)}, u32[]{:S(2)}, u32[]{:S(2)}) async-start(bf16[16,256,128]{2,1,0:T(8,128)(2,1)} %copy-done.5), calls=%async_computation.2 | async-start | bytes 2097152 | tf_op jit(solution)/shard_map/all_to_all | solution.py:303
  139.9 25.8 %shard_map.122 = (bf16[16,256,128]{2,1,0:T(8,128)(2,1)}, bf16[16,272,128]{2,1,0:T(8,128)(2,1)}) custom-call(bf16[16,256,128]{2,1,0:T(8,128)(2,1)S(1)} %all-to-all-done.1.g_ref, bf16[16,256,128]{2,1,0:T(8,128)(2,1)S(1)} %copy-done.3, f32[33,256,128]{2,1,0:T(8,128)} %get-tuple-element.35.spec_v_ref, f32[33,256,128]{2,1,0:T(8,128)} %get-tuple-element.36.spec_k_ref, ...), custom_call_target="tpu_custom_call" | custom-call | flops 3321888768 | bytes 21561344 | tf_op jit(solution)/shard_map/pallas_call | solution.py:246
  165.7 2.5 shard_map.123
  170.1 4.6 %all-to-all-start.3 = ((bf16[16,256,128]{2,1,0:T(8,128)(2,1)}), bf16[16,256,128]{2,1,0:T(8,128)(2,1)S(1)}, u32[]{:S(2)}, u32[]{:S(2)}) async-start(bf16[16,256,128]{2,1,0:T(8,128)(2,1)} %get-tuple-element.42), calls=%async_computation.3 | async-start | bytes 2097152 | tf_op jit(solution)/shard_map/all_to_all | solution.py:303
  175.2 27.5 %collective-permute-done.4 = bf16[256,2048]{1,0:T(8,128)(2,1)S(1)} collective-permute-done((bf16[256,2048]{1,0:T(8,128)(2,1)S(1)}, bf16[256,2048]{1,0:T(8,128)(2,1)S(1)}, u32[]{:S(2)}, u32[]{:S(2)}) %collective-permute-start.4) | collective-permute-done | bytes 1048608 | tf_op jit(solution)/shard_map/ppermute | solution.py:262
  205.5 6.0 %all-to-all-start.4 = ((bf16[16,272,128]{2,1,0:T(8,128)(2,1)}), bf16[16,272,128]{2,1,0:T(8,128)(2,1)S(1)}, u32[]{:S(2)}, u32[]{:S(2)}) async-start(bf16[16,272,128]{2,1,0:T(8,128)(2,1)} %get-tuple-element.51), calls=%async_computation.4 | async-start | bytes 2228224 | tf_op jit(solution)/shard_map/all_to_all | solution.py:303
  211.4 7.0 %fusion.8 = bf16[1024,2048]{1,0:T(8,128)(2,1)S(1)} fusion(bf16[1024,1024]{0,1:T(8,128)(2,1)} %pad_maximum_fusion.1, bf16[256,2048]{1,0:T(8,128)(2,1)} %collective-permute-done.6, bf16[256,2048]{1,0:T(8,128)(2,1)} %collective-permute-done.5, bf16[256,2048]{1,0:T(8,128)(2,1)} %copy-done.13, bf16[256,2048]{1,0:T(8,128)(2,1)S(1)} %get-tuple-element.47), kind=kOutput, calls=%fused_computation.8 | convolution fusion | flops 4313841664 | bytes 10485760 | tf_op jit(solution)/shard_map/dot_general | solution.py:388
  220.7 4.8 %collective-permute-start.7 = (bf16[256,2048]{1,0:T(8,128)(2,1)}, bf16[256,2048]{1,0:T(8,128)(2,1)}, u32[]{:S(2)}, u32[]{:S(2)}) collective-permute-start(bf16[256,2048]{1,0:T(8,128)(2,1)} %get-tuple-element.60), channel_id=1, source_target_pairs={{0,8},{2,10},{4,12},{6,14},{1,9},{3,11},{5,13},{7,15}} | collective-permute-start | bytes 3145736 | tf_op jit(solution)/shard_map/ppermute | solution.py:293
  227.2 25.9 %collective-permute-done.7 = bf16[256,2048]{1,0:T(8,128)(2,1)} collective-permute-done((bf16[256,2048]{1,0:T(8,128)(2,1)}, bf16[256,2048]{1,0:T(8,128)(2,1)}, u32[]{:S(2)}, u32[]{:S(2)}) %collective-permute-start.7) | collective-permute-done | bytes 1048608 | tf_op jit(solution)/shard_map/ppermute | solution.py:293
  255.1 5.4 %collective-permute-start.9 = (bf16[256,2048]{1,0:T(8,128)(2,1)S(1)}, bf16[256,2048]{1,0:T(8,128)(2,1)}, u32[]{:S(2)}, u32[]{:S(2)}) collective-permute-start(bf16[256,2048]{1,0:T(8,128)(2,1)S(1)} %fusion.13), channel_id=1, source_target_pairs={{0,8},{2,10},{4,12},{6,14},{8,16},{10,18},{12,20},{14,22},{1,9},{3... | collective-permute-start | bytes 3145736 | tf_op jit(solution)/shard_map/ppermute | solution.py:293
  260.4 21.5 %collective-permute-done.9 = bf16[256,2048]{1,0:T(8,128)(2,1)} collective-permute-done((bf16[256,2048]{1,0:T(8,128)(2,1)S(1)}, bf16[256,2048]{1,0:T(8,128)(2,1)}, u32[]{:S(2)}, u32[]{:S(2)}) %collective-permute-start.9) | collective-permute-done | bytes 1048608 | tf_op jit(solution)/shard_map/ppermute | solution.py:293
  281.9 3.9 %fusion.14 = (bf16[256,2048]{1,0:T(8,128)(2,1)}, bf16[256,2048]{1,0:T(8,128)(2,1)S(1)}) fusion(bf16[256,2048]{1,0:T(8,128)(2,1)} %collective-permute-done.9, bf16[4,256,2048]{2,1,0:T(8,128)(2,1)} %bitcast.38, s32[]{:T(128)S(6)} %select_n.69, bf16[256,2048]{1,0:T(8,128)(2,1)} %collective-permute-done.8, s32[]{:T(128)S(6)} %max.11), kind=kLoop, calls=%fused_computation.19 | loop fusion | flops 4194304 | bytes 6291464 | tf_op jit(solution)/shard_map/convert_element_type | solution.py:289
  287.5 5.2 %collective-permute-start.10 = (bf16[256,2048]{1,0:T(8,128)(2,1)}, bf16[256,2048]{1,0:T(8,128)(2,1)}, u32[]{:S(2)}, u32[]{:S(2)}) collective-permute-start(bf16[256,2048]{1,0:T(8,128)(2,1)} %get-tuple-element.57), channel_id=1, source_target_pairs={{0,8},{2,10},{4,12},{6,14},{8,16},{10,18},{12,20},{14,22},{16,24},... | collective-permute-start | bytes 3145736 | tf_op jit(solution)/shard_map/ppermute | solution.py:293
  298.9 14.7 %collective-permute-done.10 = bf16[256,2048]{1,0:T(8,128)(2,1)} collective-permute-done((bf16[256,2048]{1,0:T(8,128)(2,1)}, bf16[256,2048]{1,0:T(8,128)(2,1)}, u32[]{:S(2)}, u32[]{:S(2)}) %collective-permute-start.10) | collective-permute-done | bytes 1048608 | tf_op jit(solution)/shard_map/ppermute | solution.py:293
  313.6 26.5 %collective-permute-done.12 = bf16[256,2048]{1,0:T(8,128)(2,1)} collective-permute-done((bf16[256,2048]{1,0:T(8,128)(2,1)S(1)}, bf16[256,2048]{1,0:T(8,128)(2,1)}, u32[]{:S(2)}, u32[]{:S(2)}) %collective-permute-start.12) | collective-permute-done | bytes 1048608 | tf_op jit(solution)/shard_map/ppermute | solution.py:294
  340.1 3.7 %fusion.16 = f32[256,2048]{1,0:T(8,128)} fusion(bf16[256,2048]{1,0:T(8,128)(2,1)} %collective-permute-done.12, bf16[256,2048]{1,0:T(8,128)(2,1)} %collective-permute-done.10, bf16[4,256,2048]{2,1,0:T(8,128)(2,1)} %bitcast.40, s32[]{:T(128)S(6)} %select_n.68), kind=kLoop, calls=%fused_computation.22 | loop fusion | flops 3145728 | bytes 5242884 | tf_op jit(solution)/shard_map/mul | solution.py:396
  (60 shorter events, 38.5 us)
Async XLA Ops:
  0.6 1.6 copy-start.4
  6.0 7.6 %copy-start.12 = (bf16[256,2048]{1,0:T(8,128)(2,1)S(1)}, bf16[256,2048]{1,0:T(8,128)(2,1)}, u32[]{:S(2)}) copy-start(bf16[256,2048]{1,0:T(8,128)(2,1)} %param.10) | copy-start | bytes 3145732
  6.0 48.7 %all-to-all-start = ((bf16[16,2,256,128]{3,2,1,0:T(8,128)(2,1)}), bf16[16,2,256,128]{3,2,1,0:T(8,128)(2,1)}, u32[]{:S(2)}, u32[]{:S(2)}) async-start(bf16[16,2,256,128]{3,2,1,0:T(8,128)(2,1)} %shard_map.120), calls=%async_computation | async-start | bytes 4194304 | tf_op jit(solution)/shard_map/all_to_all | solution.py:303
  14.1 25.5 %collective-permute-start = (bf16[256,2048]{0,1:T(8,128)(2,1)S(1)}, bf16[256,2048]{0,1:T(8,128)(2,1)S(1)}, u32[]{:S(2)}, u32[]{:S(2)}) collective-permute-start(bf16[256,2048]{0,1:T(8,128)(2,1)S(1)} %copy.20), channel_id=1, source_target_pairs={{0,1},{1,0},{2,3},{3,2},{4,5},{5,4},{6,7},{7,6},{8,9},{9,8},{10,11... | collective-permute-start | bytes 3145736 | tf_op jit(solution)/shard_map/ppermute | solution.py:262
  41.0 11.5 %copy-start = (bf16[256,2048]{1,0:T(8,128)(2,1)S(1)}, bf16[256,2048]{1,0:T(8,128)(2,1)}, u32[]{:S(2)}) copy-start(bf16[256,2048]{1,0:T(8,128)(2,1)} %gate_ref.3) | copy-start | bytes 3145732
  54.7 79.3 %all-to-all-start.1 = ((bf16[16,256,128]{2,1,0:T(8,128)(2,1)}), bf16[16,256,128]{2,1,0:T(8,128)(2,1)S(1)}, u32[]{:S(2)}, u32[]{:S(2)}) async-start(bf16[16,256,128]{2,1,0:T(8,128)(2,1)} %copy-done.1), calls=%async_computation.1 | async-start | bytes 2097152 | tf_op jit(solution)/shard_map/all_to_all | solution.py:303
  67.8 24.2 %collective-permute-start.1 = (bf16[256,1024]{0,1:T(8,128)(2,1)S(1)}, bf16[256,1024]{0,1:T(8,128)(2,1)S(1)}, u32[]{:S(2)}, u32[]{:S(2)}) collective-permute-start(bf16[256,1024]{0,1:T(8,128)(2,1)S(1)} %bitcast.45), channel_id=1, source_target_pairs={{0,4},{2,6},{4,0},{6,2},{8,12},{10,14},{12,8},{14,10},{16,20},{18,... | collective-permute-start | bytes 1572872 | tf_op jit(solution)/shard_map/ppermute | solution.py:262
  69.8 22.2 %collective-permute-start.2 = (bf16[256,1024]{0,1:T(8,128)(2,1)S(1)}, bf16[256,1024]{0,1:T(8,128)(2,1)S(1)}, u32[]{:S(2)}, u32[]{:S(2)}) collective-permute-start(bf16[256,1024]{0,1:T(8,128)(2,1)S(1)} %bitcast.44), channel_id=1, source_target_pairs={{0,2},{2,0},{4,6},{6,4},{8,10},{10,8},{12,14},{14,12},{16,18},{18,... | collective-permute-start | bytes 1572872 | tf_op jit(solution)/shard_map/ppermute | solution.py:262
  69.8 32.5 %collective-permute-start.3 = (bf16[256,1024]{0,1:T(8,128)(2,1)S(1)}, bf16[256,1024]{0,1:T(8,128)(2,1)S(1)}, u32[]{:S(2)}, u32[]{:S(2)}) collective-permute-start(bf16[256,1024]{0,1:T(8,128)(2,1)S(1)} %bitcast.43), channel_id=1, source_target_pairs={{0,6},{2,4},{4,2},{6,0},{8,14},{10,12},{12,10},{14,8},{16,22},{18,... | collective-permute-start | bytes 1572872 | tf_op jit(solution)/shard_map/ppermute | solution.py:262
  133.9 31.8 %all-to-all-start.2 = ((bf16[16,256,128]{2,1,0:T(8,128)(2,1)}), bf16[16,256,128]{2,1,0:T(8,128)(2,1)}, u32[]{:S(2)}, u32[]{:S(2)}) async-start(bf16[16,256,128]{2,1,0:T(8,128)(2,1)} %copy-done.5), calls=%async_computation.2 | async-start | bytes 2097152 | tf_op jit(solution)/shard_map/all_to_all | solution.py:303
  168.2 34.4 %collective-permute-start.4 = (bf16[256,2048]{1,0:T(8,128)(2,1)S(1)}, bf16[256,2048]{1,0:T(8,128)(2,1)S(1)}, u32[]{:S(2)}, u32[]{:S(2)}) collective-permute-start(bf16[256,2048]{1,0:T(8,128)(2,1)S(1)} %get-tuple-element.47), channel_id=1, source_target_pairs={{0,4},{2,6},{4,0},{6,2},{8,12},{10,14},{12,8},{14,10},{16,20},{18,... | collective-permute-start | bytes 3145736 | tf_op jit(solution)/shard_map/ppermute | solution.py:262
  170.1 34.2 %all-to-all-start.3 = ((bf16[16,256,128]{2,1,0:T(8,128)(2,1)}), bf16[16,256,128]{2,1,0:T(8,128)(2,1)S(1)}, u32[]{:S(2)}, u32[]{:S(2)}) async-start(bf16[16,256,128]{2,1,0:T(8,128)(2,1)} %get-tuple-element.42), calls=%async_computation.3 | async-start | bytes 2097152 | tf_op jit(solution)/shard_map/all_to_all | solution.py:303
  174.8 27.9 %collective-permute-start.5 = (bf16[256,2048]{1,0:T(8,128)(2,1)S(1)}, bf16[256,2048]{1,0:T(8,128)(2,1)}, u32[]{:S(2)}, u32[]{:S(2)}) collective-permute-start(bf16[256,2048]{1,0:T(8,128)(2,1)S(1)} %get-tuple-element.47), channel_id=1, source_target_pairs={{0,2},{2,0},{4,6},{6,4},{8,10},{10,8},{12,14},{14,12},{16,18},{18,... | collective-permute-start | bytes 3145736 | tf_op jit(solution)/shard_map/ppermute | solution.py:262
  202.7 2.8 copy-start.13
  202.7 2.8 collective-permute-start.6
  205.5 47.7 %all-to-all-start.4 = ((bf16[16,272,128]{2,1,0:T(8,128)(2,1)}), bf16[16,272,128]{2,1,0:T(8,128)(2,1)S(1)}, u32[]{:S(2)}, u32[]{:S(2)}) async-start(bf16[16,272,128]{2,1,0:T(8,128)(2,1)} %get-tuple-element.51), calls=%async_computation.4 | async-start | bytes 2228224 | tf_op jit(solution)/shard_map/all_to_all | solution.py:303
  218.4 2.3 copy-start.9
  220.7 32.4 %collective-permute-start.7 = (bf16[256,2048]{1,0:T(8,128)(2,1)}, bf16[256,2048]{1,0:T(8,128)(2,1)}, u32[]{:S(2)}, u32[]{:S(2)}) collective-permute-start(bf16[256,2048]{1,0:T(8,128)(2,1)} %get-tuple-element.60), channel_id=1, source_target_pairs={{0,8},{2,10},{4,12},{6,14},{1,9},{3,11},{5,13},{7,15}} | collective-permute-start | bytes 3145736 | tf_op jit(solution)/shard_map/ppermute | solution.py:293
  225.5 27.6 %collective-permute-start.8 = (bf16[256,2048]{1,0:T(8,128)(2,1)S(1)}, bf16[256,2048]{1,0:T(8,128)(2,1)}, u32[]{:S(2)}, u32[]{:S(2)}) collective-permute-start(bf16[256,2048]{1,0:T(8,128)(2,1)S(1)} %get-tuple-element.59), channel_id=1, source_target_pairs={{24,16},{26,18},{28,20},{30,22},{25,17},{27,19},{29,21},{31,23}} | collective-permute-start | bytes 3145736 | tf_op jit(solution)/shard_map/ppermute | solution.py:294
  255.1 26.9 %collective-permute-start.9 = (bf16[256,2048]{1,0:T(8,128)(2,1)S(1)}, bf16[256,2048]{1,0:T(8,128)(2,1)}, u32[]{:S(2)}, u32[]{:S(2)}) collective-permute-start(bf16[256,2048]{1,0:T(8,128)(2,1)S(1)} %fusion.13), channel_id=1, source_target_pairs={{0,8},{2,10},{4,12},{6,14},{8,16},{10,18},{12,20},{14,22},{1,9},{3... | collective-permute-start | bytes 3145736 | tf_op jit(solution)/shard_map/ppermute | solution.py:293
  285.9 6.8 %collective-permute-start.11 = (bf16[256,2048]{1,0:T(8,128)(2,1)S(1)}, bf16[256,2048]{1,0:T(8,128)(2,1)}, u32[]{:S(2)}, u32[]{:S(2)}) collective-permute-start(bf16[256,2048]{1,0:T(8,128)(2,1)S(1)} %get-tuple-element.58), channel_id=1, source_target_pairs={{16,8},{18,10},{20,12},{22,14},{24,16},{26,18},{28,20},{30,22},{17... | collective-permute-start | bytes 3145736 | tf_op jit(solution)/shard_map/ppermute | solution.py:294
  287.5 9.7 %copy-start.8 = (f32[2048]{0:T(1024)S(1)}, f32[2048]{0:T(1024)}, u32[]{:S(2)}) copy-start(f32[2048]{0:T(1024)} %param.13) | copy-start | bytes 24580
  287.5 26.1 %collective-permute-start.10 = (bf16[256,2048]{1,0:T(8,128)(2,1)}, bf16[256,2048]{1,0:T(8,128)(2,1)}, u32[]{:S(2)}, u32[]{:S(2)}) collective-permute-start(bf16[256,2048]{1,0:T(8,128)(2,1)} %get-tuple-element.57), channel_id=1, source_target_pairs={{0,8},{2,10},{4,12},{6,14},{8,16},{10,18},{12,20},{14,22},{16,24},... | collective-permute-start | bytes 3145736 | tf_op jit(solution)/shard_map/ppermute | solution.py:293
  294.6 45.5 %collective-permute-start.12 = (bf16[256,2048]{1,0:T(8,128)(2,1)S(1)}, bf16[256,2048]{1,0:T(8,128)(2,1)}, u32[]{:S(2)}, u32[]{:S(2)}) collective-permute-start(bf16[256,2048]{1,0:T(8,128)(2,1)S(1)} %fusion.12), channel_id=1, source_target_pairs={{8,0},{10,2},{12,4},{14,6},{16,8},{18,10},{20,12},{22,14},{24,16},... | collective-permute-start | bytes 3145736 | tf_op jit(solution)/shard_map/ppermute | solution.py:294
  (8 other events, 8.3 us)
where the time goes:
time: 345 us; the launch traced here: 344 us
  waiting for transfers between devices  176 us (51%)
  starting transfers between devices  60.1 us (17%)
  Pallas kernels  59.9 us (17%)
  matrix products  18.4 us (5%)
  other arithmetic  14.9 us (4%)
  local copies, waits for them, and re-layouts  13.7 us (4%)
    ppermute x7, waiting for transfers between devices, swap(): return lax.ppermute(array, axis, [(i, i ^ bit) for i in range(size)])  84.8 us
    ppermute x3, waiting for transfers between devices, line_reduce_scatter(): right = lax.ppermute(ahead, 'seq', to_right)  62.1 us
    pallas_call x7, Pallas kernels, call(): pl.pallas_call(kernel, out_shape=outs, in_specs=specs, out_specs=[whole]...  59.9 us
    all_to_all x5, starting transfers between devices, exchange(): lax.all_to_all(blocks, 'seq', split_axis=0, concat_axis=0, tiled=True)  34.1 us
    ppermute x3, waiting for transfers between devices, line_reduce_scatter(): left = lax.ppermute(behind, 'seq', to_left)  26.5 us
    ppermute x3, starting transfers between devices, line_reduce_scatter(): right = lax.ppermute(ahead, 'seq', to_right)  15.3 us
    dot_general x1, matrix products, on_device(): jnp.dot(full_grad, out_weight, preferred_element_type=F32).astype(BF16)  11.5 us
    unnamed x29, local copies, waits for them, and re-layouts  10.4 us
  transfers between devices with their start and end apart: 18, of which 11 were waited for; matrix products, arithmetic and copies ran while one was open for 8% of the time, Pallas kernels for 16%

commit v1 on v0

--- a/solution.py
+++ b/solution.py
@@ -82,26 +82,26 @@
     return [ref[p // per, pl.ds((p % per) * RADIX + chunk * STEP, STEP), :] for p in range(half)]
 
 
-def outer_forward(x_ref, mid_ref):
+def outer_forward(x_ref, mid_ref, lanes):
     half = mid_ref.shape[0] - 1
 
     def chunk_body(chunk, carry):
         points = [x.astype(F32) for x in load_points(x_ref, chunk, half)]
         re, im = real_forward(points + [None] * half)
         for k in range(half + 1):
-            mid_ref[k, pl.ds(chunk * STEP, STEP), :] = re[k].astype(BF16)
+            mid_ref[k, pl.ds(chunk * STEP, STEP), lanes] = re[k].astype(BF16)
             low = jnp.zeros_like(re[k]) if im[k] is None else im[k]
-            mid_ref[k, pl.ds(RADIX + chunk * STEP, STEP), :] = low.astype(BF16)
+            mid_ref[k, pl.ds(RADIX + chunk * STEP, STEP), lanes] = low.astype(BF16)
         return carry
 
     lax.fori_loop(0, RADIX // STEP, chunk_body, 0)
 
 
-def outer_backward(mid_ref, chunk, scale):
+def outer_backward(mid_ref, chunk, scale, lanes):
     half = mid_ref.shape[0] - 1
-    re = [mid_ref[k, pl.ds(chunk * STEP, STEP), :].astype(F32) for k in range(half + 1)]
+    re = [mid_ref[k, pl.ds(chunk * STEP, STEP), lanes].astype(F32) for k in range(half + 1)]
     im = [
-        mid_ref[k, pl.ds(RADIX + chunk * STEP, STEP), :].astype(F32) if 0 < k < half else None
+        mid_ref[k, pl.ds(RADIX + chunk * STEP, STEP), lanes].astype(F32) if 0 < k < half else None
         for k in range(half + 1)
     ]
     return [scale * point for point in real_backward(re, im, half)[:half]]
@@ -121,25 +121,29 @@
     return jnp.concatenate([a_re * b_re + a_im * b_im, a_re * b_im - a_im * b_re]).astype(BF16)
 
 
-def conv_kernel(v_ref, k_ref, there_ref, back_ref, spec_v_ref, spec_k_ref, out_ref, mid_v, mid_k):
-    half = mid_v.shape[0] - 1
+def unrolled(count):
+    return max(d for d in range(1, 14) if count % d == 0)
+
+
+def conv_kernel(v_ref, k_ref, there_ref, back_ref, spec_ref, out_ref, mid):
+    half = mid.shape[0] - 1
+    own = out_ref.shape[2]
+    low, high = slice(0, own), slice(own, 2 * own)
     scale = 0.5 / (half * RADIX)
-    outer_forward(v_ref, mid_v)
-    outer_forward(k_ref, mid_k)
+    outer_forward(v_ref, mid, low)
+    outer_forward(k_ref, mid, high)
 
     def freq_body(k, carry):
-        spec_v = matmul(there_ref[k], mid_v[k])
-        spec_k = matmul(there_ref[k], mid_k[k])
-        spec_v_ref[k] = spec_v
-        spec_k_ref[k] = spec_k
-        mid_v[k] = matmul(back_ref[k], product(spec_v, spec_k)).astype(BF16)
+        spec = matmul(there_ref[k], mid[k])
+        spec_ref[k] = spec
+        mid[k, :, low] = matmul(back_ref[k], product(spec[:, low], spec[:, high])).astype(BF16)
         return carry
 
-    lax.fori_loop(0, half + 1, freq_body, 0)
+    lax.fori_loop(0, half + 1, freq_body, 0, unroll=unrolled(half + 1))
     per = out_ref.shape[1] // RADIX
 
     def chunk_body(chunk, carry):
-        for p, point in enumerate(outer_backward(mid_v, chunk, scale)):
+        for p, point in enumerate(outer_backward(mid, chunk, scale, low)):
             rows = pl.ds((p % per) * RADIX + chunk * STEP, STEP)
             out_ref[p // per, rows, :] = point.astype(BF16)
         return carry
@@ -147,32 +151,31 @@
     lax.fori_loop(0, RADIX // STEP, chunk_body, 0)
 
 
-def grad_kernel(
-    g_ref, k_ref, spec_v_ref, spec_k_ref, there_ref, back_ref, cg_ref, kg_ref, mid_g, mid_c
-):
-    half = mid_g.shape[0] - 1
+def grad_kernel(g_ref, k_ref, spec_ref, there_ref, back_ref, cg_ref, kg_ref, mid):
+    half = mid.shape[0] - 1
     length = half * RADIX
+    own = cg_ref.shape[2]
+    low, high = slice(0, own), slice(own, 2 * own)
     scale = 0.5 / length
-    outer_forward(g_ref, mid_g)
+    outer_forward(g_ref, mid, low)
 
     def freq_body(k, carry):
-        spec_g = matmul(there_ref[k], mid_g[k])
-        back = back_ref[k]
-        mid_c[k] = matmul(back, conj_product(spec_k_ref[k], spec_g)).astype(BF16)
-        mid_g[k] = matmul(back, conj_product(spec_v_ref[k], spec_g)).astype(BF16)
+        spec_g = matmul(there_ref[k], mid[k, :, low])
+        both = jnp.concatenate([spec_g, spec_g], axis=1)
+        mid[k] = matmul(back_ref[k], conj_product(spec_ref[k], both)).astype(BF16)
         return carry
 
-    lax.fori_loop(0, half + 1, freq_body, 0)
+    lax.fori_loop(0, half + 1, freq_body, 0, unroll=unrolled(half + 1))
     rows = g_ref.shape[1]
     per = rows // RADIX
 
     def chunk_body(chunk, total):
-        for p, point in enumerate(outer_backward(mid_c, chunk, scale)):
+        for p, point in enumerate(outer_backward(mid, chunk, scale, high)):
             here = pl.ds((p % per) * RADIX + chunk * STEP, STEP)
             cg_ref[p // per, here, :] = point.astype(BF16)
         kernel = load_points(k_ref, chunk, half)
         first = lax.broadcasted_iota(jnp.int32, total.shape, 0) + chunk * STEP
-        for p, point in enumerate(outer_backward(mid_g, chunk, scale)):
+        for p, point in enumerate(outer_backward(mid, chunk, scale, low)):
             here = pl.ds((p % per) * RADIX + chunk * STEP, STEP)
             kg_ref[p // per, here, :] = point.astype(BF16)
             place = (first + p * RADIX).astype(F32) * (1.0 / length)
@@ -208,13 +211,53 @@
         out_ref[d] = (grad_ref[:, cols].astype(F32) * gate_ref[:, cols].astype(F32)).astype(BF16)
 
 
-def out_kernel(moved_ref, grad_ref, gate_ref, d_gate_ref, gated_ref):
-    own = moved_ref.shape[2]
-    for d in range(moved_ref.shape[0]):
-        cols = slice(d * own, (d + 1) * own)
-        conv_out = moved_ref[d].astype(F32)
-        d_gate_ref[:, cols] = (grad_ref[:, cols].astype(F32) * conv_out).astype(BF16)
-        gated_ref[:, cols] = (gate_ref[:, cols].astype(F32) * conv_out).astype(BF16)
+def layer_pack_kernel(gate_ref, place_ref, out_ref):
+    inner, outer, _, own = out_ref.shape
+    for z in range(outer):
+        for w in range(inner):
+            first = (z * inner + w) * own
+            out_ref[place_ref[0] ^ w, z] = gate_ref[:, slice(first, first + own)]
+
+
+def layer_kernel(*refs, order):
+    count = len(order)
+    gates, gated_refs, homes = refs[:count], refs[count + 2 : -count], refs[-count:]
+    moved_ref, place_ref = refs[count : count + 2]
+    outer, _, rows, own = moved_ref.shape
+    per = outer // len(gated_refs)
+    for i, bit in enumerate(order):
+        for z in range(outer):
+            conv_out = moved_ref[z, place_ref[0] ^ bit]
+            homes[i][z] = conv_out
+            gated = (gates[i][z].astype(F32) * conv_out.astype(F32)).astype(BF16)
+            first = (z % per) * own
+            gated_refs[z // per][pl.ds(i * rows, rows), slice(first, first + own)] = gated
+
+
+def gate_kernel(moved_ref, grad_ref, place_ref, out_ref):
+    inner, outer, _, own = moved_ref.shape
+    for z in range(outer):
+        for w in range(inner):
+            cols = slice((z * inner + w) * own, (z * inner + w + 1) * own)
+            conv_out = moved_ref[place_ref[0] ^ w, z].astype(F32)
+            out_ref[:, cols] = (grad_ref[:, cols].astype(F32) * conv_out).astype(BF16)
+
+
+def weight_kernel(moved_ref, place_ref, out_ref, *, scale, own):
+    chunks, inner, _, wide = moved_ref.shape
+    per = wide // own
+    for z in range(chunks * per):
+        for w in range(inner):
+            cols = slice((z * inner + w) * own, (z * inner + w + 1) * own)
+            first = (z % per) * own
+            part = moved_ref[z // per, place_ref[0] ^ w, :, slice(first, first + own)]
+            out_ref[:, cols] = part.astype(F32) * scale
+
+
+def transpose_kernel(x_ref, out_ref):
+    rows = x_ref.shape[0]
+    for first in range(0, x_ref.shape[1], rows):
+        out_ref[pl.ds(first, rows), :] = x_ref[:, slice(first, first + rows)].T
 
 
 def values_kernel(moved_ref, out_ref):
@@ -265,42 +308,117 @@
 def gather_columns(block, axis):
     size = lax.axis_size(axis)
     if size != 2:
-        return lax.all_gather(block, axis, axis=1, tiled=True)
+        whole = lax.all_gather(block, axis, axis=1, tiled=True)
+        return [whole], whole
     other = swap(block, axis, size, 1)
     first = lax.axis_index(axis) == 0
-    return jnp.concatenate(
+    return [block, other], jnp.concatenate(
         [jnp.where(first, block, other), jnp.where(first, other, block)], axis=1
     )
 
 
-def line_reduce_scatter(parts, size, inner, beside):
+def turn(part):
+    return call(transpose_kernel, [struct(part.shape[::-1], BF16)], (part,))[0]
+
+
+def layer_grads(halves, inner, after):
+    order = [0]
+    bit = inner // 2
+    while bit:
+        order = order + [i ^ bit for i in order]
+        bit //= 2
+    turned = [turn(part) for part in halves]
+    if inner == 1:
+        return order, [[part] for part in turned]
+    seq = lax.axis_size("seq")
+    across = [swap(turned[0], "seq", seq, inner // 2)]
+    if len(turned) == 2:
+        late, _ = lax.optimization_barrier((across[0], after))
+        across.append(swap(late, "tp", 2, 1))
+    return order, [list(pair) for pair in zip(turned, across)]
+
+
+def outer_kernel(*refs, groups, tiles):
+    *lhs_refs, rhs_ref, out_ref = refs
+    count = len(lhs_refs) // groups
+    depth = lhs_refs[0].shape[1]
+    for group in range(groups):
+
+        @pl.when(pl.program_id(0) // tiles == group)
+        def _():
+            total = 0.0
+            for i, ref in enumerate(lhs_refs[group * count : (group + 1) * count]):
+                total = total + matmul(ref[...], rhs_ref[pl.ds(i * depth, depth), :])
+            out_ref[...] = total.astype(BF16)
+
+
+def outer_product(groups, rhs):
+    rows, depth = groups[0][0].shape
+    tile = math.gcd(rows, 1024)
+    tiles = rows // tile
+    wide = rhs.shape[1]
+
+    def lhs_spec(group):
+        return pl.BlockSpec(
+            (tile, depth), lambda i: (jnp.clip(i - group * tiles, 0, tiles - 1), 0)
+        )
+
+    flat = [part for group in groups for part in group]
+    total = rows * len(groups)
+    return pl.pallas_call(
+        functools.partial(outer_kernel, groups=len(groups), tiles=tiles),
+        grid=(len(groups) * tiles,),
+        out_shape=struct((total, wide), BF16),
+        in_specs=[lhs_spec(i) for i, group in enumerate(groups) for _ in group]
+        + [pl.BlockSpec(rhs.shape, lambda i: (0, 0))],
+        out_specs=pl.BlockSpec((tile, wide), lambda i: (i, 0)),
+        compiler_params=pltpu.CompilerParams(vmem_limit_bytes=VMEM_BYTES),
+        cost_estimate=pl.CostEstimate(
+            flops=4 * total * rhs.shape[0] * wide,
+            bytes_accessed=2 * (len(flat) * rows * depth + total * wide),
+            transcendentals=0,
+        ),
+    )(*flat, rhs)
+
+
+def line_reduce_scatter(chunks, size, inner, shift, beside, later):
     outer = size // inner
     z = lax.axis_index("seq") // inner
-    total = lax.dynamic_index_in_dim(parts, z, 0, keepdims=False).astype(F32)
-    right = left = None
+
+    def block_of(parts, at):
+        return lax.dynamic_index_in_dim(parts, at ^ shift, 0, keepdims=False)
+
+    totals = [block_of(parts, z).astype(F32) for parts in chunks]
+    flows = [None] * len(chunks)
     for step in range(1, outer):
-        ahead = lax.dynamic_index_in_dim(
-            parts, jnp.minimum(z + outer - step, outer - 1), 0, keepdims=False
-        )
-        behind = lax.dynamic_index_in_dim(
-            parts, jnp.maximum(z - outer + step, 0), 0, keepdims=False
-        )
-        if right is not None:
-            ahead = (ahead.astype(F32) + right.astype(F32)).astype(BF16)
-            behind = (behind.astype(F32) + left.astype(F32)).astype(BF16)
         to_right = [(i, i + inner) for i in range(size) if i // inner < step]
         to_left = [(i, i - inner) for i in range(size) if i // inner >= outer - step]
-        right = lax.ppermute(ahead, "seq", to_right)
-        left = lax.ppermute(behind, "seq", to_left)
+        for i, parts in enumerate(chunks):
+            ahead = block_of(parts, jnp.minimum(z + outer - step, outer - 1))
+            behind = block_of(parts, jnp.maximum(z - outer + step, 0))
+            if flows[i] is not None:
+                right, left = lax.optimization_barrier(flows[i])
+                ahead = (ahead.astype(F32) + right.astype(F32)).astype(BF16)
+                behind = (behind.astype(F32) + left.astype(F32)).astype(BF16)
+                ahead, behind = lax.optimization_barrier((ahead, behind))
+            flows[i] = (
+                lax.ppermute(ahead, "seq", to_right),
+                lax.ppermute(behind, "seq", to_left),
+            )
         if step == 1:
-            right, left, beside = lax.optimization_barrier((right, left, beside))
-    if right is not None:
-        total = total + right.astype(F32) + left.astype(F32)
-    return total, beside
-
-
-def exchange(blocks):
-    return lax.all_to_all(blocks, "seq", split_axis=0, concat_axis=0, tiled=True)
+            *flows[-1], beside, later = lax.optimization_barrier((*flows[-1], beside, later))
+    if outer > 1:
+        totals = [
+            total + right.astype(F32) + left.astype(F32)
+            for total, (right, left) in zip(totals, flows)
+        ]
+    return totals, beside, later
+
+
+def exchange(blocks, groups=None):
+    return lax.all_to_all(
+        blocks, "seq", split_axis=0, concat_axis=0, tiled=True, axis_index_groups=groups
+    )
 
 
 def on_device(values, gate, out_grad, out_weight, filt, decay):
@@ -315,13 +433,13 @@
     half = length // RADIX
     there, back = middle_tables(length)
     blocks = struct((seq, rows, own), BF16)
-    spectrum = struct((half + 1, 2 * RADIX, own), F32)
-    mid = pltpu.VMEM((half + 1, 2 * RADIX, own), BF16)
-    inner_flops = 2 * (half + 1) * (2 * RADIX) ** 2 * own
+    spectrum = struct((half + 1, 2 * RADIX, 2 * own), F32)
+    mid = pltpu.VMEM((half + 1, 2 * RADIX, 2 * own), BF16)
+    work = 300 * (half + 1) * RADIX**2 * own
     start = (me * rows).astype(jnp.int32)[None]
     rates = decay[None, :]
 
-    full_grad = gather_columns(out_grad, "tp")
+    halves, full_grad = gather_columns(out_grad, "tp")
     (packed,) = call(
         functools.partial(pack_kernel, length=length),
         [struct((seq, 2, rows, own), BF16)],
@@ -335,65 +453,82 @@
     gated_grad, moved = lax.optimization_barrier((gated_grad, moved))
     grad_c = exchange(gated_grad)
 
-    features = full_grad.shape[1] // seq
-    by_inner = full_grad.reshape(rows, outer, inner, features)
-    bits = [0]
-    high = inner // 2
-    while high:
-        bits = bits + [bit ^ high for bit in bits]
-        high //= 2
-    grads = []
-    for bit in bits:
-        target = (me % inner) ^ bit
-        piece = lax.dynamic_index_in_dim(by_inner, target, 2, keepdims=False)
-        piece = piece.reshape(rows, outer * features)
-        grads.append(swap(piece, "seq", seq, bit) if bit else piece)
-    grads = jnp.concatenate(grads, axis=0)
-
     values_c, kernel_c = moved[:, 0], moved[:, 1]
-    spec_v, spec_k, conv_out_c = call(
+    spec, conv_out_c = call(
         conv_kernel,
-        [spectrum, spectrum, blocks],
+        [spectrum, blocks],
         (values_c, kernel_c, there, back),
-        scratch=(mid, mid),
-        flops=6 * inner_flops,
-    )
-    conv_out_c, grad_c, grads = lax.optimization_barrier((conv_out_c, grad_c, grads))
-    conv_out = exchange(conv_out_c)
+        scratch=(mid,),
+        flops=work,
+    )
+    place = (me % inner).astype(jnp.int32)[None]
+    (gates,) = call(
+        layer_pack_kernel, [struct((inner, outer, rows, own), BF16)], (gate, place), scalar=(1,)
+    )
+    gates, _ = lax.optimization_barrier((gates, moved))
+    order, grads = layer_grads(halves, inner, conv_out_c)
+    gates = [swap(gates[bit], "seq", seq, bit) if bit else gates[bit] for bit in order]
+    *gates, conv_out_c = lax.optimization_barrier((*gates, conv_out_c))
+    conv_out_c, grad_c = lax.optimization_barrier((conv_out_c, grad_c))
+    layers = [[z * inner + w for z in range(outer)] for w in range(inner)]
+    conv_out = exchange(conv_out_c.reshape(outer, inner, rows, own), layers)
 
     conv_grad_c, kernel_grad_c = call(
         grad_kernel,
         [blocks, struct((seq, rows + STEP, own), BF16)],
-        (grad_c, kernel_c, spec_v, spec_k, there, back),
-        scratch=(mid, mid),
-        flops=6 * inner_flops,
-    )
+        (grad_c, kernel_c, spec, there, back),
+        scratch=(mid,),
+        flops=work,
+    )
+    flat, _ = lax.optimization_barrier((sum(grads, []), conv_grad_c))
+    count = len(flat) // len(grads)
+    grads = [flat[i : i + count] for i in range(0, len(flat), count)]
+    bit = inner // 4
+    while bit:
+        grads = [g + [swap(part, "seq", seq, bit) for part in g] for g in grads]
+        bit //= 2
     conv_grad_c, kernel_grad_c, conv_out = lax.optimization_barrier(
         (conv_grad_c, kernel_grad_c, conv_out)
     )
     conv_grad = exchange(conv_grad_c)
 
     block = struct((rows, width), BF16)
-    d_gate, gated_out = call(out_kernel, [block, block], (conv_out, grad_y, gate))
-    outs = [gated_out]
-    high = inner // 2
-    while high:
-        outs = outs + [swap(part, "seq", seq, high) for part in outs]
-        high //= 2
-    *outs, conv_grad, kernel_grad_c = lax.optimization_barrier(
-        (*outs, conv_grad, kernel_grad_c)
+    home = struct((outer, rows, own), BF16)
+    chunks = 2 if outer % 2 == 0 else 1
+    wide = outer * own // chunks
+    parts = call(
+        functools.partial(layer_kernel, order=order),
+        [struct((inner * rows, wide), BF16)] * chunks + [home] * inner,
+        (*gates, conv_out, place),
+        scalar=(inner + 1,),
+    )
+    homes = parts[chunks:]
+    terms = [outer_product(grads, part).reshape(outer, -1, wide) for part in parts[:chunks]]
+    shift = 0
+    if len(grads) == 2:
+        shift = lax.axis_index("tp") * (outer // 2)
+
+    homes = {bit: swap(part, "seq", seq, bit) if bit else part for bit, part in zip(order, homes)}
+    homes = jnp.stack([homes[bit] for bit in range(inner)])
+    (d_gate,) = call(gate_kernel, [block], (homes, grad_y, place), scalar=(2,))
+    totals, conv_grad, kernel_grad_c = line_reduce_scatter(
+        terms, seq, inner, shift, conv_grad, kernel_grad_c
     )
     kernel_grad = exchange(kernel_grad_c)
     (d_values,) = call(values_kernel, [block], (conv_grad,))
-    terms = lax.dot_general(
-        grads,
-        jnp.concatenate(outs, axis=0),
-        (((0,), (0,)), ((), ())),
-        preferred_element_type=F32,
-    ).astype(BF16)
-    terms = terms.reshape(outer, features, width)
-    total, kernel_grad = line_reduce_scatter(terms, seq, inner, kernel_grad)
-    d_out_weight = total * norm_scale
+    pieces = []
+    for total in totals:
+        total = total.astype(BF16).reshape(inner, -1, wide)
+        for bit in range(inner):
+            piece = lax.dynamic_index_in_dim(total, (me % inner) ^ bit, 0, keepdims=False)
+            pieces.append(swap(piece, "seq", seq, bit) if bit else piece)
+    pieces = jnp.stack(pieces).reshape(chunks, inner, -1, wide)
+    (d_out_weight,) = call(
+        functools.partial(weight_kernel, scale=norm_scale, own=own),
+        [struct((pieces.shape[2], width), F32)],
+        (pieces, place),
+        scalar=(1,),
+    )
     d_filt, decay_grad = call(
         functools.partial(filt_kernel, length=length),
         [struct((rows, width), F32), struct((1, width), F32)],

time: 345 us -> 271 us (0.79)
  waiting for transfers between devices: 176 us -> 81.3 us
  starting transfers between devices: 60.1 us -> 84.9 us
  local copies, waits for them, and re-layouts: 13.7 us -> 23.8 us
  matrix products: 18.4 us -> 8.37 us
    ppermute x6 -> x12, waiting for transfers between devices: 88.6 us -> 25.6 us  [the longest x6 16.7 us: line_reduce_scatter(): lax.ppermute(ahead, 'seq', to_right)]
    ppermute x7 -> x19, waiting for transfers between devices: 84.8 us -> 45.1 us  [swap(): return lax.ppermute(array, axis, [(i, i ^ bit) for i in range(size)])]
    ppermute x6 -> x12, starting transfers between devices: 19.9 us -> 40.4 us  [the longest x6 32.8 us: line_reduce_scatter(): lax.ppermute(ahead, 'seq', to_right)]
    pallas_call x7 -> x12, Pallas kernels: 59.9 us -> 43.9 us  [call(): pl.pallas_call(kernel, out_shape=outs, in_specs=specs, out_specs=[whole]...]
    pallas_call x0 -> x2, Pallas kernels: none -> 14 us  [outer_product(): pl.pallas_call(functools.partial(outer_kernel, groups=len(groups), tiles=...]
    all_to_all x5, waiting for transfers between devices: 2.54 us -> 10.6 us  [exchange(): lax.all_to_all(blocks, 'seq', split_axis=0, concat_axis=0, tiled=True, ax...]
    dot_general x1 -> x0, matrix products: 6.98 us -> none  [on_device(): lax.dot_general(grads, jnp.concatenate(outs, axis=0), (((0,), (0,)), ((),...]
    unnamed x29 -> x61, local copies, waits for them, and re-layouts: 10.4 us -> 17.1 us
  transfers between devices with their start and end apart: 18 -> 36, of which waited for: 11 -> 12; matrix products, arithmetic and copies ran while one was open for 8% -> 9% of each run, Pallas kernels for 16% -> 20%
where the time goes in v1:
time: 271 us; the launch traced here: 270 us
  starting transfers between devices  84.9 us (31%)
  waiting for transfers between devices  81.3 us (30%)
  Pallas kernels  57.9 us (21%)
  local copies, waits for them, and re-layouts  23.8 us (9%)
  other arithmetic  12.1 us (4%)
  matrix products  8.37 us (3%)
    ppermute x19, waiting for transfers between devices, swap(): return lax.ppermute(array, axis, [(i, i ^ bit) for i in range(size)])  45.1 us
    pallas_call x12, Pallas kernels, call(): pl.pallas_call(kernel, out_shape=outs, in_specs=specs, out_specs=[whole]...  43.9 us
    ppermute x6, starting transfers between devices, line_reduce_scatter(): lax.ppermute(ahead, 'seq', to_right)  32.8 us
    all_to_all x5, starting transfers between devices, exchange(): lax.all_to_all(blocks, 'seq', split_axis=0, concat_axis=0, tiled=True, ax...  32.1 us
    unnamed x61, local copies, waits for them, and re-layouts  17.1 us
    ppermute x6, waiting for transfers between devices, line_reduce_scatter(): lax.ppermute(ahead, 'seq', to_right)  16.7 us
    pallas_call x2, Pallas kernels, outer_product(): pl.pallas_call(functools.partial(outer_kernel, groups=len(groups), tiles=...  14 us
    ppermute x19, starting transfers between devices, swap(): return lax.ppermute(array, axis, [(i, i ^ bit) for i in range(size)])  12.5 us
  transfers between devices with their start and end apart: 36, of which 12 were waited for; matrix products, arithmetic and copies ran while one was open for 9% of the time, Pallas kernels for 20%

profile of v1, /device:TPU:0, one launch (start us, length us, event | category | flops | bytes accessed | tf_op | source)
XLA Modules:
  0.0 269.5 jit_solution(4152557310762146736)
XLA Ops:
  6.0 7.5 %all-to-all-start = ((bf16[16,2,256,128]{3,2,1,0:T(8,128)(2,1)}), bf16[16,2,256,128]{3,2,1,0:T(8,128)(2,1)}, u32[]{:S(2)}, u32[]{:S(2)}) async-start(bf16[16,2,256,128]{3,2,1,0:T(8,128)(2,1)} %shard_map.122), calls=%async_computation | async-start | bytes 4194304 | tf_op jit(solution)/shard_map/all_to_all | solution.py:419
  18.5 20.5 %collective-permute-done.1.x_ref = bf16[256,2048]{1,0:T(8,128)(2,1)S(1)} collective-permute-done((bf16[256,2048]{1,0:T(8,128)(2,1)S(1)}, bf16[256,2048]{1,0:T(8,128)(2,1)S(1)}, u32[]{:S(2)}, u32[]{:S(2)}) %collective-permute-start.1) | collective-permute-done | bytes 1048608 | tf_op jit(solution)/shard_map/ppermute | solution.py:305
  39.2 8.4 %convolution_convert_fusion.grad_ref = bf16[256,2048]{1,0:T(8,128)(2,1)S(1)} fusion(bf16[4096,2048]{1,0:T(8,128)(2,1)} %param.11, bf16[256,2048]{1,0:T(8,128)(2,1)S(1)} %get-tuple-element.120, bf16[256,2048]{1,0:T(8,128)(2,1)S(1)} %get-tuple-element.119), kind=kOutput, calls=%fused_computation | convolution fusion | flops 4299685888 | bytes 19922944 | tf_op jit(solution)/shard_map/dot_general | solution.py:451
  50.2 4.7 %all-to-all-done = bf16[16,2,256,128]{3,2,1,0:T(8,128)(2,1)} async-done(((bf16[16,2,256,128]{3,2,1,0:T(8,128)(2,1)}), bf16[16,2,256,128]{3,2,1,0:T(8,128)(2,1)}, u32[]{:S(2)}, u32[]{:S(2)}) %all-to-all-start) | async-done | bytes 2097184 | tf_op jit(solution)/shard_map/all_to_all | solution.py:419
  58.0 11.3 %all-to-all-start.1 = ((bf16[16,256,128]{2,1,0:T(8,128)(2,1)}), bf16[16,256,128]{2,1,0:T(8,128)(2,1)S(1)}, u32[]{:S(2)}, u32[]{:S(2)}) async-start(bf16[16,256,128]{2,1,0:T(8,128)(2,1)} %shard_map.121), calls=%async_computation.1 | async-start | bytes 2097152 | tf_op jit(solution)/shard_map/all_to_all | solution.py:419
  71.6 15.7 %shard_map.123 = (f32[33,256,256]{2,1,0:T(8,128)}, bf16[16,256,128]{2,1,0:T(8,128)(2,1)S(1)}) custom-call(bf16[16,256,128]{2,1,0:T(8,128)(2,1)S(1)} %copy-done.13, bf16[16,256,128]{2,1,0:T(8,128)(2,1)S(1)} %copy-done.11, bf16[33,256,256]{2,1,0:T(8,128)(2,1)} %constant.120.clone.there_ref, bf16[33,256,256]{2,1,0:T(8,128)(2,1)} %constant.121.clone.back_ref), custom_call_target="tpu_custom_call" | custom-call | flops 20761804800 | bytes 20447232 | tf_op jit(solution)/shard_map/pallas_call | solution.py:289
  96.1 4.5 %all-to-all-start.2 = ((bf16[4,4,256,128]{3,2,1,0:T(8,128)(2,1)}), bf16[4,4,256,128]{3,2,1,0:T(8,128)(2,1)S(1)}, u32[]{:S(2)}, u32[]{:S(2)}) async-start(bf16[4,4,256,128]{3,2,1,0:T(8,128)(2,1)} %bitcast.90), calls=%async_computation.2 | async-start | bytes 2097152 | tf_op jit(solution)/shard_map/all_to_all | solution.py:419
  103.0 15.2 %shard_map.125 = (bf16[16,256,128]{2,1,0:T(8,128)(2,1)S(1)}, bf16[16,272,128]{2,1,0:T(8,128)(2,1)S(1)}) custom-call(bf16[16,256,128]{2,1,0:T(8,128)(2,1)S(1)} %copy-done.8, bf16[16,256,128]{2,1,0:T(8,128)(2,1)S(1)} %copy-done.12, f32[33,256,256]{2,1,0:T(8,128)} %get-tuple-element.62.spec_ref, bf16[33,256,256]{2,1,0:T(8,128)(2,1)} %constant.120.clone.there_ref, ...), custom_call_target="tpu_custom_call" | custom-call | flops 20761804800 | bytes 21561344 | tf_op jit(solution)/shard_map/pallas_call | solution.py:289
  121.3 5.9 %all-to-all-done.2.refs_4_ = bf16[4,4,256,128]{3,2,1,0:T(8,128)(2,1)S(1)} async-done(((bf16[4,4,256,128]{3,2,1,0:T(8,128)(2,1)}), bf16[4,4,256,128]{3,2,1,0:T(8,128)(2,1)S(1)}, u32[]{:S(2)}, u32[]{:S(2)}) %all-to-all-start.2) | async-done | bytes 1048608 | tf_op jit(solution)/shard_map/all_to_all | solution.py:419
  127.2 3.7 %all-to-all-start.3 = ((bf16[16,256,128]{2,1,0:T(8,128)(2,1)}), bf16[16,256,128]{2,1,0:T(8,128)(2,1)S(1)}, u32[]{:S(2)}, u32[]{:S(2)}) async-start(bf16[16,256,128]{2,1,0:T(8,128)(2,1)} %copy-done.6), calls=%async_computation.3 | async-start | bytes 2097152 | tf_op jit(solution)/shard_map/all_to_all | solution.py:419
  137.0 7.0 %shard_map.131 = bf16[4096,256]{1,0:T(8,128)(2,1)} custom-call(bf16[2048,256]{1,0:T(8,128)(2,1)} %shard_map.119.refs_0_, bf16[2048,256]{1,0:T(8,128)(2,1)} %collective-permute-done.refs_1_, bf16[2048,256]{1,0:T(8,128)(2,1)} %collective-permute-done.6.refs_2_, bf16[2048,256]{1,0:T(8,128)(2,1)} %collective-permute-done.7.refs_3_, ...), custom_call_target="tpu_custom_call" | custom-call | flops 4294967296 | bytes 10485760 | tf_op jit(solution)/shard_map/pallas_call | solution.py:368
  145.3 4.5 %collective-permute-start.15 = (bf16[1024,256]{1,0:T(8,128)(2,1)S(1)}, bf16[1024,256]{1,0:T(8,128)(2,1)}, u32[]{:S(2)}, u32[]{:S(2)}) collective-permute-start(bf16[1024,256]{1,0:T(8,128)(2,1)S(1)} %get-tuple-element.114), channel_id=1, source_target_pairs={{0,8},{2,10},{4,12},{6,14},{1,9},{3,11},{5,13},{7,15}} | collective-permute-start | bytes 1572872 | tf_op jit(solution)/shard_map/ppermute | solution.py:405
  151.3 6.9 %shard_map.127 = bf16[4096,256]{1,0:T(8,128)(2,1)} custom-call(bf16[2048,256]{1,0:T(8,128)(2,1)} %shard_map.119.refs_0_, bf16[2048,256]{1,0:T(8,128)(2,1)} %collective-permute-done.refs_1_, bf16[2048,256]{1,0:T(8,128)(2,1)} %collective-permute-done.6.refs_2_, bf16[2048,256]{1,0:T(8,128)(2,1)} %collective-permute-done.7.refs_3_, ...), custom_call_target="tpu_custom_call" | custom-call | flops 4294967296 | bytes 10485760 | tf_op jit(solution)/shard_map/pallas_call | solution.py:368
  164.0 9.6 %collective-permute-done.10 = bf16[1024,256]{1,0:T(8,128)(2,1)} collective-permute-done((bf16[1024,256]{1,0:T(8,128)(2,1)}, bf16[1024,256]{1,0:T(8,128)(2,1)}, u32[]{:S(2)}, u32[]{:S(2)}) %collective-permute-start.10) | collective-permute-done | bytes 524320 | tf_op jit(solution)/shard_map/ppermute | solution.py:405
  173.5 3.8 %fusion.4 = (bf16[1024,256]{1,0:T(8,128)(2,1)}, bf16[1024,256]{1,0:T(8,128)(2,1)}, bf16[1024,256]{1,0:T(8,128)(2,1)}, bf16[1024,256]{1,0:T(8,128)(2,1)}) fusion(bf16[1024,256]{1,0:T(8,128)(2,1)} %collective-permute-done.11, bf16[4,1024,256]{2,1,0:T(8,128)(2,1)} %bitcast.99, s32[]{:T(128)S(6)} %select_n.95, bf16[1024,256]{1,0:T(8,128)(2,1)} %collective-permute-done.10, ...), kind=kLoop, calls=%fused_computation.10 | loop fusion | flops 4194304 | bytes 6291464 | tf_op jit(solution)/shard_map/convert_element_type | solution.py:402
  177.3 5.2 %collective-permute-start.17 = (bf16[1024,256]{1,0:T(8,128)(2,1)}, bf16[1024,256]{1,0:T(8,128)(2,1)}, u32[]{:S(2)}, u32[]{:S(2)}) collective-permute-start(bf16[1024,256]{1,0:T(8,128)(2,1)} %get-tuple-element.89), channel_id=1, source_target_pairs={{0,8},{2,10},{4,12},{6,14},{8,16},{10,18},{12,20},{14,22},{1,9},{3... | collective-permute-start | bytes 1572872 | tf_op jit(solution)/shard_map/ppermute | solution.py:405
  183.9 3.9 %collective-permute-start.24 = (bf16[1024,256]{1,0:T(8,128)(2,1)}, bf16[1024,256]{1,0:T(8,128)(2,1)S(1)}, u32[]{:S(2)}, u32[]{:S(2)}) collective-permute-start(bf16[1024,256]{1,0:T(8,128)(2,1)} %get-tuple-element.99), channel_id=1, source_target_pairs={{0,8},{2,10},{4,12},{6,14},{8,16},{10,18},{12,20},{14,22},{1,9},{3... | collective-permute-start | bytes 1572872 | tf_op jit(solution)/shard_map/ppermute | solution.py:405
  188.6 5.7 %collective-permute-done.17 = bf16[1024,256]{1,0:T(8,128)(2,1)} collective-permute-done((bf16[1024,256]{1,0:T(8,128)(2,1)}, bf16[1024,256]{1,0:T(8,128)(2,1)}, u32[]{:S(2)}, u32[]{:S(2)}) %collective-permute-start.17) | collective-permute-done | bytes 524320 | tf_op jit(solution)/shard_map/ppermute | solution.py:405
  197.1 10.2 %collective-permute-start.19 = (bf16[1024,256]{1,0:T(8,128)(2,1)}, bf16[1024,256]{1,0:T(8,128)(2,1)}, u32[]{:S(2)}, u32[]{:S(2)}) collective-permute-start(bf16[1024,256]{1,0:T(8,128)(2,1)} %get-tuple-element.93), channel_id=1, source_target_pairs={{0,8},{2,10},{4,12},{6,14},{8,16},{10,18},{12,20},{14,22},{16,24},... | collective-permute-start | bytes 1572872 | tf_op jit(solution)/shard_map/ppermute | solution.py:405
  209.9 6.9 %collective-permute-start.26 = (bf16[1024,256]{1,0:T(8,128)(2,1)}, bf16[1024,256]{1,0:T(8,128)(2,1)}, u32[]{:S(2)}, u32[]{:S(2)}) collective-permute-start(bf16[1024,256]{1,0:T(8,128)(2,1)} %get-tuple-element.103), channel_id=1, source_target_pairs={{0,8},{2,10},{4,12},{6,14},{8,16},{10,18},{12,20},{14,22},{16,24},... | collective-permute-start | bytes 1572872 | tf_op jit(solution)/shard_map/ppermute | solution.py:405
  218.2 5.0 %all-to-all-start.4 = ((bf16[16,272,128]{2,1,0:T(8,128)(2,1)}), bf16[16,272,128]{2,1,0:T(8,128)(2,1)S(1)}, u32[]{:S(2)}, u32[]{:S(2)}) async-start(bf16[16,272,128]{2,1,0:T(8,128)(2,1)} %copy-done.5), calls=%async_computation.4 | async-start | bytes 2228224 | tf_op jit(solution)/shard_map/all_to_all | solution.py:419
  228.3 8.8 %collective-permute-done.27 = bf16[1024,256]{1,0:T(8,128)(2,1)} collective-permute-done((bf16[1024,256]{1,0:T(8,128)(2,1)}, bf16[1024,256]{1,0:T(8,128)(2,1)}, u32[]{:S(2)}, u32[]{:S(2)}) %collective-permute-start.27) | collective-permute-done | bytes 524320 | tf_op jit(solution)/shard_map/ppermute | solution.py:406
  238.9 13.2 %collective-permute-done.22 = bf16[256,256]{1,0:T(8,128)(2,1)S(1)} collective-permute-done((bf16[256,256]{1,0:T(8,128)(2,1)S(1)}, bf16[256,256]{1,0:T(8,128)(2,1)S(1)}, u32[]{:S(2)}, u32[]{:S(2)}) %collective-permute-start.22) | collective-permute-done | bytes 131104 | tf_op jit(solution)/shard_map/ppermute | solution.py:305
  260.2 5.0 %collective-permute-done.29 = bf16[256,256]{1,0:T(8,128)(2,1)S(1)} collective-permute-done((bf16[256,256]{1,0:T(8,128)(2,1)S(1)}, bf16[256,256]{1,0:T(8,128)(2,1)S(1)}, u32[]{:S(2)}, u32[]{:S(2)}) %collective-permute-start.29) | collective-permute-done | bytes 131104 | tf_op jit(solution)/shard_map/ppermute | solution.py:305
  (138 shorter events, 75.2 us)
Async XLA Ops:
  6.0 48.9 %all-to-all-start = ((bf16[16,2,256,128]{3,2,1,0:T(8,128)(2,1)}), bf16[16,2,256,128]{3,2,1,0:T(8,128)(2,1)}, u32[]{:S(2)}, u32[]{:S(2)}) async-start(bf16[16,2,256,128]{3,2,1,0:T(8,128)(2,1)} %shard_map.122), calls=%async_computation | async-start | bytes 4194304 | tf_op jit(solution)/shard_map/all_to_all | solution.py:419
  13.5 25.5 %collective-permute-start.1 = (bf16[256,2048]{1,0:T(8,128)(2,1)S(1)}, bf16[256,2048]{1,0:T(8,128)(2,1)S(1)}, u32[]{:S(2)}, u32[]{:S(2)}) collective-permute-start(bf16[256,2048]{1,0:T(8,128)(2,1)S(1)} %copy-done.1), channel_id=1, source_target_pairs={{0,1},{1,0},{2,3},{3,2},{4,5},{5,4},{6,7},{7,6},{8,9},{9,8},{10,11... | collective-permute-start | bytes 3145736 | tf_op jit(solution)/shard_map/ppermute | solution.py:305
  16.5 71.8 %collective-permute-start = (bf16[2048,256]{1,0:T(8,128)(2,1)}, bf16[2048,256]{1,0:T(8,128)(2,1)}, u32[]{:S(2)}, u32[]{:S(2)}) collective-permute-start(bf16[2048,256]{1,0:T(8,128)(2,1)} %shard_map.119.refs_0_), channel_id=1, source_target_pairs={{0,4},{2,6},{4,0},{6,2},{8,12},{10,14},{12,8},{14,10},{16,20},{18,... | collective-permute-start | bytes 3145736 | tf_op jit(solution)/shard_map/ppermute | solution.py:305
  58.0 37.1 %all-to-all-start.1 = ((bf16[16,256,128]{2,1,0:T(8,128)(2,1)}), bf16[16,256,128]{2,1,0:T(8,128)(2,1)S(1)}, u32[]{:S(2)}, u32[]{:S(2)}) async-start(bf16[16,256,128]{2,1,0:T(8,128)(2,1)} %shard_map.121), calls=%async_computation.1 | async-start | bytes 2097152 | tf_op jit(solution)/shard_map/all_to_all | solution.py:419
  69.4 20.4 %collective-permute-start.3 = (bf16[4,256,128]{2,1,0:T(8,128)(2,1)S(1)}, bf16[4,256,128]{2,1,0:T(8,128)(2,1)S(1)}, u32[]{:S(2)}, u32[]{:S(2)}) collective-permute-start(bf16[4,256,128]{2,1,0:T(8,128)(2,1)S(1)} %get-tuple-element.123), channel_id=1, source_target_pairs={{0,4},{2,6},{4,0},{6,2},{8,12},{10,14},{12,8},{14,10},{16,20},{18,... | collective-permute-start | bytes 786440 | tf_op jit(solution)/shard_map/ppermute | solution.py:305
  71.4 19.2 %collective-permute-start.4 = (bf16[4,256,128]{2,1,0:T(8,128)(2,1)S(1)}, bf16[4,256,128]{2,1,0:T(8,128)(2,1)S(1)}, u32[]{:S(2)}, u32[]{:S(2)}) collective-permute-start(bf16[4,256,128]{2,1,0:T(8,128)(2,1)S(1)} %get-tuple-element.122), channel_id=1, source_target_pairs={{0,2},{2,0},{4,6},{6,4},{8,10},{10,8},{12,14},{14,12},{16,18},{18,... | collective-permute-start | bytes 786440 | tf_op jit(solution)/shard_map/ppermute | solution.py:305
  71.4 23.0 %collective-permute-start.5 = (bf16[4,256,128]{2,1,0:T(8,128)(2,1)S(1)}, bf16[4,256,128]{2,1,0:T(8,128)(2,1)S(1)}, u32[]{:S(2)}, u32[]{:S(2)}) collective-permute-start(bf16[4,256,128]{2,1,0:T(8,128)(2,1)S(1)} %get-tuple-element.121), channel_id=1, source_target_pairs={{0,6},{2,4},{4,2},{6,0},{8,14},{10,12},{12,10},{14,8},{16,22},{18,... | collective-permute-start | bytes 786440 | tf_op jit(solution)/shard_map/ppermute | solution.py:305
  88.3 32.0 %collective-permute-start.2 = (bf16[2048,256]{1,0:T(8,128)(2,1)}, bf16[2048,256]{1,0:T(8,128)(2,1)}, u32[]{:S(2)}, u32[]{:S(2)}) collective-permute-start(bf16[2048,256]{1,0:T(8,128)(2,1)} %collective-permute-done.refs_1_), channel_id=1, source_target_pairs={{0,1},{1,0},{2,3},{3,2},{4,5},{5,4},{6,7},{7,6},{8,9},{9,8},{10,11... | collective-permute-start | bytes 3145736 | tf_op jit(solution)/shard_map/ppermute | solution.py:305
  96.1 31.1 %all-to-all-start.2 = ((bf16[4,4,256,128]{3,2,1,0:T(8,128)(2,1)}), bf16[4,4,256,128]{3,2,1,0:T(8,128)(2,1)S(1)}, u32[]{:S(2)}, u32[]{:S(2)}) async-start(bf16[4,4,256,128]{3,2,1,0:T(8,128)(2,1)} %bitcast.90), calls=%async_computation.2 | async-start | bytes 2097152 | tf_op jit(solution)/shard_map/all_to_all | solution.py:419
  120.2 16.8 %collective-permute-start.6 = (bf16[2048,256]{1,0:T(8,128)(2,1)}, bf16[2048,256]{1,0:T(8,128)(2,1)}, u32[]{:S(2)}, u32[]{:S(2)}) collective-permute-start(bf16[2048,256]{1,0:T(8,128)(2,1)} %shard_map.119.refs_0_), channel_id=1, source_target_pairs={{0,2},{2,0},{4,6},{6,4},{8,10},{10,8},{12,14},{14,12},{16,18},{18,... | collective-permute-start | bytes 3145736 | tf_op jit(solution)/shard_map/ppermute | solution.py:305
  120.7 16.4 %collective-permute-start.7 = (bf16[2048,256]{1,0:T(8,128)(2,1)}, bf16[2048,256]{1,0:T(8,128)(2,1)}, u32[]{:S(2)}, u32[]{:S(2)}) collective-permute-start(bf16[2048,256]{1,0:T(8,128)(2,1)} %collective-permute-done.refs_1_), channel_id=1, source_target_pairs={{0,2},{2,0},{4,6},{6,4},{8,10},{10,8},{12,14},{14,12},{16,18},{18,... | collective-permute-start | bytes 3145736 | tf_op jit(solution)/shard_map/ppermute | solution.py:305
  127.2 46.3 %all-to-all-start.3 = ((bf16[16,256,128]{2,1,0:T(8,128)(2,1)}), bf16[16,256,128]{2,1,0:T(8,128)(2,1)S(1)}, u32[]{:S(2)}, u32[]{:S(2)}) async-start(bf16[16,256,128]{2,1,0:T(8,128)(2,1)} %copy-done.6), calls=%async_computation.3 | async-start | bytes 2097152 | tf_op jit(solution)/shard_map/all_to_all | solution.py:419
  145.3 18.7 %collective-permute-start.15 = (bf16[1024,256]{1,0:T(8,128)(2,1)S(1)}, bf16[1024,256]{1,0:T(8,128)(2,1)}, u32[]{:S(2)}, u32[]{:S(2)}) collective-permute-start(bf16[1024,256]{1,0:T(8,128)(2,1)S(1)} %get-tuple-element.114), channel_id=1, source_target_pairs={{0,8},{2,10},{4,12},{6,14},{1,9},{3,11},{5,13},{7,15}} | collective-permute-start | bytes 1572872 | tf_op jit(solution)/shard_map/ppermute | solution.py:405
  177.3 17.1 %collective-permute-start.17 = (bf16[1024,256]{1,0:T(8,128)(2,1)}, bf16[1024,256]{1,0:T(8,128)(2,1)}, u32[]{:S(2)}, u32[]{:S(2)}) collective-permute-start(bf16[1024,256]{1,0:T(8,128)(2,1)} %get-tuple-element.89), channel_id=1, source_target_pairs={{0,8},{2,10},{4,12},{6,14},{8,16},{10,18},{12,20},{14,22},{1,9},{3... | collective-permute-start | bytes 1572872 | tf_op jit(solution)/shard_map/ppermute | solution.py:405
  183.9 24.7 %collective-permute-start.24 = (bf16[1024,256]{1,0:T(8,128)(2,1)}, bf16[1024,256]{1,0:T(8,128)(2,1)S(1)}, u32[]{:S(2)}, u32[]{:S(2)}) collective-permute-start(bf16[1024,256]{1,0:T(8,128)(2,1)} %get-tuple-element.99), channel_id=1, source_target_pairs={{0,8},{2,10},{4,12},{6,14},{8,16},{10,18},{12,20},{14,22},{1,9},{3... | collective-permute-start | bytes 1572872 | tf_op jit(solution)/shard_map/ppermute | solution.py:405
  187.9 20.7 %collective-permute-start.25 = (bf16[1024,256]{1,0:T(8,128)(2,1)}, bf16[1024,256]{1,0:T(8,128)(2,1)S(1)}, u32[]{:S(2)}, u32[]{:S(2)}) collective-permute-start(bf16[1024,256]{1,0:T(8,128)(2,1)} %get-tuple-element.100), channel_id=1, source_target_pairs={{16,8},{18,10},{20,12},{22,14},{24,16},{26,18},{28,20},{30,22},{17... | collective-permute-start | bytes 1572872 | tf_op jit(solution)/shard_map/ppermute | solution.py:406
  197.1 26.1 %collective-permute-start.19 = (bf16[1024,256]{1,0:T(8,128)(2,1)}, bf16[1024,256]{1,0:T(8,128)(2,1)}, u32[]{:S(2)}, u32[]{:S(2)}) collective-permute-start(bf16[1024,256]{1,0:T(8,128)(2,1)} %get-tuple-element.93), channel_id=1, source_target_pairs={{0,8},{2,10},{4,12},{6,14},{8,16},{10,18},{12,20},{14,22},{16,24},... | collective-permute-start | bytes 1572872 | tf_op jit(solution)/shard_map/ppermute | solution.py:405
  207.3 18.0 %collective-permute-start.20 = (bf16[1024,256]{1,0:T(8,128)(2,1)}, bf16[1024,256]{1,0:T(8,128)(2,1)}, u32[]{:S(2)}, u32[]{:S(2)}) collective-permute-start(bf16[1024,256]{1,0:T(8,128)(2,1)} %get-tuple-element.94), channel_id=1, source_target_pairs={{8,0},{10,2},{12,4},{14,6},{16,8},{18,10},{20,12},{22,14},{24,16},... | collective-permute-start | bytes 1572872 | tf_op jit(solution)/shard_map/ppermute | solution.py:406
  209.9 18.4 %collective-permute-start.26 = (bf16[1024,256]{1,0:T(8,128)(2,1)}, bf16[1024,256]{1,0:T(8,128)(2,1)}, u32[]{:S(2)}, u32[]{:S(2)}) collective-permute-start(bf16[1024,256]{1,0:T(8,128)(2,1)} %get-tuple-element.103), channel_id=1, source_target_pairs={{0,8},{2,10},{4,12},{6,14},{8,16},{10,18},{12,20},{14,22},{16,24},... | collective-permute-start | bytes 1572872 | tf_op jit(solution)/shard_map/ppermute | solution.py:405
  216.8 20.4 %collective-permute-start.27 = (bf16[1024,256]{1,0:T(8,128)(2,1)}, bf16[1024,256]{1,0:T(8,128)(2,1)}, u32[]{:S(2)}, u32[]{:S(2)}) collective-permute-start(bf16[1024,256]{1,0:T(8,128)(2,1)} %get-tuple-element.104), channel_id=1, source_target_pairs={{8,0},{10,2},{12,4},{14,6},{16,8},{18,10},{20,12},{22,14},{24,16},... | collective-permute-start | bytes 1572872 | tf_op jit(solution)/shard_map/ppermute | solution.py:406
  218.1 37.0 %collective-permute-start.12 = (bf16[4,256,128]{2,1,0:T(8,128)(2,1)}, bf16[4,256,128]{2,1,0:T(8,128)(2,1)}, u32[]{:S(2)}, u32[]{:S(2)}) collective-permute-start(bf16[4,256,128]{2,1,0:T(8,128)(2,1)} %get-tuple-element.80), channel_id=1, source_target_pairs={{0,2},{2,0},{4,6},{6,4},{8,10},{10,8},{12,14},{14,12},{16,18},{18,... | collective-permute-start | bytes 786440 | tf_op jit(solution)/shard_map/ppermute | solution.py:305
  218.2 49.5 %all-to-all-start.4 = ((bf16[16,272,128]{2,1,0:T(8,128)(2,1)}), bf16[16,272,128]{2,1,0:T(8,128)(2,1)S(1)}, u32[]{:S(2)}, u32[]{:S(2)}) async-start(bf16[16,272,128]{2,1,0:T(8,128)(2,1)} %copy-done.5), calls=%async_computation.4 | async-start | bytes 2228224 | tf_op jit(solution)/shard_map/all_to_all | solution.py:419
  223.3 31.9 %collective-permute-start.13 = (bf16[4,256,128]{2,1,0:T(8,128)(2,1)}, bf16[4,256,128]{2,1,0:T(8,128)(2,1)S(1)}, u32[]{:S(2)}, u32[]{:S(2)}) collective-permute-start(bf16[4,256,128]{2,1,0:T(8,128)(2,1)} %copy-done.26), channel_id=1, source_target_pairs={{0,4},{2,6},{4,0},{6,2},{8,12},{10,14},{12,8},{14,10},{16,20},{18,... | collective-permute-start | bytes 786440 | tf_op jit(solution)/shard_map/ppermute | solution.py:305
  225.3 29.9 %collective-permute-start.14 = (bf16[4,256,128]{2,1,0:T(8,128)(2,1)S(1)}, bf16[4,256,128]{2,1,0:T(8,128)(2,1)S(1)}, u32[]{:S(2)}, u32[]{:S(2)}) collective-permute-start(bf16[4,256,128]{2,1,0:T(8,128)(2,1)S(1)} %copy-done.25), channel_id=1, source_target_pairs={{0,6},{2,4},{4,2},{6,0},{8,14},{10,12},{12,10},{14,8},{16,22},{18,... | collective-permute-start | bytes 786440 | tf_op jit(solution)/shard_map/ppermute | solution.py:305
  (40 other events, 293.9 us)

commit v2 on v1

--- a/solution.py
+++ b/solution.py
@@ -77,16 +77,18 @@
     return [point for pair in zip(even, odd) for point in pair]
 
 
-def load_points(ref, chunk, half):
-    per = ref.shape[1] // RADIX
-    return [ref[p // per, pl.ds((p % per) * RADIX + chunk * STEP, STEP), :] for p in range(half)]
-
-
-def outer_forward(x_ref, mid_ref, lanes):
+def load_points(ref, chunk, half, field=0):
+    per = ref.shape[2] // RADIX
+    return [
+        ref[p // per, field, pl.ds((p % per) * RADIX + chunk * STEP, STEP), :] for p in range(half)
+    ]
+
+
+def outer_forward(x_ref, mid_ref, lanes, field=0):
     half = mid_ref.shape[0] - 1
 
     def chunk_body(chunk, carry):
-        points = [x.astype(F32) for x in load_points(x_ref, chunk, half)]
+        points = [x.astype(F32) for x in load_points(x_ref, chunk, half, field)]
         re, im = real_forward(points + [None] * half)
         for k in range(half + 1):
             mid_ref[k, pl.ds(chunk * STEP, STEP), lanes] = re[k].astype(BF16)
@@ -125,13 +127,13 @@
     return max(d for d in range(1, 14) if count % d == 0)
 
 
-def conv_kernel(v_ref, k_ref, there_ref, back_ref, spec_ref, out_ref, mid):
+def conv_kernel(fields_ref, there_ref, back_ref, spec_ref, out_ref, mid):
     half = mid.shape[0] - 1
     own = out_ref.shape[2]
     low, high = slice(0, own), slice(own, 2 * own)
     scale = 0.5 / (half * RADIX)
-    outer_forward(v_ref, mid, low)
-    outer_forward(k_ref, mid, high)
+    outer_forward(fields_ref, mid, low, 0)
+    outer_forward(fields_ref, mid, high, 1)
 
     def freq_body(k, carry):
         spec = matmul(there_ref[k], mid[k])
@@ -151,7 +153,7 @@
     lax.fori_loop(0, RADIX // STEP, chunk_body, 0)
 
 
-def grad_kernel(g_ref, k_ref, spec_ref, there_ref, back_ref, cg_ref, kg_ref, mid):
+def grad_kernel(g_ref, fields_ref, spec_ref, there_ref, back_ref, cg_ref, kg_ref, mid):
     half = mid.shape[0] - 1
     length = half * RADIX
     own = cg_ref.shape[2]
@@ -166,14 +168,14 @@
         return carry
 
     lax.fori_loop(0, half + 1, freq_body, 0, unroll=unrolled(half + 1))
-    rows = g_ref.shape[1]
+    rows = g_ref.shape[2]
     per = rows // RADIX
 
     def chunk_body(chunk, total):
         for p, point in enumerate(outer_backward(mid, chunk, scale, high)):
             here = pl.ds((p % per) * RADIX + chunk * STEP, STEP)
             cg_ref[p // per, here, :] = point.astype(BF16)
-        kernel = load_points(k_ref, chunk, half)
+        kernel = load_points(fields_ref, chunk, half, 1)
         first = lax.broadcasted_iota(jnp.int32, total.shape, 0) + chunk * STEP
         for p, point in enumerate(outer_backward(mid, chunk, scale, low)):
             here = pl.ds((p % per) * RADIX + chunk * STEP, STEP)
@@ -182,12 +184,12 @@
             total = total + place * point * kernel[p].astype(F32)
         return total
 
-    total = jnp.zeros((STEP, g_ref.shape[2]), F32)
+    total = jnp.zeros((STEP, own), F32)
     total = lax.fori_loop(0, RADIX // STEP, chunk_body, total)
     total = -(1.0 / math.sqrt(length)) * jnp.sum(total, axis=0, keepdims=True)
-    high = total.astype(BF16).astype(F32)
-    row = lax.broadcasted_iota(jnp.int32, (STEP, g_ref.shape[2]), 0)
-    extra = jnp.where(row == 0, high, jnp.where(row == 1, total - high, 0.0)).astype(BF16)
+    leading = total.astype(BF16).astype(F32)
+    row = lax.broadcasted_iota(jnp.int32, (STEP, own), 0)
+    extra = jnp.where(row == 0, leading, jnp.where(row == 1, total - leading, 0.0)).astype(BF16)
     for device in range(kg_ref.shape[0]):
         kg_ref[device, pl.ds(rows, STEP), :] = extra
 
@@ -205,10 +207,10 @@
 
 
 def gated_kernel(grad_ref, gate_ref, out_ref):
-    own = out_ref.shape[2]
+    own = out_ref.shape[3]
     for d in range(out_ref.shape[0]):
         cols = slice(d * own, (d + 1) * own)
-        out_ref[d] = (grad_ref[:, cols].astype(F32) * gate_ref[:, cols].astype(F32)).astype(BF16)
+        out_ref[d, 0] = (grad_ref[:, cols].astype(F32) * gate_ref[:, cols].astype(F32)).astype(BF16)
 
 
 def layer_pack_kernel(gate_ref, place_ref, out_ref):
@@ -221,17 +223,15 @@
 
 def layer_kernel(*refs, order):
     count = len(order)
-    gates, gated_refs, homes = refs[:count], refs[count + 2 : -count], refs[-count:]
-    moved_ref, place_ref = refs[count : count + 2]
+    gates, homes = refs[:count], refs[count + 3 :]
+    moved_ref, place_ref, gated_ref = refs[count : count + 3]
     outer, _, rows, own = moved_ref.shape
-    per = outer // len(gated_refs)
     for i, bit in enumerate(order):
         for z in range(outer):
             conv_out = moved_ref[z, place_ref[0] ^ bit]
             homes[i][z] = conv_out
             gated = (gates[i][z].astype(F32) * conv_out.astype(F32)).astype(BF16)
-            first = (z % per) * own
-            gated_refs[z // per][pl.ds(i * rows, rows), slice(first, first + own)] = gated
+            gated_ref[pl.ds(i * rows, rows), slice(z * own, (z + 1) * own)] = gated
 
 
 def gate_kernel(moved_ref, grad_ref, place_ref, out_ref):
@@ -338,13 +338,14 @@
     return order, [list(pair) for pair in zip(turned, across)]
 
 
-def outer_kernel(*refs, groups, tiles):
+def outer_kernel(at_ref, *refs, groups, tiles):
     *lhs_refs, rhs_ref, out_ref = refs
     count = len(lhs_refs) // groups
     depth = lhs_refs[0].shape[1]
+    tile = at_ref[0] * pl.num_programs(0) + pl.program_id(0)
     for group in range(groups):
 
-        @pl.when(pl.program_id(0) // tiles == group)
+        @pl.when(tile // tiles == group)
         def _():
             total = 0.0
             for i, ref in enumerate(lhs_refs[group * count : (group + 1) * count]):
@@ -352,67 +353,67 @@
             out_ref[...] = total.astype(BF16)
 
 
-def outer_product(groups, rhs):
+def outer_product(groups, rhs, at, blocks):
     rows, depth = groups[0][0].shape
-    tile = math.gcd(rows, 1024)
+    size = rows * len(groups) // blocks
+    tile = math.gcd(size, 512)
     tiles = rows // tile
+    steps = size // tile
     wide = rhs.shape[1]
 
     def lhs_spec(group):
         return pl.BlockSpec(
-            (tile, depth), lambda i: (jnp.clip(i - group * tiles, 0, tiles - 1), 0)
+            (tile, depth),
+            lambda i, at_ref: (
+                jnp.clip(at_ref[0] * steps + i - group * tiles, 0, tiles - 1),
+                0,
+            ),
         )
 
     flat = [part for group in groups for part in group]
-    total = rows * len(groups)
     return pl.pallas_call(
         functools.partial(outer_kernel, groups=len(groups), tiles=tiles),
-        grid=(len(groups) * tiles,),
-        out_shape=struct((total, wide), BF16),
-        in_specs=[lhs_spec(i) for i, group in enumerate(groups) for _ in group]
-        + [pl.BlockSpec(rhs.shape, lambda i: (0, 0))],
-        out_specs=pl.BlockSpec((tile, wide), lambda i: (i, 0)),
+        grid_spec=pltpu.PrefetchScalarGridSpec(
+            num_scalar_prefetch=1,
+            grid=(steps,),
+            in_specs=[lhs_spec(i) for i, group in enumerate(groups) for _ in group]
+            + [pl.BlockSpec(rhs.shape, lambda i, at_ref: (0, 0))],
+            out_specs=pl.BlockSpec((tile, wide), lambda i, at_ref: (i, 0)),
+        ),
+        out_shape=struct((size, wide), BF16),
         compiler_params=pltpu.CompilerParams(vmem_limit_bytes=VMEM_BYTES),
         cost_estimate=pl.CostEstimate(
-            flops=4 * total * rhs.shape[0] * wide,
-            bytes_accessed=2 * (len(flat) * rows * depth + total * wide),
+            flops=4 * size * rhs.shape[0] * wide,
+            bytes_accessed=2 * (len(groups[0]) * size * depth + size * wide),
             transcendentals=0,
         ),
-    )(*flat, rhs)
-
-
-def line_reduce_scatter(chunks, size, inner, shift, beside, later):
-    outer = size // inner
-    z = lax.axis_index("seq") // inner
-
-    def block_of(parts, at):
-        return lax.dynamic_index_in_dim(parts, at ^ shift, 0, keepdims=False)
-
-    totals = [block_of(parts, z).astype(F32) for parts in chunks]
-    flows = [None] * len(chunks)
-    for step in range(1, outer):
-        to_right = [(i, i + inner) for i in range(size) if i // inner < step]
-        to_left = [(i, i - inner) for i in range(size) if i // inner >= outer - step]
-        for i, parts in enumerate(chunks):
-            ahead = block_of(parts, jnp.minimum(z + outer - step, outer - 1))
-            behind = block_of(parts, jnp.maximum(z - outer + step, 0))
-            if flows[i] is not None:
-                right, left = lax.optimization_barrier(flows[i])
-                ahead = (ahead.astype(F32) + right.astype(F32)).astype(BF16)
-                behind = (behind.astype(F32) + left.astype(F32)).astype(BF16)
-                ahead, behind = lax.optimization_barrier((ahead, behind))
-            flows[i] = (
-                lax.ppermute(ahead, "seq", to_right),
-                lax.ppermute(behind, "seq", to_left),
-            )
-        if step == 1:
-            *flows[-1], beside, later = lax.optimization_barrier((*flows[-1], beside, later))
-    if outer > 1:
-        totals = [
-            total + right.astype(F32) + left.astype(F32)
-            for total, (right, left) in zip(totals, flows)
-        ]
-    return totals, beside, later
+    )(at.astype(jnp.int32)[None], *flat, rhs)
+
+
+def halving_reduce_scatter(parts, size, inner, pieces):
+    outer = len(parts)
+    parts = list(parts)
+    wide = parts[0].shape[1] // pieces
+    cut = [slice(i * wide, (i + 1) * wide) for i in range(pieces)]
+    before = None
+    bit = 1
+    while bit < outer:
+        for d in reversed(range(bit, outer, 2 * bit)):
+            sent = parts[d]
+            if before is not None and d == bit and 2 * bit < outer:
+                sent, _ = lax.optimization_barrier((sent, before))
+            if 2 * bit < outer:
+                before = moved = swap(sent, "seq", size, bit * inner)
+                parts[d - bit] = parts[d - bit].astype(F32) + moved.astype(F32)
+                if d > bit:
+                    parts[d - bit] = parts[d - bit].astype(BF16)
+            else:
+                parts[0] = [
+                    parts[0][:, c] + swap(sent[:, c], "seq", size, bit * inner).astype(F32)
+                    for c in cut
+                ]
+        bit *= 2
+    return parts[0] if outer > 1 else [parts[0][:, c] for c in cut]
 
 
 def exchange(blocks, groups=None):
@@ -449,15 +450,14 @@
     moved = exchange(packed)
 
     grad_y = jnp.dot(full_grad, out_weight, preferred_element_type=F32).astype(BF16)
-    (gated_grad,) = call(gated_kernel, [blocks], (grad_y, gate))
+    (gated_grad,) = call(gated_kernel, [struct((seq, 1, rows, own), BF16)], (grad_y, gate))
     gated_grad, moved = lax.optimization_barrier((gated_grad, moved))
     grad_c = exchange(gated_grad)
 
-    values_c, kernel_c = moved[:, 0], moved[:, 1]
     spec, conv_out_c = call(
         conv_kernel,
         [spectrum, blocks],
-        (values_c, kernel_c, there, back),
+        (moved, there, back),
         scratch=(mid,),
         flops=work,
     )
@@ -468,54 +468,59 @@
     gates, _ = lax.optimization_barrier((gates, moved))
     order, grads = layer_grads(halves, inner, conv_out_c)
     gates = [swap(gates[bit], "seq", seq, bit) if bit else gates[bit] for bit in order]
-    *gates, conv_out_c = lax.optimization_barrier((*gates, conv_out_c))
     conv_out_c, grad_c = lax.optimization_barrier((conv_out_c, grad_c))
     layers = [[z * inner + w for z in range(outer)] for w in range(inner)]
     conv_out = exchange(conv_out_c.reshape(outer, inner, rows, own), layers)
 
-    conv_grad_c, kernel_grad_c = call(
+    conv_grad, kernel_grad = call(
         grad_kernel,
         [blocks, struct((seq, rows + STEP, own), BF16)],
-        (grad_c, kernel_c, spec, there, back),
+        (grad_c, moved, spec, there, back),
         scratch=(mid,),
         flops=work,
     )
-    flat, _ = lax.optimization_barrier((sum(grads, []), conv_grad_c))
+    flat, gates, _ = lax.optimization_barrier((sum(grads, []), gates, conv_grad))
     count = len(flat) // len(grads)
     grads = [flat[i : i + count] for i in range(0, len(flat), count)]
     bit = inner // 4
     while bit:
         grads = [g + [swap(part, "seq", seq, bit) for part in g] for g in grads]
         bit //= 2
-    conv_grad_c, kernel_grad_c, conv_out = lax.optimization_barrier(
-        (conv_grad_c, kernel_grad_c, conv_out)
-    )
-    conv_grad = exchange(conv_grad_c)
+    conv_grad, conv_out = lax.optimization_barrier((conv_grad, conv_out))
+    conv_grad = exchange(conv_grad)
 
     block = struct((rows, width), BF16)
     home = struct((outer, rows, own), BF16)
-    chunks = 2 if outer % 2 == 0 else 1
-    wide = outer * own // chunks
-    parts = call(
+    gated_out, *homes = call(
         functools.partial(layer_kernel, order=order),
-        [struct((inner * rows, wide), BF16)] * chunks + [home] * inner,
+        [struct((inner * rows, outer * own), BF16)] + [home] * inner,
         (*gates, conv_out, place),
         scalar=(inner + 1,),
     )
-    homes = parts[chunks:]
-    terms = [outer_product(grads, part).reshape(outer, -1, wide) for part in parts[:chunks]]
     shift = 0
     if len(grads) == 2:
         shift = lax.axis_index("tp") * (outer // 2)
+    terms = [None] * outer
+    for d in sorted(range(outer), key=lambda d: (-(d % 2), -d)):
+        terms[d] = outer_product(grads, gated_out, (me // inner) ^ d ^ shift, outer)
+        gated_out, _ = lax.optimization_barrier((gated_out, terms[d]))
+    kernel_grad, conv_grad, _ = lax.optimization_barrier((kernel_grad, conv_grad, terms[1 % outer]))
+    kernel_grad = exchange(kernel_grad)
+    (d_values,) = call(values_kernel, [block], (conv_grad,))
 
     homes = {bit: swap(part, "seq", seq, bit) if bit else part for bit, part in zip(order, homes)}
     homes = jnp.stack([homes[bit] for bit in range(inner)])
     (d_gate,) = call(gate_kernel, [block], (homes, grad_y, place), scalar=(2,))
-    totals, conv_grad, kernel_grad_c = line_reduce_scatter(
-        terms, seq, inner, shift, conv_grad, kernel_grad_c
-    )
-    kernel_grad = exchange(kernel_grad_c)
-    (d_values,) = call(values_kernel, [block], (conv_grad,))
+    d_filt, decay_grad = call(
+        functools.partial(filt_kernel, length=length),
+        [struct((rows, width), F32), struct((1, width), F32)],
+        (kernel_grad, rates, start),
+        scalar=(2,),
+    )
+    chunks = 2 if outer % 2 == 0 else 1
+    wide = outer * own // chunks
+    totals = halving_reduce_scatter(terms, seq, inner, chunks)
+    totals[-1], d_gate, d_values = lax.optimization_barrier((totals[-1], d_gate, d_values))
     pieces = []
     for total in totals:
         total = total.astype(BF16).reshape(inner, -1, wide)
@@ -529,12 +534,6 @@
         (pieces, place),
         scalar=(1,),
     )
-    d_filt, decay_grad = call(
-        functools.partial(filt_kernel, length=length),
-        [struct((rows, width), F32), struct((1, width), F32)],
-        (kernel_grad, rates, start),
-        scalar=(2,),
-    )
     return (d_values, d_gate, d_filt, decay_grad[0], d_out_weight)
 
 

time: 271 us -> 253 us (0.934)
  starting transfers between devices: 84.9 us -> 51.3 us
  waiting for transfers between devices: 81.3 us -> 108 us
  local copies, waits for them, and re-layouts: 23.8 us -> 14.1 us
  other arithmetic: 12.1 us -> 7.28 us
  Pallas kernels: 57.9 us -> 61.3 us
    ppermute x19 -> x23, waiting for transfers between devices: 45.1 us -> 99.9 us  [swap(): return lax.ppermute(array, axis, [(i, i ^ bit) for i in range(size)])]
    ppermute x12 -> x0, starting transfers between devices: 40.4 us -> none  [the longest x6 32.8 us: line_reduce_scatter(): lax.ppermute(ahead, 'seq', to_right)]
    ppermute x12 -> x0, waiting for transfers between devices: 25.6 us -> none  [the longest x6 16.7 us: line_reduce_scatter(): lax.ppermute(ahead, 'seq', to_right)]
    squeeze x3 -> x0, local copies, waits for them, and re-layouts: 6.58 us -> none  [the longest x2 3.49 us: block_of(): return lax.dynamic_index_in_dim(parts, at ^ shift, 0, keepdims=False)]
    convert_element_type x3 -> x1, other arithmetic: 7.82 us -> 1.51 us  [halving_reduce_scatter(): parts[d - bit] = parts[d - bit].astype(BF16)]
    unnamed x61 -> x53, local copies, waits for them, and re-layouts: 17.1 us -> 10.9 us
    all_to_all x5, starting transfers between devices: 32.1 us -> 35.6 us  [exchange(): lax.all_to_all(blocks, 'seq', split_axis=0, concat_axis=0, tiled=True, ax...]
    ppermute x19 -> x23, starting transfers between devices: 12.5 us -> 15.7 us  [swap(): return lax.ppermute(array, axis, [(i, i ^ bit) for i in range(size)])]
  transfers between devices with their start and end apart: 36 -> 28, of which waited for: 12 -> 10; matrix products, arithmetic and copies ran while one was open for 9% -> 8% of each run, Pallas kernels for 20% -> 21%
where the time goes in v2:
time: 253 us; the launch traced here: 252 us
  waiting for transfers between devices  108 us (43%)
  Pallas kernels  61.3 us (24%)
  starting transfers between devices  51.3 us (20%)
  local copies, waits for them, and re-layouts  14.1 us (6%)
  matrix products  8.37 us (3%)
  other arithmetic  7.28 us (3%)
    ppermute x23, waiting for transfers between devices, swap(): return lax.ppermute(array, axis, [(i, i ^ bit) for i in range(size)])  99.9 us
    pallas_call x12, Pallas kernels, call(): pl.pallas_call(kernel, out_shape=outs, in_specs=specs, out_specs=[whole]...  45.9 us
    all_to_all x5, starting transfers between devices, exchange(): lax.all_to_all(blocks, 'seq', split_axis=0, concat_axis=0, tiled=True, ax...  35.6 us
    ppermute x23, starting transfers between devices, swap(): return lax.ppermute(array, axis, [(i, i ^ bit) for i in range(size)])  15.7 us
    pallas_call x4, Pallas kernels, outer_product(): pl.pallas_call(functools.partial(outer_kernel, groups=len(groups), tiles=...  15.3 us
    unnamed x53, local copies, waits for them, and re-layouts  10.9 us
    all_to_all x5, waiting for transfers between devices, exchange(): lax.all_to_all(blocks, 'seq', split_axis=0, concat_axis=0, tiled=True, ax...  8.43 us
    dot_general x1, matrix products, on_device(): jnp.dot(full_grad, out_weight, preferred_element_type=F32).astype(BF16)  8.37 us
  transfers between devices with their start and end apart: 28, of which 10 were waited for; matrix products, arithmetic and copies ran while one was open for 8% of the time, Pallas kernels for 21%

profile of v2, /device:TPU:0, one launch (start us, length us, event | category | flops | bytes accessed | tf_op | source)
XLA Modules:
  0.0 251.8 jit_solution(15156623181376371615)
XLA Ops:
  6.0 7.4 %all-to-all-start = ((bf16[16,2,256,128]{3,2,1,0:T(8,128)(2,1)}), bf16[16,2,256,128]{3,2,1,0:T(8,128)(2,1)}, u32[]{:S(2)}, u32[]{:S(2)}) async-start(bf16[16,2,256,128]{3,2,1,0:T(8,128)(2,1)} %shard_map.122), calls=%async_computation | async-start | bytes 4194304 | tf_op jit(solution)/shard_map/all_to_all | solution.py:420
  16.6 1.9 collective-permute-start
  18.7 20.5 %collective-permute-done.1.x_ref = bf16[256,2048]{1,0:T(8,128)(2,1)} collective-permute-done((bf16[256,2048]{1,0:T(8,128)(2,1)}, bf16[256,2048]{1,0:T(8,128)(2,1)}, u32[]{:S(2)}, u32[]{:S(2)}) %collective-permute-start.1) | collective-permute-done | bytes 1048608 | tf_op jit(solution)/shard_map/ppermute | solution.py:305
  40.9 8.4 %convolution_convert_fusion.grad_ref = bf16[256,2048]{1,0:T(8,128)(2,1)S(1)} fusion(bf16[4096,2048]{1,0:T(8,128)(2,1)} %param.11, bf16[256,2048]{1,0:T(8,128)(2,1)S(1)} %get-tuple-element.78, bf16[256,2048]{1,0:T(8,128)(2,1)S(1)} %get-tuple-element.77), kind=kOutput, calls=%fused_computation | convolution fusion | flops 4299685888 | bytes 19922944 | tf_op jit(solution)/shard_map/dot_general | solution.py:452
  54.7 11.2 %all-to-all-start.1 = ((bf16[16,1,256,128]{3,2,1,0:T(8,128)(2,1)}), bf16[16,1,256,128]{3,2,1,0:T(8,128)(2,1)}, u32[]{:S(2)}, u32[]{:S(2)}) async-start(bf16[16,1,256,128]{3,2,1,0:T(8,128)(2,1)} %copy-done.5), calls=%async_computation.1 | async-start | bytes 2097152 | tf_op jit(solution)/shard_map/all_to_all | solution.py:420
  66.0 2.1 slice_bitcast_fusion
  70.2 16.3 %shard_map.123 = (f32[33,256,256]{2,1,0:T(8,128)}, bf16[16,256,128]{2,1,0:T(8,128)(2,1)S(1)}) custom-call(bf16[16,2,256,128]{3,2,1,0:T(8,128)(2,1)} %all-to-all-done.fields_ref, bf16[33,256,256]{2,1,0:T(8,128)(2,1)} %constant.84.clone.there_ref, bf16[33,256,256]{2,1,0:T(8,128)(2,1)} %constant.85.clone.back_ref), custom_call_target="tpu_custom_call" | custom-call | flops 20761804800 | bytes 20447232 | tf_op jit(solution)/shard_map/pallas_call | solution.py:289
  89.0 6.3 %all-to-all-start.2 = ((bf16[4,4,256,128]{3,2,1,0:T(8,128)(2,1)}), bf16[4,4,256,128]{3,2,1,0:T(8,128)(2,1)}, u32[]{:S(2)}, u32[]{:S(2)}) async-start(bf16[4,4,256,128]{3,2,1,0:T(8,128)(2,1)} %bitcast.50), calls=%async_computation.2 | async-start | bytes 2097152 | tf_op jit(solution)/shard_map/all_to_all | solution.py:420
  95.3 16.3 %shard_map.125 = (bf16[16,256,128]{2,1,0:T(8,128)(2,1)S(1)}, bf16[16,272,128]{2,1,0:T(8,128)(2,1)S(1)}) custom-call(bf16[16,1,256,128]{3,2,1,0:T(8,128)(2,1)} %all-to-all-done.1.g_ref, bf16[16,2,256,128]{3,2,1,0:T(8,128)(2,1)} %all-to-all-done.fields_ref, f32[33,256,256]{2,1,0:T(8,128)} %get-tuple-element.47.spec_ref, ...), custom_call_target="tpu_custom_call" | custom-call | flops 20761804800 | bytes 22609920 | tf_op jit(solution)/shard_map/pallas_call | solution.py:289
  114.7 6.8 %all-to-all-done.2.refs_4_ = bf16[4,4,256,128]{3,2,1,0:T(8,128)(2,1)} async-done(((bf16[4,4,256,128]{3,2,1,0:T(8,128)(2,1)}), bf16[4,4,256,128]{3,2,1,0:T(8,128)(2,1)}, u32[]{:S(2)}, u32[]{:S(2)}) %all-to-all-start.2) | async-done | bytes 1048608 | tf_op jit(solution)/shard_map/all_to_all | solution.py:420
  121.5 1.9 shard_map.126
  125.8 4.3 %shard_map.127 = bf16[1024,512]{1,0:T(8,128)(2,1)} custom-call(s32[1]{0:T(128)} %bitcast.9.at_ref, bf16[2048,256]{1,0:T(8,128)(2,1)S(1)} %shard_map.119.refs_0_, bf16[2048,256]{1,0:T(8,128)(2,1)S(1)} %collective-permute-done.refs_1_, bf16[2048,256]{1,0:T(8,128)(2,1)} %collective-permute-done.6.refs_2_, bf16[2048,256]{1,0:T(8,128)(2,1)} %collective-permute-done.7.refs_3_, ...), custom_call_target="tpu_custom_call" | custom-call | flops 2147483648 | bytes 3145728 | tf_op jit(solution)/shard_map/pallas_call | solution.py:374
  130.2 4.8 %all-to-all-start.3 = ((bf16[16,256,128]{2,1,0:T(8,128)(2,1)}), bf16[16,256,128]{2,1,0:T(8,128)(2,1)S(1)}, u32[]{:S(2)}, u32[]{:S(2)}) async-start(bf16[16,256,128]{2,1,0:T(8,128)(2,1)} %copy-done.11), calls=%async_computation.3 | async-start | bytes 2097152 | tf_op jit(solution)/shard_map/all_to_all | solution.py:420
  135.1 4.2 %shard_map.128 = bf16[1024,512]{1,0:T(8,128)(2,1)} custom-call(s32[1]{0:T(128)} %bitcast.10.at_ref, bf16[2048,256]{1,0:T(8,128)(2,1)S(1)} %shard_map.119.refs_0_, bf16[2048,256]{1,0:T(8,128)(2,1)S(1)} %collective-permute-done.refs_1_, bf16[2048,256]{1,0:T(8,128)(2,1)} %collective-permute-done.6.refs_2_, bf16[2048,256]{1,0:T(8,128)(2,1)} %collective-permute-done.7.refs_3_, ...), custom_call_target="tpu_custom_call" | custom-call | flops 2147483648 | bytes 3145728 | tf_op jit(solution)/shard_map/pallas_call | solution.py:374
  139.2 28.6 %collective-permute-done.10 = bf16[1024,512]{1,0:T(8,128)(2,1)} collective-permute-done((bf16[1024,512]{1,0:T(8,128)(2,1)}, bf16[1024,512]{1,0:T(8,128)(2,1)}, u32[]{:S(2)}, u32[]{:S(2)}) %collective-permute-start.10) | collective-permute-done | bytes 1048608 | tf_op jit(solution)/shard_map/ppermute | solution.py:305
  167.8 3.5 %shard_map.129 = bf16[1024,512]{1,0:T(8,128)(2,1)S(1)} custom-call(s32[1]{0:T(128)} %bitcast.11.at_ref, bf16[2048,256]{1,0:T(8,128)(2,1)S(1)} %shard_map.119.refs_0_, bf16[2048,256]{1,0:T(8,128)(2,1)S(1)} %collective-permute-done.refs_1_, bf16[2048,256]{1,0:T(8,128)(2,1)} %collective-permute-done.6.refs_2_, ...), custom_call_target="tpu_custom_call" | custom-call | flops 2147483648 | bytes 3145728 | tf_op jit(solution)/shard_map/pallas_call | solution.py:374
  175.8 3.4 %shard_map.130 = bf16[1024,512]{1,0:T(8,128)(2,1)S(1)} custom-call(s32[1]{0:T(128)} %bitcast.at_ref, bf16[2048,256]{1,0:T(8,128)(2,1)S(1)} %shard_map.119.refs_0_, bf16[2048,256]{1,0:T(8,128)(2,1)S(1)} %collective-permute-done.refs_1_, bf16[2048,256]{1,0:T(8,128)(2,1)} %collective-permute-done.6.refs_2_, bf16[2048,256]{1,0:T(8,128)(2,1)} %collective-permute-done.7.refs_3_, ...), custom_call_target="tpu_custom_call" | custom-call | flops 2147483648 | bytes 3145728 | tf_op jit(solution)/shard_map/pallas_call | solution.py:374
  180.5 4.7 %collective-permute-done.15 = bf16[4,256,128]{2,1,0:T(8,128)(2,1)S(1)} collective-permute-done((bf16[4,256,128]{2,1,0:T(8,128)(2,1)S(1)}, bf16[4,256,128]{2,1,0:T(8,128)(2,1)S(1)}, u32[]{:S(2)}, u32[]{:S(2)}) %collective-permute-start.15) | collective-permute-done | bytes 262176 | tf_op jit(solution)/shard_map/ppermute | solution.py:305
  188.0 5.9 %all-to-all-start.4 = ((bf16[16,272,128]{2,1,0:T(8,128)(2,1)}), bf16[16,272,128]{2,1,0:T(8,128)(2,1)S(1)}, u32[]{:S(2)}, u32[]{:S(2)}) async-start(bf16[16,272,128]{2,1,0:T(8,128)(2,1)} %copy-done.10), calls=%async_computation.4 | async-start | bytes 2228224 | tf_op jit(solution)/shard_map/all_to_all | solution.py:420
  193.9 16.2 %collective-permute-done.11 = bf16[1024,512]{1,0:T(8,128)(2,1)} collective-permute-done((bf16[1024,512]{1,0:T(8,128)(2,1)}, bf16[1024,512]{1,0:T(8,128)(2,1)}, u32[]{:S(2)}, u32[]{:S(2)}) %collective-permute-start.11) | collective-permute-done | bytes 1048608 | tf_op jit(solution)/shard_map/ppermute | solution.py:305
  213.0 3.4 %collective-permute-start.18 = (bf16[256,256]{1,0:T(8,128)(2,1)S(1)}, bf16[256,256]{1,0:T(8,128)(2,1)S(1)}, u32[]{:S(2)}, u32[]{:S(2)}) collective-permute-start(bf16[256,256]{1,0:T(8,128)(2,1)S(1)} %get-tuple-element.90), channel_id=1, source_target_pairs={{0,4},{2,6},{4,0},{6,2},{8,12},{10,14},{12,8},{14,10},{16,20},{18,... | collective-permute-start | bytes 393224 | tf_op jit(solution)/shard_map/ppermute | solution.py:305
  216.5 20.6 %collective-permute-done.12 = bf16[1024,256]{1,0:T(8,128)(2,1)} collective-permute-done((bf16[1024,256]{1,0:T(8,128)(2,1)}, bf16[1024,256]{1,0:T(8,128)(2,1)}, u32[]{:S(2)}, u32[]{:S(2)}) %collective-permute-start.12) | collective-permute-done | bytes 524320 | tf_op jit(solution)/shard_map/ppermute | solution.py:305
  240.5 5.9 %collective-permute-done.21 = bf16[256,256]{1,0:T(8,128)(2,1)S(1)} collective-permute-done((bf16[256,256]{1,0:T(8,128)(2,1)S(1)}, bf16[256,256]{1,0:T(8,128)(2,1)S(1)}, u32[]{:S(2)}, u32[]{:S(2)}) %collective-permute-start.21) | collective-permute-done | bytes 131104 | tf_op jit(solution)/shard_map/ppermute | solution.py:305
  246.4 2.1 collective-permute-done.22
  (113 shorter events, 44.0 us)
Async XLA Ops:
  6.0 48.8 %all-to-all-start = ((bf16[16,2,256,128]{3,2,1,0:T(8,128)(2,1)}), bf16[16,2,256,128]{3,2,1,0:T(8,128)(2,1)}, u32[]{:S(2)}, u32[]{:S(2)}) async-start(bf16[16,2,256,128]{3,2,1,0:T(8,128)(2,1)} %shard_map.122), calls=%async_computation | async-start | bytes 4194304 | tf_op jit(solution)/shard_map/all_to_all | solution.py:420
  13.4 25.8 %collective-permute-start.1 = (bf16[256,2048]{1,0:T(8,128)(2,1)}, bf16[256,2048]{1,0:T(8,128)(2,1)}, u32[]{:S(2)}, u32[]{:S(2)}) collective-permute-start(bf16[256,2048]{1,0:T(8,128)(2,1)} %x_ref.1), channel_id=1, source_target_pairs={{0,1},{1,0},{2,3},{3,2},{4,5},{5,4},{6,7},{7,6},{8,9},{9,8},{10,11... | collective-permute-start | bytes 3145736 | tf_op jit(solution)/shard_map/ppermute | solution.py:305
  16.6 70.9 %collective-permute-start = (bf16[2048,256]{1,0:T(8,128)(2,1)S(1)}, bf16[2048,256]{1,0:T(8,128)(2,1)S(1)}, u32[]{:S(2)}, u32[]{:S(2)}) collective-permute-start(bf16[2048,256]{1,0:T(8,128)(2,1)S(1)} %shard_map.119.refs_0_), channel_id=1, source_target_pairs={{0,4},{2,6},{4,0},{6,2},{8,12},{10,14},{12,8},{14,10},{16,20},{18,... | collective-permute-start | bytes 3145736 | tf_op jit(solution)/shard_map/ppermute | solution.py:305
  54.7 34.3 %all-to-all-start.1 = ((bf16[16,1,256,128]{3,2,1,0:T(8,128)(2,1)}), bf16[16,1,256,128]{3,2,1,0:T(8,128)(2,1)}, u32[]{:S(2)}, u32[]{:S(2)}) async-start(bf16[16,1,256,128]{3,2,1,0:T(8,128)(2,1)} %copy-done.5), calls=%async_computation.1 | async-start | bytes 2097152 | tf_op jit(solution)/shard_map/all_to_all | solution.py:420
  68.1 45.5 %collective-permute-start.3 = (bf16[4,256,128]{2,1,0:T(8,128)(2,1)}, bf16[4,256,128]{2,1,0:T(8,128)(2,1)}, u32[]{:S(2)}, u32[]{:S(2)}) collective-permute-start(bf16[4,256,128]{2,1,0:T(8,128)(2,1)} %get-tuple-element.83), channel_id=1, source_target_pairs={{0,4},{2,6},{4,0},{6,2},{8,12},{10,14},{12,8},{14,10},{16,20},{18,... | collective-permute-start | bytes 786440 | tf_op jit(solution)/shard_map/ppermute | solution.py:305
  69.9 43.6 %collective-permute-start.4 = (bf16[4,256,128]{2,1,0:T(8,128)(2,1)}, bf16[4,256,128]{2,1,0:T(8,128)(2,1)}, u32[]{:S(2)}, u32[]{:S(2)}) collective-permute-start(bf16[4,256,128]{2,1,0:T(8,128)(2,1)} %get-tuple-element.82), channel_id=1, source_target_pairs={{0,2},{2,0},{4,6},{6,4},{8,10},{10,8},{12,14},{14,12},{16,18},{18,... | collective-permute-start | bytes 786440 | tf_op jit(solution)/shard_map/ppermute | solution.py:305
  69.9 43.6 %collective-permute-start.5 = (bf16[4,256,128]{2,1,0:T(8,128)(2,1)}, bf16[4,256,128]{2,1,0:T(8,128)(2,1)}, u32[]{:S(2)}, u32[]{:S(2)}) collective-permute-start(bf16[4,256,128]{2,1,0:T(8,128)(2,1)} %get-tuple-element.81), channel_id=1, source_target_pairs={{0,6},{2,4},{4,2},{6,0},{8,14},{10,12},{12,10},{14,8},{16,22},{18,... | collective-permute-start | bytes 786440 | tf_op jit(solution)/shard_map/ppermute | solution.py:305
  87.5 26.1 %collective-permute-start.2 = (bf16[2048,256]{1,0:T(8,128)(2,1)S(1)}, bf16[2048,256]{1,0:T(8,128)(2,1)}, u32[]{:S(2)}, u32[]{:S(2)}) collective-permute-start(bf16[2048,256]{1,0:T(8,128)(2,1)S(1)} %collective-permute-done.refs_1_), channel_id=1, source_target_pairs={{0,1},{1,0},{2,3},{3,2},{4,5},{5,4},{6,7},{7,6},{8,9},{9,8},{10,11... | collective-permute-start | bytes 3145736 | tf_op jit(solution)/shard_map/ppermute | solution.py:305
  89.0 32.5 %all-to-all-start.2 = ((bf16[4,4,256,128]{3,2,1,0:T(8,128)(2,1)}), bf16[4,4,256,128]{3,2,1,0:T(8,128)(2,1)}, u32[]{:S(2)}, u32[]{:S(2)}) async-start(bf16[4,4,256,128]{3,2,1,0:T(8,128)(2,1)} %bitcast.50), calls=%async_computation.2 | async-start | bytes 2097152 | tf_op jit(solution)/shard_map/all_to_all | solution.py:420
  113.6 12.2 %collective-permute-start.6 = (bf16[2048,256]{1,0:T(8,128)(2,1)S(1)}, bf16[2048,256]{1,0:T(8,128)(2,1)}, u32[]{:S(2)}, u32[]{:S(2)}) collective-permute-start(bf16[2048,256]{1,0:T(8,128)(2,1)S(1)} %shard_map.119.refs_0_), channel_id=1, source_target_pairs={{0,2},{2,0},{4,6},{6,4},{8,10},{10,8},{12,14},{14,12},{16,18},{18,... | collective-permute-start | bytes 3145736 | tf_op jit(solution)/shard_map/ppermute | solution.py:305
  113.7 12.1 %collective-permute-start.7 = (bf16[2048,256]{1,0:T(8,128)(2,1)S(1)}, bf16[2048,256]{1,0:T(8,128)(2,1)}, u32[]{:S(2)}, u32[]{:S(2)}) collective-permute-start(bf16[2048,256]{1,0:T(8,128)(2,1)S(1)} %collective-permute-done.refs_1_), channel_id=1, source_target_pairs={{0,2},{2,0},{4,6},{6,4},{8,10},{10,8},{12,14},{14,12},{16,18},{18,... | collective-permute-start | bytes 3145736 | tf_op jit(solution)/shard_map/ppermute | solution.py:305
  114.2 11.6 %collective-permute-start.8 = (bf16[2048,256]{1,0:T(8,128)(2,1)S(1)}, bf16[2048,256]{1,0:T(8,128)(2,1)}, u32[]{:S(2)}, u32[]{:S(2)}) collective-permute-start(bf16[2048,256]{1,0:T(8,128)(2,1)S(1)} %shard_map.120.refs_4_), channel_id=1, source_target_pairs={{0,2},{2,0},{4,6},{6,4},{8,10},{10,8},{12,14},{14,12},{16,18},{18,... | collective-permute-start | bytes 3145736 | tf_op jit(solution)/shard_map/ppermute | solution.py:305
  114.2 11.6 %collective-permute-start.9 = (bf16[2048,256]{1,0:T(8,128)(2,1)}, bf16[2048,256]{1,0:T(8,128)(2,1)}, u32[]{:S(2)}, u32[]{:S(2)}) collective-permute-start(bf16[2048,256]{1,0:T(8,128)(2,1)} %collective-permute-done.2.refs_5_), channel_id=1, source_target_pairs={{0,2},{2,0},{4,6},{6,4},{8,10},{10,8},{12,14},{14,12},{16,18},{18,... | collective-permute-start | bytes 3145736 | tf_op jit(solution)/shard_map/ppermute | solution.py:305
  130.1 37.7 %collective-permute-start.10 = (bf16[1024,512]{1,0:T(8,128)(2,1)}, bf16[1024,512]{1,0:T(8,128)(2,1)}, u32[]{:S(2)}, u32[]{:S(2)}) collective-permute-start(bf16[1024,512]{1,0:T(8,128)(2,1)} %shard_map.127), channel_id=1, source_target_pairs={{0,8},{2,10},{4,12},{6,14},{8,0},{10,2},{12,4},{14,6},{16,24},{18,... | collective-permute-start | bytes 3145736 | tf_op jit(solution)/shard_map/ppermute | solution.py:305
  130.2 56.5 %all-to-all-start.3 = ((bf16[16,256,128]{2,1,0:T(8,128)(2,1)}), bf16[16,256,128]{2,1,0:T(8,128)(2,1)S(1)}, u32[]{:S(2)}, u32[]{:S(2)}) async-start(bf16[16,256,128]{2,1,0:T(8,128)(2,1)} %copy-done.11), calls=%async_computation.3 | async-start | bytes 2097152 | tf_op jit(solution)/shard_map/all_to_all | solution.py:420
  167.8 42.3 %collective-permute-start.11 = (bf16[1024,512]{1,0:T(8,128)(2,1)}, bf16[1024,512]{1,0:T(8,128)(2,1)}, u32[]{:S(2)}, u32[]{:S(2)}) collective-permute-start(bf16[1024,512]{1,0:T(8,128)(2,1)} %shard_map.128), channel_id=1, source_target_pairs={{0,8},{2,10},{4,12},{6,14},{8,0},{10,2},{12,4},{14,6},{16,24},{18,... | collective-permute-start | bytes 3145736 | tf_op jit(solution)/shard_map/ppermute | solution.py:305
  171.5 13.8 %collective-permute-start.15 = (bf16[4,256,128]{2,1,0:T(8,128)(2,1)S(1)}, bf16[4,256,128]{2,1,0:T(8,128)(2,1)S(1)}, u32[]{:S(2)}, u32[]{:S(2)}) collective-permute-start(bf16[4,256,128]{2,1,0:T(8,128)(2,1)S(1)} %copy-done.19), channel_id=1, source_target_pairs={{0,6},{2,4},{4,2},{6,0},{8,14},{10,12},{12,10},{14,8},{16,22},{18,... | collective-permute-start | bytes 786440 | tf_op jit(solution)/shard_map/ppermute | solution.py:305
  175.8 35.8 %collective-permute-start.16 = (bf16[1024,256]{1,0:T(8,128)(2,1)}, bf16[1024,256]{1,0:T(8,128)(2,1)}, u32[]{:S(2)}, u32[]{:S(2)}) collective-permute-start(bf16[1024,256]{1,0:T(8,128)(2,1)} %get-tuple-element.79), channel_id=1, source_target_pairs={{0,16},{2,18},{4,20},{6,22},{8,24},{10,26},{12,28},{14,30},{16,0},... | collective-permute-start | bytes 1572872 | tf_op jit(solution)/shard_map/ppermute | solution.py:305
  186.7 50.4 %collective-permute-start.12 = (bf16[1024,256]{1,0:T(8,128)(2,1)}, bf16[1024,256]{1,0:T(8,128)(2,1)}, u32[]{:S(2)}, u32[]{:S(2)}) collective-permute-start(bf16[1024,256]{1,0:T(8,128)(2,1)} %get-tuple-element.80), channel_id=1, source_target_pairs={{0,16},{2,18},{4,20},{6,22},{8,24},{10,26},{12,28},{14,30},{16,0},... | collective-permute-start | bytes 1572872 | tf_op jit(solution)/shard_map/ppermute | solution.py:305
  188.0 62.1 %all-to-all-start.4 = ((bf16[16,272,128]{2,1,0:T(8,128)(2,1)}), bf16[16,272,128]{2,1,0:T(8,128)(2,1)S(1)}, u32[]{:S(2)}, u32[]{:S(2)}) async-start(bf16[16,272,128]{2,1,0:T(8,128)(2,1)} %copy-done.10), calls=%async_computation.4 | async-start | bytes 2228224 | tf_op jit(solution)/shard_map/all_to_all | solution.py:420
  212.9 25.4 %collective-permute-start.17 = (bf16[256,256]{1,0:T(8,128)(2,1)S(1)}, bf16[256,256]{1,0:T(8,128)(2,1)S(1)}, u32[]{:S(2)}, u32[]{:S(2)}) collective-permute-start(bf16[256,256]{1,0:T(8,128)(2,1)S(1)} %get-tuple-element.91), channel_id=1, source_target_pairs={{0,2},{2,0},{4,6},{6,4},{8,10},{10,8},{12,14},{14,12},{16,18},{18,... | collective-permute-start | bytes 393224 | tf_op jit(solution)/shard_map/ppermute | solution.py:305
  213.0 25.4 %collective-permute-start.18 = (bf16[256,256]{1,0:T(8,128)(2,1)S(1)}, bf16[256,256]{1,0:T(8,128)(2,1)S(1)}, u32[]{:S(2)}, u32[]{:S(2)}) collective-permute-start(bf16[256,256]{1,0:T(8,128)(2,1)S(1)} %get-tuple-element.90), channel_id=1, source_target_pairs={{0,4},{2,6},{4,0},{6,2},{8,12},{10,14},{12,8},{14,10},{16,20},{18,... | collective-permute-start | bytes 393224 | tf_op jit(solution)/shard_map/ppermute | solution.py:305
  216.4 22.0 %collective-permute-start.19 = (bf16[256,256]{1,0:T(8,128)(2,1)S(1)}, bf16[256,256]{1,0:T(8,128)(2,1)S(1)}, u32[]{:S(2)}, u32[]{:S(2)}) collective-permute-start(bf16[256,256]{1,0:T(8,128)(2,1)S(1)} %get-tuple-element.89), channel_id=1, source_target_pairs={{0,6},{2,4},{4,2},{6,0},{8,14},{10,12},{12,10},{14,8},{16,22},{18,... | collective-permute-start | bytes 393224 | tf_op jit(solution)/shard_map/ppermute | solution.py:305
  239.1 9.4 %collective-permute-start.22 = (bf16[256,256]{1,0:T(8,128)(2,1)S(1)}, bf16[256,256]{1,0:T(8,128)(2,1)S(1)}, u32[]{:S(2)}, u32[]{:S(2)}) collective-permute-start(bf16[256,256]{1,0:T(8,128)(2,1)S(1)} %get-tuple-element.85), channel_id=1, source_target_pairs={{0,6},{2,4},{4,2},{6,0},{8,14},{10,12},{12,10},{14,8},{16,22},{18,... | collective-permute-start | bytes 393224 | tf_op jit(solution)/shard_map/ppermute | solution.py:305
  (28 other events, 202.0 us)

commit v3 on v2

--- a/solution.py
+++ b/solution.py
@@ -321,21 +321,17 @@
     return call(transpose_kernel, [struct(part.shape[::-1], BF16)], (part,))[0]
 
 
-def layer_grads(halves, inner, after):
+def layer_grads(halves, inner):
     order = [0]
     bit = inner // 2
     while bit:
         order = order + [i ^ bit for i in order]
         bit //= 2
     turned = [turn(part) for part in halves]
-    if inner == 1:
-        return order, [[part] for part in turned]
-    seq = lax.axis_size("seq")
-    across = [swap(turned[0], "seq", seq, inner // 2)]
-    if len(turned) == 2:
-        late, _ = lax.optimization_barrier((across[0], after))
-        across.append(swap(late, "tp", 2, 1))
-    return order, [list(pair) for pair in zip(turned, across)]
+    across = []
+    if inner > 1:
+        across = [swap(turned[0], "seq", lax.axis_size("seq"), inner // 2)]
+    return order, turned, across
 
 
 def outer_kernel(at_ref, *refs, groups, tiles):
@@ -390,7 +386,7 @@
     )(at.astype(jnp.int32)[None], *flat, rhs)
 
 
-def halving_reduce_scatter(parts, size, inner, pieces):
+def halving_reduce_scatter(parts, size, inner, pieces, beside, late):
     outer = len(parts)
     parts = list(parts)
     wide = parts[0].shape[1] // pieces
@@ -403,7 +399,12 @@
             if before is not None and d == bit and 2 * bit < outer:
                 sent, _ = lax.optimization_barrier((sent, before))
             if 2 * bit < outer:
-                before = moved = swap(sent, "seq", size, bit * inner)
+                moved = swap(sent, "seq", size, bit * inner)
+                if before is None:
+                    moved, beside = lax.optimization_barrier((moved, beside))
+                elif d == 1:
+                    moved, late = lax.optimization_barrier((moved, late))
+                before = moved
                 parts[d - bit] = parts[d - bit].astype(F32) + moved.astype(F32)
                 if d > bit:
                     parts[d - bit] = parts[d - bit].astype(BF16)
@@ -413,7 +414,9 @@
                     for c in cut
                 ]
         bit *= 2
-    return parts[0] if outer > 1 else [parts[0][:, c] for c in cut]
+    if outer == 1:
+        parts[0] = [parts[0][:, c] for c in cut]
+    return parts[0], beside, late
 
 
 def exchange(blocks, groups=None):
@@ -454,6 +457,14 @@
     gated_grad, moved = lax.optimization_barrier((gated_grad, moved))
     grad_c = exchange(gated_grad)
 
+    place = (me % inner).astype(jnp.int32)[None]
+    (gates,) = call(
+        layer_pack_kernel, [struct((inner, outer, rows, own), BF16)], (gate, place), scalar=(1,)
+    )
+    gates, _ = lax.optimization_barrier((gates, moved))
+    order, turned, across = layer_grads(halves, inner)
+    if across:
+        across[0], *turned, moved = lax.optimization_barrier((across[0], *turned, moved))
     spec, conv_out_c = call(
         conv_kernel,
         [spectrum, blocks],
@@ -461,17 +472,16 @@
         scratch=(mid,),
         flops=work,
     )
-    place = (me % inner).astype(jnp.int32)[None]
-    (gates,) = call(
-        layer_pack_kernel, [struct((inner, outer, rows, own), BF16)], (gate, place), scalar=(1,)
-    )
-    gates, _ = lax.optimization_barrier((gates, moved))
-    order, grads = layer_grads(halves, inner, conv_out_c)
+    if len(turned) == 2 and across:
+        late, _ = lax.optimization_barrier((across[0], conv_out_c))
+        across.append(swap(late, "tp", 2, 1))
+    grads = [list(pair) for pair in (zip(turned, across) if across else zip(turned))]
     gates = [swap(gates[bit], "seq", seq, bit) if bit else gates[bit] for bit in order]
     conv_out_c, grad_c = lax.optimization_barrier((conv_out_c, grad_c))
     layers = [[z * inner + w for z in range(outer)] for w in range(inner)]
     conv_out = exchange(conv_out_c.reshape(outer, inner, rows, own), layers)
 
+    *gates, grad_c = lax.optimization_barrier((*gates, grad_c))
     conv_grad, kernel_grad = call(
         grad_kernel,
         [blocks, struct((seq, rows + STEP, own), BF16)],
@@ -506,20 +516,22 @@
         gated_out, _ = lax.optimization_barrier((gated_out, terms[d]))
     kernel_grad, conv_grad, _ = lax.optimization_barrier((kernel_grad, conv_grad, terms[1 % outer]))
     kernel_grad = exchange(kernel_grad)
-    (d_values,) = call(values_kernel, [block], (conv_grad,))
 
     homes = {bit: swap(part, "seq", seq, bit) if bit else part for bit, part in zip(order, homes)}
     homes = jnp.stack([homes[bit] for bit in range(inner)])
     (d_gate,) = call(gate_kernel, [block], (homes, grad_y, place), scalar=(2,))
+    chunks = 1
+    wide = outer * own // chunks
+    totals, conv_grad, kernel_grad = halving_reduce_scatter(
+        terms, seq, inner, chunks, conv_grad, kernel_grad
+    )
+    (d_values,) = call(values_kernel, [block], (conv_grad,))
     d_filt, decay_grad = call(
         functools.partial(filt_kernel, length=length),
         [struct((rows, width), F32), struct((1, width), F32)],
         (kernel_grad, rates, start),
         scalar=(2,),
     )
-    chunks = 2 if outer % 2 == 0 else 1
-    wide = outer * own // chunks
-    totals = halving_reduce_scatter(terms, seq, inner, chunks)
     totals[-1], d_gate, d_values = lax.optimization_barrier((totals[-1], d_gate, d_values))
     pieces = []
     for total in totals:

time: 253 us -> 251 us (level)
  local copies, waits for them, and re-layouts: 14.1 us -> 11.2 us
  Pallas kernels: 61.3 us -> 63.9 us
    ppermute x23 -> x19, waiting for transfers between devices: 99.9 us -> 88.7 us  [swap(): return lax.ppermute(array, axis, [(i, i ^ bit) for i in range(size)])]
    all_to_all x5, waiting for transfers between devices: 8.43 us -> 16.9 us  [exchange(): lax.all_to_all(blocks, 'seq', split_axis=0, concat_axis=0, tiled=True, ax...]
    pallas_call x12, Pallas kernels: 45.9 us -> 49.5 us  [call(): pl.pallas_call(kernel, out_shape=outs, in_specs=specs, out_specs=[whole]...]
    ppermute x23 -> x19, starting transfers between devices: 15.7 us -> 18 us  [swap(): return lax.ppermute(array, axis, [(i, i ^ bit) for i in range(size)])]
    unnamed x53 -> x34, local copies, waits for them, and re-layouts: 10.9 us -> 9.09 us
  transfers between devices with their start and end apart: 28 -> 24, of which waited for: 10 -> 14; matrix products, arithmetic and copies ran while one was open for 8% -> 6% of each run, Pallas kernels for 21% -> 24%
where the time goes in v3:
time: 251 us; the launch traced here: 250 us
  waiting for transfers between devices  106 us (42%)
  Pallas kernels  63.9 us (25%)
  starting transfers between devices  52.1 us (21%)
  local copies, waits for them, and re-layouts  11.2 us (4%)
  matrix products  8.37 us (3%)
  other arithmetic  7.48 us (3%)
    ppermute x19, waiting for transfers between devices, swap(): return lax.ppermute(array, axis, [(i, i ^ bit) for i in range(size)])  88.7 us
    pallas_call x12, Pallas kernels, call(): pl.pallas_call(kernel, out_shape=outs, in_specs=specs, out_specs=[whole]...  49.5 us
    all_to_all x5, starting transfers between devices, exchange(): lax.all_to_all(blocks, 'seq', split_axis=0, concat_axis=0, tiled=True, ax...  34.1 us
    ppermute x19, starting transfers between devices, swap(): return lax.ppermute(array, axis, [(i, i ^ bit) for i in range(size)])  18 us
    all_to_all x5, waiting for transfers between devices, exchange(): lax.all_to_all(blocks, 'seq', split_axis=0, concat_axis=0, tiled=True, ax...  16.9 us
    pallas_call x4, Pallas kernels, outer_product(): pl.pallas_call(functools.partial(outer_kernel, groups=len(groups), tiles=...  14.3 us
    unnamed x34, local copies, waits for them, and re-layouts  9.09 us
    dot_general x1, matrix products, on_device(): jnp.dot(full_grad, out_weight, preferred_element_type=F32).astype(BF16)  8.37 us
  transfers between devices with their start and end apart: 24, of which 14 were waited for; matrix products, arithmetic and copies ran while one was open for 6% of the time, Pallas kernels for 24%

profile of v3, /device:TPU:0, one launch (start us, length us, event | category | flops | bytes accessed | tf_op | source)
XLA Modules:
  0.0 249.6 jit_solution(11236163269916763689)
XLA Ops:
  6.0 7.4 %all-to-all-start = ((bf16[16,2,256,128]{3,2,1,0:T(8,128)(2,1)}), bf16[16,2,256,128]{3,2,1,0:T(8,128)(2,1)}, u32[]{:S(2)}, u32[]{:S(2)}) async-start(bf16[16,2,256,128]{3,2,1,0:T(8,128)(2,1)} %shard_map.122), calls=%async_computation | async-start | bytes 4194304 | tf_op jit(solution)/shard_map/all_to_all | solution.py:423
  18.7 20.5 %collective-permute-done.1.x_ref = bf16[256,2048]{1,0:T(8,128)(2,1)} collective-permute-done((bf16[256,2048]{1,0:T(8,128)(2,1)}, bf16[256,2048]{1,0:T(8,128)(2,1)}, u32[]{:S(2)}, u32[]{:S(2)}) %collective-permute-start.1) | collective-permute-done | bytes 1048608 | tf_op jit(solution)/shard_map/ppermute | solution.py:305
  40.9 8.4 %convolution_convert_fusion.grad_ref = bf16[256,2048]{1,0:T(8,128)(2,1)S(1)} fusion(bf16[4096,2048]{1,0:T(8,128)(2,1)} %param.11, bf16[256,2048]{1,0:T(8,128)(2,1)S(1)} %get-tuple-element.104, bf16[256,2048]{1,0:T(8,128)(2,1)S(1)} %get-tuple-element.103), kind=kOutput, calls=%fused_computation | convolution fusion | flops 4299685888 | bytes 19922944 | tf_op jit(solution)/shard_map/dot_general | solution.py:455
  54.7 11.2 %all-to-all-start.1 = ((bf16[16,1,256,128]{3,2,1,0:T(8,128)(2,1)}), bf16[16,1,256,128]{3,2,1,0:T(8,128)(2,1)}, u32[]{:S(2)}, u32[]{:S(2)}) async-start(bf16[16,1,256,128]{3,2,1,0:T(8,128)(2,1)} %copy-done.5), calls=%async_computation.1 | async-start | bytes 2097152 | tf_op jit(solution)/shard_map/all_to_all | solution.py:423
  70.2 16.3 %shard_map.123 = (f32[33,256,256]{2,1,0:T(8,128)}, bf16[16,256,128]{2,1,0:T(8,128)(2,1)S(1)}) custom-call(bf16[16,2,256,128]{3,2,1,0:T(8,128)(2,1)} %all-to-all-done.fields_ref, bf16[33,256,256]{2,1,0:T(8,128)(2,1)} %constant.68.clone.there_ref, bf16[33,256,256]{2,1,0:T(8,128)(2,1)} %constant.69.clone.back_ref), custom_call_target="tpu_custom_call" | custom-call | flops 20761804800 | bytes 20447232 | tf_op jit(solution)/shard_map/pallas_call | solution.py:289
  91.1 4.5 %all-to-all-start.2 = ((bf16[4,4,256,128]{3,2,1,0:T(8,128)(2,1)}), bf16[4,4,256,128]{3,2,1,0:T(8,128)(2,1)}, u32[]{:S(2)}, u32[]{:S(2)}) async-start(bf16[4,4,256,128]{3,2,1,0:T(8,128)(2,1)} %bitcast.34), calls=%async_computation.2 | async-start | bytes 2097152 | tf_op jit(solution)/shard_map/all_to_all | solution.py:423
  95.7 17.0 %shard_map.125 = (bf16[16,256,128]{2,1,0:T(8,128)(2,1)S(1)}, bf16[16,272,128]{2,1,0:T(8,128)(2,1)}) custom-call(bf16[16,1,256,128]{3,2,1,0:T(8,128)(2,1)} %all-to-all-done.1.g_ref, bf16[16,2,256,128]{3,2,1,0:T(8,128)(2,1)} %all-to-all-done.fields_ref, f32[33,256,256]{2,1,0:T(8,128)} %get-tuple-element.69.spec_ref, ...), custom_call_target="tpu_custom_call" | custom-call | flops 20761804800 | bytes 22609920 | tf_op jit(solution)/shard_map/pallas_call | solution.py:289
  113.7 8.6 %all-to-all-done.2.refs_4_ = bf16[4,4,256,128]{3,2,1,0:T(8,128)(2,1)} async-done(((bf16[4,4,256,128]{3,2,1,0:T(8,128)(2,1)}), bf16[4,4,256,128]{3,2,1,0:T(8,128)(2,1)}, u32[]{:S(2)}, u32[]{:S(2)}) %all-to-all-start.2) | async-done | bytes 1048608 | tf_op jit(solution)/shard_map/all_to_all | solution.py:423
  122.3 4.3 %all-to-all-start.3 = ((bf16[16,256,128]{2,1,0:T(8,128)(2,1)}), bf16[16,256,128]{2,1,0:T(8,128)(2,1)}, u32[]{:S(2)}, u32[]{:S(2)}) async-start(bf16[16,256,128]{2,1,0:T(8,128)(2,1)} %copy-done.8), calls=%async_computation.3 | async-start | bytes 2097152 | tf_op jit(solution)/shard_map/all_to_all | solution.py:423
  134.0 3.4 %shard_map.127 = bf16[1024,512]{1,0:T(8,128)(2,1)S(1)} custom-call(s32[1]{0:T(128)} %bitcast.9.at_ref, bf16[2048,256]{1,0:T(8,128)(2,1)S(1)} %shard_map.119.refs_0_, bf16[2048,256]{1,0:T(8,128)(2,1)S(1)} %collective-permute-done.refs_1_, bf16[2048,256]{1,0:T(8,128)(2,1)} %collective-permute-done.6.refs_2_, bf16[2048,256]{1,0:T(8,128)(2,1)} %collective-permute-done.7.refs_3_, ...), custom_call_target="tpu_custom_call" | custom-call | flops 2147483648 | bytes 3145728 | tf_op jit(solution)/shard_map/pallas_call | solution.py:370
  139.2 4.1 %shard_map.128 = bf16[1024,512]{1,0:T(8,128)(2,1)} custom-call(s32[1]{0:T(128)} %bitcast.10.at_ref, bf16[2048,256]{1,0:T(8,128)(2,1)S(1)} %shard_map.119.refs_0_, bf16[2048,256]{1,0:T(8,128)(2,1)S(1)} %collective-permute-done.refs_1_, bf16[2048,256]{1,0:T(8,128)(2,1)} %collective-permute-done.6.refs_2_, bf16[2048,256]{1,0:T(8,128)(2,1)} %collective-permute-done.7.refs_3_, ...), custom_call_target="tpu_custom_call" | custom-call | flops 2147483648 | bytes 3145728 | tf_op jit(solution)/shard_map/pallas_call | solution.py:370
  143.3 6.6 %all-to-all-done.3.moved_ref = bf16[16,256,128]{2,1,0:T(8,128)(2,1)} async-done(((bf16[16,256,128]{2,1,0:T(8,128)(2,1)}), bf16[16,256,128]{2,1,0:T(8,128)(2,1)}, u32[]{:S(2)}, u32[]{:S(2)}) %all-to-all-start.3) | async-done | bytes 1048608 | tf_op jit(solution)/shard_map/all_to_all | solution.py:423
  150.0 6.6 %all-to-all-start.4 = ((bf16[16,272,128]{2,1,0:T(8,128)(2,1)}), bf16[16,272,128]{2,1,0:T(8,128)(2,1)}, u32[]{:S(2)}, u32[]{:S(2)}) async-start(bf16[16,272,128]{2,1,0:T(8,128)(2,1)} %get-tuple-element.90), calls=%async_computation.4 | async-start | bytes 2228224 | tf_op jit(solution)/shard_map/all_to_all | solution.py:423
  156.6 3.4 %shard_map.129 = bf16[1024,512]{1,0:T(8,128)(2,1)S(1)} custom-call(s32[1]{0:T(128)} %bitcast.11.at_ref, bf16[2048,256]{1,0:T(8,128)(2,1)S(1)} %shard_map.119.refs_0_, bf16[2048,256]{1,0:T(8,128)(2,1)S(1)} %collective-permute-done.refs_1_, bf16[2048,256]{1,0:T(8,128)(2,1)} %collective-permute-done.6.refs_2_, ...), custom_call_target="tpu_custom_call" | custom-call | flops 2147483648 | bytes 3145728 | tf_op jit(solution)/shard_map/pallas_call | solution.py:370
  160.0 18.4 %collective-permute-done.10 = bf16[1024,512]{1,0:T(8,128)(2,1)} collective-permute-done((bf16[1024,512]{1,0:T(8,128)(2,1)S(1)}, bf16[1024,512]{1,0:T(8,128)(2,1)}, u32[]{:S(2)}, u32[]{:S(2)}) %collective-permute-start.10) | collective-permute-done | bytes 1048608 | tf_op jit(solution)/shard_map/ppermute | solution.py:305
  180.9 4.2 %collective-permute-start.12 = (bf16[1024,512]{1,0:T(8,128)(2,1)}, bf16[1024,512]{1,0:T(8,128)(2,1)}, u32[]{:S(2)}, u32[]{:S(2)}) collective-permute-start(bf16[1024,512]{1,0:T(8,128)(2,1)} %add_convert_fusion), channel_id=1, source_target_pairs={{0,16},{2,18},{4,20},{6,22},{8,24},{10,26},{12,28},{14,30},{16,0},... | collective-permute-start | bytes 3145736 | tf_op jit(solution)/shard_map/ppermute | solution.py:305
  186.9 3.4 %shard_map.130 = bf16[1024,512]{1,0:T(8,128)(2,1)S(1)} custom-call(s32[1]{0:T(128)} %bitcast.at_ref, bf16[2048,256]{1,0:T(8,128)(2,1)S(1)} %shard_map.119.refs_0_, bf16[2048,256]{1,0:T(8,128)(2,1)S(1)} %collective-permute-done.refs_1_, bf16[2048,256]{1,0:T(8,128)(2,1)} %collective-permute-done.6.refs_2_, bf16[2048,256]{1,0:T(8,128)(2,1)} %collective-permute-done.7.refs_3_, ...), custom_call_target="tpu_custom_call" | custom-call | flops 2147483648 | bytes 3145728 | tf_op jit(solution)/shard_map/pallas_call | solution.py:370
  190.4 5.2 %collective-permute-done.14 = bf16[4,256,128]{2,1,0:T(8,128)(2,1)} collective-permute-done((bf16[4,256,128]{2,1,0:T(8,128)(2,1)}, bf16[4,256,128]{2,1,0:T(8,128)(2,1)}, u32[]{:S(2)}, u32[]{:S(2)}) %collective-permute-start.14) | collective-permute-done | bytes 262176 | tf_op jit(solution)/shard_map/ppermute | solution.py:305
  195.6 5.1 %collective-permute-done.15 = bf16[4,256,128]{2,1,0:T(8,128)(2,1)} collective-permute-done((bf16[4,256,128]{2,1,0:T(8,128)(2,1)S(1)}, bf16[4,256,128]{2,1,0:T(8,128)(2,1)}, u32[]{:S(2)}, u32[]{:S(2)}) %collective-permute-start.15) | collective-permute-done | bytes 262176 | tf_op jit(solution)/shard_map/ppermute | solution.py:305
  203.3 2.5 shard_map.132
  205.8 26.1 %collective-permute-done.11 = bf16[1024,512]{1,0:T(8,128)(2,1)} collective-permute-done((bf16[1024,512]{1,0:T(8,128)(2,1)}, bf16[1024,512]{1,0:T(8,128)(2,1)}, u32[]{:S(2)}, u32[]{:S(2)}) %collective-permute-start.11) | collective-permute-done | bytes 1048608 | tf_op jit(solution)/shard_map/ppermute | solution.py:305
  235.9 3.0 %shard_map.133 = (f32[256,2048]{1,0:T(8,128)}, f32[1,2048]{1,0:T(1,128)}) custom-call(bf16[16,272,128]{2,1,0:T(8,128)(2,1)} %all-to-all-done.4.moved_ref, f32[1,2048]{1,0:T(1,128)S(1)} %bitcast.37, s32[1]{0:T(128)} %bitcast.2.start_ref), custom_call_target="tpu_custom_call" | custom-call | bytes 3227652 | tf_op jit(solution)/shard_map/pallas_call | solution.py:289
  238.9 4.3 %collective-permute-done.17 = bf16[256,512]{1,0:T(8,128)(2,1)S(1)} collective-permute-done((bf16[256,512]{1,0:T(8,128)(2,1)S(1)}, bf16[256,512]{1,0:T(8,128)(2,1)S(1)}, u32[]{:S(2)}, u32[]{:S(2)}) %collective-permute-start.17) | collective-permute-done | bytes 262176 | tf_op jit(solution)/shard_map/ppermute | solution.py:305
  243.2 4.7 %collective-permute-done.18 = bf16[256,512]{1,0:T(8,128)(2,1)S(1)} collective-permute-done((bf16[256,512]{1,0:T(8,128)(2,1)S(1)}, bf16[256,512]{1,0:T(8,128)(2,1)S(1)}, u32[]{:S(2)}, u32[]{:S(2)}) %collective-permute-start.18) | collective-permute-done | bytes 262176 | tf_op jit(solution)/shard_map/ppermute | solution.py:305
  (82 shorter events, 49.4 us)
Async XLA Ops:
  6.0 48.8 %all-to-all-start = ((bf16[16,2,256,128]{3,2,1,0:T(8,128)(2,1)}), bf16[16,2,256,128]{3,2,1,0:T(8,128)(2,1)}, u32[]{:S(2)}, u32[]{:S(2)}) async-start(bf16[16,2,256,128]{3,2,1,0:T(8,128)(2,1)} %shard_map.122), calls=%async_computation | async-start | bytes 4194304 | tf_op jit(solution)/shard_map/all_to_all | solution.py:423
  13.4 25.8 %collective-permute-start.1 = (bf16[256,2048]{1,0:T(8,128)(2,1)}, bf16[256,2048]{1,0:T(8,128)(2,1)}, u32[]{:S(2)}, u32[]{:S(2)}) collective-permute-start(bf16[256,2048]{1,0:T(8,128)(2,1)} %x_ref.1), channel_id=1, source_target_pairs={{0,1},{1,0},{2,3},{3,2},{4,5},{5,4},{6,7},{7,6},{8,9},{9,8},{10,11... | collective-permute-start | bytes 3145736 | tf_op jit(solution)/shard_map/ppermute | solution.py:305
  16.6 53.6 %collective-permute-start = (bf16[2048,256]{1,0:T(8,128)(2,1)S(1)}, bf16[2048,256]{1,0:T(8,128)(2,1)S(1)}, u32[]{:S(2)}, u32[]{:S(2)}) collective-permute-start(bf16[2048,256]{1,0:T(8,128)(2,1)S(1)} %shard_map.119.refs_0_), channel_id=1, source_target_pairs={{0,4},{2,6},{4,0},{6,2},{8,12},{10,14},{12,8},{14,10},{16,20},{18,... | collective-permute-start | bytes 3145736 | tf_op jit(solution)/shard_map/ppermute | solution.py:305
  54.7 34.3 %all-to-all-start.1 = ((bf16[16,1,256,128]{3,2,1,0:T(8,128)(2,1)}), bf16[16,1,256,128]{3,2,1,0:T(8,128)(2,1)}, u32[]{:S(2)}, u32[]{:S(2)}) async-start(bf16[16,1,256,128]{3,2,1,0:T(8,128)(2,1)} %copy-done.5), calls=%async_computation.1 | async-start | bytes 2097152 | tf_op jit(solution)/shard_map/all_to_all | solution.py:423
  68.0 21.0 %collective-permute-start.3 = (bf16[4,256,128]{2,1,0:T(8,128)(2,1)}, bf16[4,256,128]{2,1,0:T(8,128)(2,1)}, u32[]{:S(2)}, u32[]{:S(2)}) collective-permute-start(bf16[4,256,128]{2,1,0:T(8,128)(2,1)} %get-tuple-element.111), channel_id=1, source_target_pairs={{0,4},{2,6},{4,0},{6,2},{8,12},{10,14},{12,8},{14,10},{16,20},{18,... | collective-permute-start | bytes 786440 | tf_op jit(solution)/shard_map/ppermute | solution.py:305
  69.9 19.1 %collective-permute-start.4 = (bf16[4,256,128]{2,1,0:T(8,128)(2,1)}, bf16[4,256,128]{2,1,0:T(8,128)(2,1)}, u32[]{:S(2)}, u32[]{:S(2)}) collective-permute-start(bf16[4,256,128]{2,1,0:T(8,128)(2,1)} %get-tuple-element.110), channel_id=1, source_target_pairs={{0,2},{2,0},{4,6},{6,4},{8,10},{10,8},{12,14},{14,12},{16,18},{18,... | collective-permute-start | bytes 786440 | tf_op jit(solution)/shard_map/ppermute | solution.py:305
  69.9 21.2 %collective-permute-start.5 = (bf16[4,256,128]{2,1,0:T(8,128)(2,1)}, bf16[4,256,128]{2,1,0:T(8,128)(2,1)}, u32[]{:S(2)}, u32[]{:S(2)}) collective-permute-start(bf16[4,256,128]{2,1,0:T(8,128)(2,1)} %get-tuple-element.109), channel_id=1, source_target_pairs={{0,6},{2,4},{4,2},{6,0},{8,14},{10,12},{12,10},{14,8},{16,22},{18,... | collective-permute-start | bytes 786440 | tf_op jit(solution)/shard_map/ppermute | solution.py:305
  87.4 39.2 %collective-permute-start.2 = (bf16[2048,256]{1,0:T(8,128)(2,1)S(1)}, bf16[2048,256]{1,0:T(8,128)(2,1)}, u32[]{:S(2)}, u32[]{:S(2)}) collective-permute-start(bf16[2048,256]{1,0:T(8,128)(2,1)S(1)} %collective-permute-done.refs_1_), channel_id=1, source_target_pairs={{0,1},{1,0},{2,3},{3,2},{4,5},{5,4},{6,7},{7,6},{8,9},{9,8},{10,11... | collective-permute-start | bytes 3145736 | tf_op jit(solution)/shard_map/ppermute | solution.py:305
  91.1 31.1 %all-to-all-start.2 = ((bf16[4,4,256,128]{3,2,1,0:T(8,128)(2,1)}), bf16[4,4,256,128]{3,2,1,0:T(8,128)(2,1)}, u32[]{:S(2)}, u32[]{:S(2)}) async-start(bf16[4,4,256,128]{3,2,1,0:T(8,128)(2,1)} %bitcast.34), calls=%async_computation.2 | async-start | bytes 2097152 | tf_op jit(solution)/shard_map/all_to_all | solution.py:423
  122.3 27.7 %all-to-all-start.3 = ((bf16[16,256,128]{2,1,0:T(8,128)(2,1)}), bf16[16,256,128]{2,1,0:T(8,128)(2,1)}, u32[]{:S(2)}, u32[]{:S(2)}) async-start(bf16[16,256,128]{2,1,0:T(8,128)(2,1)} %copy-done.8), calls=%async_computation.3 | async-start | bytes 2097152 | tf_op jit(solution)/shard_map/all_to_all | solution.py:423
  126.6 5.1 %collective-permute-start.6 = (bf16[2048,256]{1,0:T(8,128)(2,1)S(1)}, bf16[2048,256]{1,0:T(8,128)(2,1)}, u32[]{:S(2)}, u32[]{:S(2)}) collective-permute-start(bf16[2048,256]{1,0:T(8,128)(2,1)S(1)} %shard_map.119.refs_0_), channel_id=1, source_target_pairs={{0,2},{2,0},{4,6},{6,4},{8,10},{10,8},{12,14},{14,12},{16,18},{18,... | collective-permute-start | bytes 3145736 | tf_op jit(solution)/shard_map/ppermute | solution.py:305
  126.9 5.6 %collective-permute-start.7 = (bf16[2048,256]{1,0:T(8,128)(2,1)S(1)}, bf16[2048,256]{1,0:T(8,128)(2,1)}, u32[]{:S(2)}, u32[]{:S(2)}) collective-permute-start(bf16[2048,256]{1,0:T(8,128)(2,1)S(1)} %collective-permute-done.refs_1_), channel_id=1, source_target_pairs={{0,2},{2,0},{4,6},{6,4},{8,10},{10,8},{12,14},{14,12},{16,18},{18,... | collective-permute-start | bytes 3145736 | tf_op jit(solution)/shard_map/ppermute | solution.py:305
  127.2 6.8 %collective-permute-start.8 = (bf16[2048,256]{1,0:T(8,128)(2,1)S(1)}, bf16[2048,256]{1,0:T(8,128)(2,1)}, u32[]{:S(2)}, u32[]{:S(2)}) collective-permute-start(bf16[2048,256]{1,0:T(8,128)(2,1)S(1)} %shard_map.120.refs_4_), channel_id=1, source_target_pairs={{0,2},{2,0},{4,6},{6,4},{8,10},{10,8},{12,14},{14,12},{16,18},{18,... | collective-permute-start | bytes 3145736 | tf_op jit(solution)/shard_map/ppermute | solution.py:305
  127.4 6.6 %collective-permute-start.9 = (bf16[2048,256]{1,0:T(8,128)(2,1)}, bf16[2048,256]{1,0:T(8,128)(2,1)}, u32[]{:S(2)}, u32[]{:S(2)}) collective-permute-start(bf16[2048,256]{1,0:T(8,128)(2,1)} %collective-permute-done.2.refs_5_), channel_id=1, source_target_pairs={{0,2},{2,0},{4,6},{6,4},{8,10},{10,8},{12,14},{14,12},{16,18},{18,... | collective-permute-start | bytes 3145736 | tf_op jit(solution)/shard_map/ppermute | solution.py:305
  137.4 41.0 %collective-permute-start.10 = (bf16[1024,512]{1,0:T(8,128)(2,1)S(1)}, bf16[1024,512]{1,0:T(8,128)(2,1)}, u32[]{:S(2)}, u32[]{:S(2)}) collective-permute-start(bf16[1024,512]{1,0:T(8,128)(2,1)S(1)} %shard_map.127), channel_id=1, source_target_pairs={{0,8},{2,10},{4,12},{6,14},{8,0},{10,2},{12,4},{14,6},{16,24},{18,... | collective-permute-start | bytes 3145736 | tf_op jit(solution)/shard_map/ppermute | solution.py:305
  150.0 81.9 %all-to-all-start.4 = ((bf16[16,272,128]{2,1,0:T(8,128)(2,1)}), bf16[16,272,128]{2,1,0:T(8,128)(2,1)}, u32[]{:S(2)}, u32[]{:S(2)}) async-start(bf16[16,272,128]{2,1,0:T(8,128)(2,1)} %get-tuple-element.90), calls=%async_computation.4 | async-start | bytes 2228224 | tf_op jit(solution)/shard_map/all_to_all | solution.py:423
  178.4 53.4 %collective-permute-start.11 = (bf16[1024,512]{1,0:T(8,128)(2,1)}, bf16[1024,512]{1,0:T(8,128)(2,1)}, u32[]{:S(2)}, u32[]{:S(2)}) collective-permute-start(bf16[1024,512]{1,0:T(8,128)(2,1)} %shard_map.128), channel_id=1, source_target_pairs={{0,8},{2,10},{4,12},{6,14},{8,0},{10,2},{12,4},{14,6},{16,24},{18,... | collective-permute-start | bytes 3145736 | tf_op jit(solution)/shard_map/ppermute | solution.py:305
  180.9 51.0 %collective-permute-start.12 = (bf16[1024,512]{1,0:T(8,128)(2,1)}, bf16[1024,512]{1,0:T(8,128)(2,1)}, u32[]{:S(2)}, u32[]{:S(2)}) collective-permute-start(bf16[1024,512]{1,0:T(8,128)(2,1)} %add_convert_fusion), channel_id=1, source_target_pairs={{0,16},{2,18},{4,20},{6,22},{8,24},{10,26},{12,28},{14,30},{16,0},... | collective-permute-start | bytes 3145736 | tf_op jit(solution)/shard_map/ppermute | solution.py:305
  185.1 5.3 %collective-permute-start.13 = (bf16[4,256,128]{2,1,0:T(8,128)(2,1)}, bf16[4,256,128]{2,1,0:T(8,128)(2,1)}, u32[]{:S(2)}, u32[]{:S(2)}) collective-permute-start(bf16[4,256,128]{2,1,0:T(8,128)(2,1)} %get-tuple-element.93), channel_id=1, source_target_pairs={{0,2},{2,0},{4,6},{6,4},{8,10},{10,8},{12,14},{14,12},{16,18},{18,... | collective-permute-start | bytes 786440 | tf_op jit(solution)/shard_map/ppermute | solution.py:305
  185.1 10.5 %collective-permute-start.14 = (bf16[4,256,128]{2,1,0:T(8,128)(2,1)}, bf16[4,256,128]{2,1,0:T(8,128)(2,1)}, u32[]{:S(2)}, u32[]{:S(2)}) collective-permute-start(bf16[4,256,128]{2,1,0:T(8,128)(2,1)} %get-tuple-element.94), channel_id=1, source_target_pairs={{0,4},{2,6},{4,0},{6,2},{8,12},{10,14},{12,8},{14,10},{16,20},{18,... | collective-permute-start | bytes 786440 | tf_op jit(solution)/shard_map/ppermute | solution.py:305
  186.3 14.4 %collective-permute-start.15 = (bf16[4,256,128]{2,1,0:T(8,128)(2,1)S(1)}, bf16[4,256,128]{2,1,0:T(8,128)(2,1)}, u32[]{:S(2)}, u32[]{:S(2)}) collective-permute-start(bf16[4,256,128]{2,1,0:T(8,128)(2,1)S(1)} %copy-done.16), channel_id=1, source_target_pairs={{0,6},{2,4},{4,2},{6,0},{8,14},{10,12},{12,10},{14,8},{16,22},{18,... | collective-permute-start | bytes 786440 | tf_op jit(solution)/shard_map/ppermute | solution.py:305
  233.9 5.0 %collective-permute-start.16 = (bf16[256,512]{1,0:T(8,128)(2,1)S(1)}, bf16[256,512]{1,0:T(8,128)(2,1)S(1)}, u32[]{:S(2)}, u32[]{:S(2)}) collective-permute-start(bf16[256,512]{1,0:T(8,128)(2,1)S(1)} %get-tuple-element.108), channel_id=1, source_target_pairs={{0,2},{2,0},{4,6},{6,4},{8,10},{10,8},{12,14},{14,12},{16,18},{18,... | collective-permute-start | bytes 786440 | tf_op jit(solution)/shard_map/ppermute | solution.py:305
  234.0 9.2 %collective-permute-start.17 = (bf16[256,512]{1,0:T(8,128)(2,1)S(1)}, bf16[256,512]{1,0:T(8,128)(2,1)S(1)}, u32[]{:S(2)}, u32[]{:S(2)}) collective-permute-start(bf16[256,512]{1,0:T(8,128)(2,1)S(1)} %get-tuple-element.107), channel_id=1, source_target_pairs={{0,4},{2,6},{4,0},{6,2},{8,12},{10,14},{12,8},{14,10},{16,20},{18,... | collective-permute-start | bytes 786440 | tf_op jit(solution)/shard_map/ppermute | solution.py:305
  235.6 12.3 %collective-permute-start.18 = (bf16[256,512]{1,0:T(8,128)(2,1)S(1)}, bf16[256,512]{1,0:T(8,128)(2,1)S(1)}, u32[]{:S(2)}, u32[]{:S(2)}) collective-permute-start(bf16[256,512]{1,0:T(8,128)(2,1)S(1)} %get-tuple-element.106), channel_id=1, source_target_pairs={{0,6},{2,4},{4,2},{6,0},{8,14},{10,12},{12,10},{14,8},{16,22},{18,... | collective-permute-start | bytes 786440 | tf_op jit(solution)/shard_map/ppermute | solution.py:305
  (17 other events, 169.8 us)

commit v4 on v3

--- a/solution.py
+++ b/solution.py
@@ -352,7 +352,7 @@
 def outer_product(groups, rhs, at, blocks):
     rows, depth = groups[0][0].shape
     size = rows * len(groups) // blocks
-    tile = math.gcd(size, 512)
+    tile = math.gcd(size, 1024)
     tiles = rows // tile
     steps = size // tile
     wide = rhs.shape[1]

time: 251 us -> 251 us (level)
  no operation moved by 1% of the time
where the time goes in v4:
time: 251 us; the launch traced here: 250 us
  waiting for transfers between devices  105 us (42%)
  Pallas kernels  64.4 us (26%)
  starting transfers between devices  52.1 us (21%)
  local copies, waits for them, and re-layouts  11.2 us (4%)
  matrix products  8.37 us (3%)
  other arithmetic  7.48 us (3%)
    ppermute x19, waiting for transfers between devices, swap(): return lax.ppermute(array, axis, [(i, i ^ bit) for i in range(size)])  88.6 us
    pallas_call x12, Pallas kernels, call(): pl.pallas_call(kernel, out_shape=outs, in_specs=specs, out_specs=[whole]...  49.5 us
    all_to_all x5, starting transfers between devices, exchange(): lax.all_to_all(blocks, 'seq', split_axis=0, concat_axis=0, tiled=True, ax...  34.1 us
    ppermute x19, starting transfers between devices, swap(): return lax.ppermute(array, axis, [(i, i ^ bit) for i in range(size)])  18.1 us
    all_to_all x5, waiting for transfers between devices, exchange(): lax.all_to_all(blocks, 'seq', split_axis=0, concat_axis=0, tiled=True, ax...  16.4 us
    pallas_call x4, Pallas kernels, outer_product(): pl.pallas_call(functools.partial(outer_kernel, groups=len(groups), tiles=...  14.9 us
    unnamed x34, local copies, waits for them, and re-layouts  9.09 us
    dot_general x1, matrix products, on_device(): jnp.dot(full_grad, out_weight, preferred_element_type=F32).astype(BF16)  8.37 us
  transfers between devices with their start and end apart: 24, of which 14 were waited for; matrix products, arithmetic and copies ran while one was open for 6% of the time, Pallas kernels for 24%

profile of v4, /device:TPU:0, one launch (start us, length us, event | category | flops | bytes accessed | tf_op | source)
XLA Modules:
  0.0 249.6 jit_solution(4348374333332489745)
XLA Ops:
  6.0 7.4 %all-to-all-start = ((bf16[16,2,256,128]{3,2,1,0:T(8,128)(2,1)}), bf16[16,2,256,128]{3,2,1,0:T(8,128)(2,1)}, u32[]{:S(2)}, u32[]{:S(2)}) async-start(bf16[16,2,256,128]{3,2,1,0:T(8,128)(2,1)} %shard_map.122), calls=%async_computation | async-start | bytes 4194304 | tf_op jit(solution)/shard_map/all_to_all | solution.py:423
  18.7 20.5 %collective-permute-done.1.x_ref = bf16[256,2048]{1,0:T(8,128)(2,1)} collective-permute-done((bf16[256,2048]{1,0:T(8,128)(2,1)}, bf16[256,2048]{1,0:T(8,128)(2,1)}, u32[]{:S(2)}, u32[]{:S(2)}) %collective-permute-start.1) | collective-permute-done | bytes 1048608 | tf_op jit(solution)/shard_map/ppermute | solution.py:305
  40.9 8.4 %convolution_convert_fusion.grad_ref = bf16[256,2048]{1,0:T(8,128)(2,1)S(1)} fusion(bf16[4096,2048]{1,0:T(8,128)(2,1)} %param.11, bf16[256,2048]{1,0:T(8,128)(2,1)S(1)} %get-tuple-element.104, bf16[256,2048]{1,0:T(8,128)(2,1)S(1)} %get-tuple-element.103), kind=kOutput, calls=%fused_computation | convolution fusion | flops 4299685888 | bytes 19922944 | tf_op jit(solution)/shard_map/dot_general | solution.py:455
  54.7 11.2 %all-to-all-start.1 = ((bf16[16,1,256,128]{3,2,1,0:T(8,128)(2,1)}), bf16[16,1,256,128]{3,2,1,0:T(8,128)(2,1)}, u32[]{:S(2)}, u32[]{:S(2)}) async-start(bf16[16,1,256,128]{3,2,1,0:T(8,128)(2,1)} %copy-done.5), calls=%async_computation.1 | async-start | bytes 2097152 | tf_op jit(solution)/shard_map/all_to_all | solution.py:423
  70.2 16.3 %shard_map.123 = (f32[33,256,256]{2,1,0:T(8,128)}, bf16[16,256,128]{2,1,0:T(8,128)(2,1)S(1)}) custom-call(bf16[16,2,256,128]{3,2,1,0:T(8,128)(2,1)} %all-to-all-done.fields_ref, bf16[33,256,256]{2,1,0:T(8,128)(2,1)} %constant.68.clone.there_ref, bf16[33,256,256]{2,1,0:T(8,128)(2,1)} %constant.69.clone.back_ref), custom_call_target="tpu_custom_call" | custom-call | flops 20761804800 | bytes 20447232 | tf_op jit(solution)/shard_map/pallas_call | solution.py:289
  91.1 4.5 %all-to-all-start.2 = ((bf16[4,4,256,128]{3,2,1,0:T(8,128)(2,1)}), bf16[4,4,256,128]{3,2,1,0:T(8,128)(2,1)}, u32[]{:S(2)}, u32[]{:S(2)}) async-start(bf16[4,4,256,128]{3,2,1,0:T(8,128)(2,1)} %bitcast.34), calls=%async_computation.2 | async-start | bytes 2097152 | tf_op jit(solution)/shard_map/all_to_all | solution.py:423
  95.7 17.0 %shard_map.125 = (bf16[16,256,128]{2,1,0:T(8,128)(2,1)S(1)}, bf16[16,272,128]{2,1,0:T(8,128)(2,1)}) custom-call(bf16[16,1,256,128]{3,2,1,0:T(8,128)(2,1)} %all-to-all-done.1.g_ref, bf16[16,2,256,128]{3,2,1,0:T(8,128)(2,1)} %all-to-all-done.fields_ref, f32[33,256,256]{2,1,0:T(8,128)} %get-tuple-element.69.spec_ref, ...), custom_call_target="tpu_custom_call" | custom-call | flops 20761804800 | bytes 22609920 | tf_op jit(solution)/shard_map/pallas_call | solution.py:289
  113.7 8.6 %all-to-all-done.2.refs_4_ = bf16[4,4,256,128]{3,2,1,0:T(8,128)(2,1)} async-done(((bf16[4,4,256,128]{3,2,1,0:T(8,128)(2,1)}), bf16[4,4,256,128]{3,2,1,0:T(8,128)(2,1)}, u32[]{:S(2)}, u32[]{:S(2)}) %all-to-all-start.2) | async-done | bytes 1048608 | tf_op jit(solution)/shard_map/all_to_all | solution.py:423
  122.3 4.3 %all-to-all-start.3 = ((bf16[16,256,128]{2,1,0:T(8,128)(2,1)}), bf16[16,256,128]{2,1,0:T(8,128)(2,1)}, u32[]{:S(2)}, u32[]{:S(2)}) async-start(bf16[16,256,128]{2,1,0:T(8,128)(2,1)} %copy-done.8), calls=%async_computation.3 | async-start | bytes 2097152 | tf_op jit(solution)/shard_map/all_to_all | solution.py:423
  134.0 3.4 %shard_map.127 = bf16[1024,512]{1,0:T(8,128)(2,1)S(1)} custom-call(s32[1]{0:T(128)} %bitcast.9.at_ref, bf16[2048,256]{1,0:T(8,128)(2,1)S(1)} %shard_map.119.refs_0_, bf16[2048,256]{1,0:T(8,128)(2,1)S(1)} %collective-permute-done.refs_1_, bf16[2048,256]{1,0:T(8,128)(2,1)} %collective-permute-done.6.refs_2_, bf16[2048,256]{1,0:T(8,128)(2,1)} %collective-permute-done.7.refs_3_, ...), custom_call_target="tpu_custom_call" | custom-call | flops 2147483648 | bytes 3145728 | tf_op jit(solution)/shard_map/pallas_call | solution.py:370
  139.2 4.6 %shard_map.128 = bf16[1024,512]{1,0:T(8,128)(2,1)} custom-call(s32[1]{0:T(128)} %bitcast.10.at_ref, bf16[2048,256]{1,0:T(8,128)(2,1)S(1)} %shard_map.119.refs_0_, bf16[2048,256]{1,0:T(8,128)(2,1)S(1)} %collective-permute-done.refs_1_, bf16[2048,256]{1,0:T(8,128)(2,1)} %collective-permute-done.6.refs_2_, bf16[2048,256]{1,0:T(8,128)(2,1)} %collective-permute-done.7.refs_3_, ...), custom_call_target="tpu_custom_call" | custom-call | flops 2147483648 | bytes 3145728 | tf_op jit(solution)/shard_map/pallas_call | solution.py:370
  143.8 6.2 %all-to-all-done.3.moved_ref = bf16[16,256,128]{2,1,0:T(8,128)(2,1)} async-done(((bf16[16,256,128]{2,1,0:T(8,128)(2,1)}), bf16[16,256,128]{2,1,0:T(8,128)(2,1)}, u32[]{:S(2)}, u32[]{:S(2)}) %all-to-all-start.3) | async-done | bytes 1048608 | tf_op jit(solution)/shard_map/all_to_all | solution.py:423
  150.0 6.6 %all-to-all-start.4 = ((bf16[16,272,128]{2,1,0:T(8,128)(2,1)}), bf16[16,272,128]{2,1,0:T(8,128)(2,1)}, u32[]{:S(2)}, u32[]{:S(2)}) async-start(bf16[16,272,128]{2,1,0:T(8,128)(2,1)} %get-tuple-element.90), calls=%async_computation.4 | async-start | bytes 2228224 | tf_op jit(solution)/shard_map/all_to_all | solution.py:423
  156.6 3.4 %shard_map.129 = bf16[1024,512]{1,0:T(8,128)(2,1)S(1)} custom-call(s32[1]{0:T(128)} %bitcast.11.at_ref, bf16[2048,256]{1,0:T(8,128)(2,1)S(1)} %shard_map.119.refs_0_, bf16[2048,256]{1,0:T(8,128)(2,1)S(1)} %collective-permute-done.refs_1_, bf16[2048,256]{1,0:T(8,128)(2,1)} %collective-permute-done.6.refs_2_, ...), custom_call_target="tpu_custom_call" | custom-call | flops 2147483648 | bytes 3145728 | tf_op jit(solution)/shard_map/pallas_call | solution.py:370
  160.0 18.4 %collective-permute-done.10 = bf16[1024,512]{1,0:T(8,128)(2,1)} collective-permute-done((bf16[1024,512]{1,0:T(8,128)(2,1)S(1)}, bf16[1024,512]{1,0:T(8,128)(2,1)}, u32[]{:S(2)}, u32[]{:S(2)}) %collective-permute-start.10) | collective-permute-done | bytes 1048608 | tf_op jit(solution)/shard_map/ppermute | solution.py:305
  180.9 4.2 %collective-permute-start.12 = (bf16[1024,512]{1,0:T(8,128)(2,1)}, bf16[1024,512]{1,0:T(8,128)(2,1)}, u32[]{:S(2)}, u32[]{:S(2)}) collective-permute-start(bf16[1024,512]{1,0:T(8,128)(2,1)} %add_convert_fusion), channel_id=1, source_target_pairs={{0,16},{2,18},{4,20},{6,22},{8,24},{10,26},{12,28},{14,30},{16,0},... | collective-permute-start | bytes 3145736 | tf_op jit(solution)/shard_map/ppermute | solution.py:305
  186.9 3.5 %shard_map.130 = bf16[1024,512]{1,0:T(8,128)(2,1)S(1)} custom-call(s32[1]{0:T(128)} %bitcast.at_ref, bf16[2048,256]{1,0:T(8,128)(2,1)S(1)} %shard_map.119.refs_0_, bf16[2048,256]{1,0:T(8,128)(2,1)S(1)} %collective-permute-done.refs_1_, bf16[2048,256]{1,0:T(8,128)(2,1)} %collective-permute-done.6.refs_2_, bf16[2048,256]{1,0:T(8,128)(2,1)} %collective-permute-done.7.refs_3_, ...), custom_call_target="tpu_custom_call" | custom-call | flops 2147483648 | bytes 3145728 | tf_op jit(solution)/shard_map/pallas_call | solution.py:370
  190.4 5.2 %collective-permute-done.14 = bf16[4,256,128]{2,1,0:T(8,128)(2,1)} collective-permute-done((bf16[4,256,128]{2,1,0:T(8,128)(2,1)}, bf16[4,256,128]{2,1,0:T(8,128)(2,1)}, u32[]{:S(2)}, u32[]{:S(2)}) %collective-permute-start.14) | collective-permute-done | bytes 262176 | tf_op jit(solution)/shard_map/ppermute | solution.py:305
  195.6 5.1 %collective-permute-done.15 = bf16[4,256,128]{2,1,0:T(8,128)(2,1)} collective-permute-done((bf16[4,256,128]{2,1,0:T(8,128)(2,1)S(1)}, bf16[4,256,128]{2,1,0:T(8,128)(2,1)}, u32[]{:S(2)}, u32[]{:S(2)}) %collective-permute-start.15) | collective-permute-done | bytes 262176 | tf_op jit(solution)/shard_map/ppermute | solution.py:305
  203.3 2.5 shard_map.132
  205.8 26.1 %collective-permute-done.11 = bf16[1024,512]{1,0:T(8,128)(2,1)} collective-permute-done((bf16[1024,512]{1,0:T(8,128)(2,1)}, bf16[1024,512]{1,0:T(8,128)(2,1)}, u32[]{:S(2)}, u32[]{:S(2)}) %collective-permute-start.11) | collective-permute-done | bytes 1048608 | tf_op jit(solution)/shard_map/ppermute | solution.py:305
  235.9 3.0 %shard_map.133 = (f32[256,2048]{1,0:T(8,128)}, f32[1,2048]{1,0:T(1,128)}) custom-call(bf16[16,272,128]{2,1,0:T(8,128)(2,1)} %all-to-all-done.4.moved_ref, f32[1,2048]{1,0:T(1,128)S(1)} %bitcast.37, s32[1]{0:T(128)} %bitcast.2.start_ref), custom_call_target="tpu_custom_call" | custom-call | bytes 3227652 | tf_op jit(solution)/shard_map/pallas_call | solution.py:289
  238.9 4.3 %collective-permute-done.17 = bf16[256,512]{1,0:T(8,128)(2,1)S(1)} collective-permute-done((bf16[256,512]{1,0:T(8,128)(2,1)S(1)}, bf16[256,512]{1,0:T(8,128)(2,1)S(1)}, u32[]{:S(2)}, u32[]{:S(2)}) %collective-permute-start.17) | collective-permute-done | bytes 262176 | tf_op jit(solution)/shard_map/ppermute | solution.py:305
  243.2 4.7 %collective-permute-done.18 = bf16[256,512]{1,0:T(8,128)(2,1)S(1)} collective-permute-done((bf16[256,512]{1,0:T(8,128)(2,1)S(1)}, bf16[256,512]{1,0:T(8,128)(2,1)S(1)}, u32[]{:S(2)}, u32[]{:S(2)}) %collective-permute-start.18) | collective-permute-done | bytes 262176 | tf_op jit(solution)/shard_map/ppermute | solution.py:305
  (82 shorter events, 49.4 us)
Async XLA Ops:
  6.0 48.8 %all-to-all-start = ((bf16[16,2,256,128]{3,2,1,0:T(8,128)(2,1)}), bf16[16,2,256,128]{3,2,1,0:T(8,128)(2,1)}, u32[]{:S(2)}, u32[]{:S(2)}) async-start(bf16[16,2,256,128]{3,2,1,0:T(8,128)(2,1)} %shard_map.122), calls=%async_computation | async-start | bytes 4194304 | tf_op jit(solution)/shard_map/all_to_all | solution.py:423
  13.4 25.8 %collective-permute-start.1 = (bf16[256,2048]{1,0:T(8,128)(2,1)}, bf16[256,2048]{1,0:T(8,128)(2,1)}, u32[]{:S(2)}, u32[]{:S(2)}) collective-permute-start(bf16[256,2048]{1,0:T(8,128)(2,1)} %x_ref.1), channel_id=1, source_target_pairs={{0,1},{1,0},{2,3},{3,2},{4,5},{5,4},{6,7},{7,6},{8,9},{9,8},{10,11... | collective-permute-start | bytes 3145736 | tf_op jit(solution)/shard_map/ppermute | solution.py:305
  16.6 53.6 %collective-permute-start = (bf16[2048,256]{1,0:T(8,128)(2,1)S(1)}, bf16[2048,256]{1,0:T(8,128)(2,1)S(1)}, u32[]{:S(2)}, u32[]{:S(2)}) collective-permute-start(bf16[2048,256]{1,0:T(8,128)(2,1)S(1)} %shard_map.119.refs_0_), channel_id=1, source_target_pairs={{0,4},{2,6},{4,0},{6,2},{8,12},{10,14},{12,8},{14,10},{16,20},{18,... | collective-permute-start | bytes 3145736 | tf_op jit(solution)/shard_map/ppermute | solution.py:305
  54.7 34.3 %all-to-all-start.1 = ((bf16[16,1,256,128]{3,2,1,0:T(8,128)(2,1)}), bf16[16,1,256,128]{3,2,1,0:T(8,128)(2,1)}, u32[]{:S(2)}, u32[]{:S(2)}) async-start(bf16[16,1,256,128]{3,2,1,0:T(8,128)(2,1)} %copy-done.5), calls=%async_computation.1 | async-start | bytes 2097152 | tf_op jit(solution)/shard_map/all_to_all | solution.py:423
  68.0 21.0 %collective-permute-start.3 = (bf16[4,256,128]{2,1,0:T(8,128)(2,1)}, bf16[4,256,128]{2,1,0:T(8,128)(2,1)}, u32[]{:S(2)}, u32[]{:S(2)}) collective-permute-start(bf16[4,256,128]{2,1,0:T(8,128)(2,1)} %get-tuple-element.111), channel_id=1, source_target_pairs={{0,4},{2,6},{4,0},{6,2},{8,12},{10,14},{12,8},{14,10},{16,20},{18,... | collective-permute-start | bytes 786440 | tf_op jit(solution)/shard_map/ppermute | solution.py:305
  69.9 19.1 %collective-permute-start.4 = (bf16[4,256,128]{2,1,0:T(8,128)(2,1)}, bf16[4,256,128]{2,1,0:T(8,128)(2,1)}, u32[]{:S(2)}, u32[]{:S(2)}) collective-permute-start(bf16[4,256,128]{2,1,0:T(8,128)(2,1)} %get-tuple-element.110), channel_id=1, source_target_pairs={{0,2},{2,0},{4,6},{6,4},{8,10},{10,8},{12,14},{14,12},{16,18},{18,... | collective-permute-start | bytes 786440 | tf_op jit(solution)/shard_map/ppermute | solution.py:305
  69.9 21.2 %collective-permute-start.5 = (bf16[4,256,128]{2,1,0:T(8,128)(2,1)}, bf16[4,256,128]{2,1,0:T(8,128)(2,1)}, u32[]{:S(2)}, u32[]{:S(2)}) collective-permute-start(bf16[4,256,128]{2,1,0:T(8,128)(2,1)} %get-tuple-element.109), channel_id=1, source_target_pairs={{0,6},{2,4},{4,2},{6,0},{8,14},{10,12},{12,10},{14,8},{16,22},{18,... | collective-permute-start | bytes 786440 | tf_op jit(solution)/shard_map/ppermute | solution.py:305
  87.4 39.2 %collective-permute-start.2 = (bf16[2048,256]{1,0:T(8,128)(2,1)S(1)}, bf16[2048,256]{1,0:T(8,128)(2,1)}, u32[]{:S(2)}, u32[]{:S(2)}) collective-permute-start(bf16[2048,256]{1,0:T(8,128)(2,1)S(1)} %collective-permute-done.refs_1_), channel_id=1, source_target_pairs={{0,1},{1,0},{2,3},{3,2},{4,5},{5,4},{6,7},{7,6},{8,9},{9,8},{10,11... | collective-permute-start | bytes 3145736 | tf_op jit(solution)/shard_map/ppermute | solution.py:305
  91.1 31.1 %all-to-all-start.2 = ((bf16[4,4,256,128]{3,2,1,0:T(8,128)(2,1)}), bf16[4,4,256,128]{3,2,1,0:T(8,128)(2,1)}, u32[]{:S(2)}, u32[]{:S(2)}) async-start(bf16[4,4,256,128]{3,2,1,0:T(8,128)(2,1)} %bitcast.34), calls=%async_computation.2 | async-start | bytes 2097152 | tf_op jit(solution)/shard_map/all_to_all | solution.py:423
  122.3 27.7 %all-to-all-start.3 = ((bf16[16,256,128]{2,1,0:T(8,128)(2,1)}), bf16[16,256,128]{2,1,0:T(8,128)(2,1)}, u32[]{:S(2)}, u32[]{:S(2)}) async-start(bf16[16,256,128]{2,1,0:T(8,128)(2,1)} %copy-done.8), calls=%async_computation.3 | async-start | bytes 2097152 | tf_op jit(solution)/shard_map/all_to_all | solution.py:423
  126.6 5.1 %collective-permute-start.6 = (bf16[2048,256]{1,0:T(8,128)(2,1)S(1)}, bf16[2048,256]{1,0:T(8,128)(2,1)}, u32[]{:S(2)}, u32[]{:S(2)}) collective-permute-start(bf16[2048,256]{1,0:T(8,128)(2,1)S(1)} %shard_map.119.refs_0_), channel_id=1, source_target_pairs={{0,2},{2,0},{4,6},{6,4},{8,10},{10,8},{12,14},{14,12},{16,18},{18,... | collective-permute-start | bytes 3145736 | tf_op jit(solution)/shard_map/ppermute | solution.py:305
  126.9 5.6 %collective-permute-start.7 = (bf16[2048,256]{1,0:T(8,128)(2,1)S(1)}, bf16[2048,256]{1,0:T(8,128)(2,1)}, u32[]{:S(2)}, u32[]{:S(2)}) collective-permute-start(bf16[2048,256]{1,0:T(8,128)(2,1)S(1)} %collective-permute-done.refs_1_), channel_id=1, source_target_pairs={{0,2},{2,0},{4,6},{6,4},{8,10},{10,8},{12,14},{14,12},{16,18},{18,... | collective-permute-start | bytes 3145736 | tf_op jit(solution)/shard_map/ppermute | solution.py:305
  127.2 6.8 %collective-permute-start.8 = (bf16[2048,256]{1,0:T(8,128)(2,1)S(1)}, bf16[2048,256]{1,0:T(8,128)(2,1)}, u32[]{:S(2)}, u32[]{:S(2)}) collective-permute-start(bf16[2048,256]{1,0:T(8,128)(2,1)S(1)} %shard_map.120.refs_4_), channel_id=1, source_target_pairs={{0,2},{2,0},{4,6},{6,4},{8,10},{10,8},{12,14},{14,12},{16,18},{18,... | collective-permute-start | bytes 3145736 | tf_op jit(solution)/shard_map/ppermute | solution.py:305
  127.4 6.6 %collective-permute-start.9 = (bf16[2048,256]{1,0:T(8,128)(2,1)}, bf16[2048,256]{1,0:T(8,128)(2,1)}, u32[]{:S(2)}, u32[]{:S(2)}) collective-permute-start(bf16[2048,256]{1,0:T(8,128)(2,1)} %collective-permute-done.2.refs_5_), channel_id=1, source_target_pairs={{0,2},{2,0},{4,6},{6,4},{8,10},{10,8},{12,14},{14,12},{16,18},{18,... | collective-permute-start | bytes 3145736 | tf_op jit(solution)/shard_map/ppermute | solution.py:305
  137.4 41.0 %collective-permute-start.10 = (bf16[1024,512]{1,0:T(8,128)(2,1)S(1)}, bf16[1024,512]{1,0:T(8,128)(2,1)}, u32[]{:S(2)}, u32[]{:S(2)}) collective-permute-start(bf16[1024,512]{1,0:T(8,128)(2,1)S(1)} %shard_map.127), channel_id=1, source_target_pairs={{0,8},{2,10},{4,12},{6,14},{8,0},{10,2},{12,4},{14,6},{16,24},{18,... | collective-permute-start | bytes 3145736 | tf_op jit(solution)/shard_map/ppermute | solution.py:305
  150.0 81.9 %all-to-all-start.4 = ((bf16[16,272,128]{2,1,0:T(8,128)(2,1)}), bf16[16,272,128]{2,1,0:T(8,128)(2,1)}, u32[]{:S(2)}, u32[]{:S(2)}) async-start(bf16[16,272,128]{2,1,0:T(8,128)(2,1)} %get-tuple-element.90), calls=%async_computation.4 | async-start | bytes 2228224 | tf_op jit(solution)/shard_map/all_to_all | solution.py:423
  178.4 53.4 %collective-permute-start.11 = (bf16[1024,512]{1,0:T(8,128)(2,1)}, bf16[1024,512]{1,0:T(8,128)(2,1)}, u32[]{:S(2)}, u32[]{:S(2)}) collective-permute-start(bf16[1024,512]{1,0:T(8,128)(2,1)} %shard_map.128), channel_id=1, source_target_pairs={{0,8},{2,10},{4,12},{6,14},{8,0},{10,2},{12,4},{14,6},{16,24},{18,... | collective-permute-start | bytes 3145736 | tf_op jit(solution)/shard_map/ppermute | solution.py:305
  180.9 51.0 %collective-permute-start.12 = (bf16[1024,512]{1,0:T(8,128)(2,1)}, bf16[1024,512]{1,0:T(8,128)(2,1)}, u32[]{:S(2)}, u32[]{:S(2)}) collective-permute-start(bf16[1024,512]{1,0:T(8,128)(2,1)} %add_convert_fusion), channel_id=1, source_target_pairs={{0,16},{2,18},{4,20},{6,22},{8,24},{10,26},{12,28},{14,30},{16,0},... | collective-permute-start | bytes 3145736 | tf_op jit(solution)/shard_map/ppermute | solution.py:305
  185.1 5.3 %collective-permute-start.13 = (bf16[4,256,128]{2,1,0:T(8,128)(2,1)}, bf16[4,256,128]{2,1,0:T(8,128)(2,1)}, u32[]{:S(2)}, u32[]{:S(2)}) collective-permute-start(bf16[4,256,128]{2,1,0:T(8,128)(2,1)} %get-tuple-element.93), channel_id=1, source_target_pairs={{0,2},{2,0},{4,6},{6,4},{8,10},{10,8},{12,14},{14,12},{16,18},{18,... | collective-permute-start | bytes 786440 | tf_op jit(solution)/shard_map/ppermute | solution.py:305
  185.1 10.5 %collective-permute-start.14 = (bf16[4,256,128]{2,1,0:T(8,128)(2,1)}, bf16[4,256,128]{2,1,0:T(8,128)(2,1)}, u32[]{:S(2)}, u32[]{:S(2)}) collective-permute-start(bf16[4,256,128]{2,1,0:T(8,128)(2,1)} %get-tuple-element.94), channel_id=1, source_target_pairs={{0,4},{2,6},{4,0},{6,2},{8,12},{10,14},{12,8},{14,10},{16,20},{18,... | collective-permute-start | bytes 786440 | tf_op jit(solution)/shard_map/ppermute | solution.py:305
  186.3 14.4 %collective-permute-start.15 = (bf16[4,256,128]{2,1,0:T(8,128)(2,1)S(1)}, bf16[4,256,128]{2,1,0:T(8,128)(2,1)}, u32[]{:S(2)}, u32[]{:S(2)}) collective-permute-start(bf16[4,256,128]{2,1,0:T(8,128)(2,1)S(1)} %copy-done.16), channel_id=1, source_target_pairs={{0,6},{2,4},{4,2},{6,0},{8,14},{10,12},{12,10},{14,8},{16,22},{18,... | collective-permute-start | bytes 786440 | tf_op jit(solution)/shard_map/ppermute | solution.py:305
  233.9 5.0 %collective-permute-start.16 = (bf16[256,512]{1,0:T(8,128)(2,1)S(1)}, bf16[256,512]{1,0:T(8,128)(2,1)S(1)}, u32[]{:S(2)}, u32[]{:S(2)}) collective-permute-start(bf16[256,512]{1,0:T(8,128)(2,1)S(1)} %get-tuple-element.108), channel_id=1, source_target_pairs={{0,2},{2,0},{4,6},{6,4},{8,10},{10,8},{12,14},{14,12},{16,18},{18,... | collective-permute-start | bytes 786440 | tf_op jit(solution)/shard_map/ppermute | solution.py:305
  234.0 9.2 %collective-permute-start.17 = (bf16[256,512]{1,0:T(8,128)(2,1)S(1)}, bf16[256,512]{1,0:T(8,128)(2,1)S(1)}, u32[]{:S(2)}, u32[]{:S(2)}) collective-permute-start(bf16[256,512]{1,0:T(8,128)(2,1)S(1)} %get-tuple-element.107), channel_id=1, source_target_pairs={{0,4},{2,6},{4,0},{6,2},{8,12},{10,14},{12,8},{14,10},{16,20},{18,... | collective-permute-start | bytes 786440 | tf_op jit(solution)/shard_map/ppermute | solution.py:305
  235.6 12.3 %collective-permute-start.18 = (bf16[256,512]{1,0:T(8,128)(2,1)S(1)}, bf16[256,512]{1,0:T(8,128)(2,1)S(1)}, u32[]{:S(2)}, u32[]{:S(2)}) collective-permute-start(bf16[256,512]{1,0:T(8,128)(2,1)S(1)} %get-tuple-element.106), channel_id=1, source_target_pairs={{0,6},{2,4},{4,2},{6,0},{8,14},{10,12},{12,10},{14,8},{16,22},{18,... | collective-permute-start | bytes 786440 | tf_op jit(solution)/shard_map/ppermute | solution.py:305
  (17 other events, 169.7 us)
